TPU v7x, 32 devices: a whole 2x2x4 slice. The times are simulated.
32 devices in a mesh: seq: 4 (over z), fsdp: 8 (over y, x, core).
Axes of the slice: x: 2, y: 2, z: 4, core: 2. Of those that a mesh axis runs over, the one named last changes fastest.
Arguments:
- stream_in: bfloat16 [16, 1024, 1024], P('fsdp', 'seq'), may hold values from -6 to 6
- timestep: bfloat16 [16, 1024], P('fsdp'), may hold values from -3 to 3
- doc_start: int32 [16, 1024], P('fsdp'), may hold values from 0 to 1023, as said below
- query_weight: bfloat16 [1024, 1024], P('fsdp'), may hold values from -0.1875 to 0.1875
- key_weight: bfloat16 [1024, 1024], P('fsdp'), may hold values from -0.1875 to 0.1875
- value_weight: bfloat16 [1024, 1024], P('fsdp'), may hold values from -0.1875 to 0.1875
- output_weight: bfloat16 [1024, 1024], P('fsdp'), may hold values from -0.75 to 0.75
- query_bias: bfloat16 [1024], P('fsdp'), may hold values from -3 to 3
- value_bias: bfloat16 [1024], P('fsdp'), may hold values from -3 to 3
- output_bias: bfloat16 [1024], P('fsdp'), may hold values from -3 to 3
- first_gain: bfloat16 [1024], P('fsdp'), may hold values from 0.5 to 1.5
- first_shift: bfloat16 [1024], P('fsdp'), may hold values from -3 to 3
- inner_weight: bfloat16 [1024, 4096], P('fsdp'), may hold values from -0.1875 to 0.1875
- inner_bias: bfloat16 [4096], P('fsdp'), may hold values from -3 to 3
- outer_weight: bfloat16 [4096, 1024], P('fsdp'), may hold values from -0.09375 to 0.09375
- outer_bias: bfloat16 [1024], P('fsdp'), may hold values from -3 to 3
- second_gain: bfloat16 [1024], P('fsdp'), may hold values from 0.5 to 1.5
- second_shift: bfloat16 [1024], P('fsdp'), may hold values from -3 to 3
- cotangent: bfloat16 [16, 1024, 1024], P('fsdp', 'seq'), may hold values from -6 to 6
Outputs:
- layer_out: bfloat16 [16, 1024, 1024], P('fsdp', 'seq')
- input_grad: float32 [16, 1024, 1024], P('fsdp', 'seq')
- query_weight_grad: float32 [1024, 1024], P('fsdp')
- key_weight_grad: float32 [1024, 1024], P('fsdp')
- value_weight_grad: float32 [1024, 1024], P('fsdp')
- output_weight_grad: float32 [1024, 1024], P('fsdp')
- query_bias_grad: float32 [1024], P('fsdp')
- value_bias_grad: float32 [1024], P('fsdp')
- output_bias_grad: float32 [1024], P('fsdp')
- first_gain_grad: float32 [1024], P('fsdp')
- first_shift_grad: float32 [1024], P('fsdp')
- inner_weight_grad: float32 [1024, 4096], P('fsdp')
- inner_bias_grad: float32 [4096], P('fsdp')
- outer_weight_grad: float32 [4096, 1024], P('fsdp')
- outer_bias_grad: float32 [1024], P('fsdp')
- second_gain_grad: float32 [1024], P('fsdp')
- second_shift_grad: float32 [1024], P('fsdp')
Inputs may be any that keep to these rules, and one draw needn't show every extreme that they name: `doc_start`: each entry is the position of the first token of its document in the stream; a document is a run of equal entries of 1 to 512 positions, each stream holds one document of exactly 512 positions, and the last position of each stream is a document of its own.
All inputs are finite; a program needn't handle non-finite values.
Results may differ from a plain program's by a relative error of at most 0.017.
Values may be sent and summed in bfloat16 or wider, within the bound.
No kernel may reach another device: no remote copies, remote signals or barrier semaphores. Data moves between devices by JAX's collectives and lax.ppermute only.
A program may use at most 192 MiB of HBM per device.

v0:
```python
from functools import partial

import jax
import jax.numpy as jnp
from jax import lax
from jax.sharding import PartitionSpec as P

HEAD_DIM = 64


def layer_norm(rows, gain, shift):
    centred = rows - jnp.mean(rows, axis=-1, keepdims=True)
    factor = lax.rsqrt(jnp.mean(centred * centred, axis=-1, keepdims=True) + 1e-05)
    normed = centred * factor
    return (normed * gain + shift, normed, factor)


def norm_back(upstream, normed, factor, gain):
    scaled = upstream * gain
    return factor * (
        scaled
        - jnp.mean(scaled, axis=-1, keepdims=True)
        - normed * jnp.mean(scaled * normed, axis=-1, keepdims=True)
    )


def matmul(left, right):
    return jnp.dot(left, right, preferred_element_type=jnp.float32)


def contract_rows(left, right):
    return lax.dot_general(
        left, right, (((0,), (0,)), ((), ())), preferred_element_type=jnp.float32
    )


def contract_cols(left, right):
    return lax.dot_general(
        left, right, (((1,), (1,)), ((), ())), preferred_element_type=jnp.float32
    )


def column_sum(rows):
    return jnp.sum(rows.astype(jnp.float32), axis=0)


def block_scores(query_block, start_block, key_rows, starts):
    scores = jnp.einsum("qhd,khd->hqk", query_block, key_rows, preferred_element_type=jnp.float32)
    same = start_block[:, None] == starts[None, :]
    return jnp.where(same[None], scores, -1e30)


def attend_forward(query_heads, key_heads, value_heads, starts):
    length, width = query_heads.shape
    heads = width // HEAD_DIM
    block = min(512, length)
    count = length // block
    query_blocks = query_heads.reshape(count, block, heads, HEAD_DIM)
    start_blocks = starts.reshape(count, block)
    key_rows = key_heads.reshape(length, heads, HEAD_DIM)
    value_rows = value_heads.reshape(length, heads, HEAD_DIM)

    def one_block(pair):
        query_block, start_block = pair
        scores = block_scores(query_block, start_block, key_rows, starts)
        peak = jnp.max(scores, axis=-1, keepdims=True)
        weights = jnp.exp(scores - peak)
        total = jnp.sum(weights, axis=-1, keepdims=True)
        probs_low = (weights / total).astype(jnp.bfloat16)
        mixed = jnp.einsum(
            "hqk,khd->qhd", probs_low, value_rows, preferred_element_type=jnp.float32
        )
        return (mixed.reshape(block, width).astype(jnp.bfloat16), (peak + jnp.log(total))[..., 0])

    mixed, logsum = lax.map(one_block, (query_blocks, start_blocks))
    return (mixed.reshape(length, width), logsum)


def attend_backward(query_heads, key_heads, value_heads, starts, logsum, grad_heads):
    length, width = query_heads.shape
    heads = width // HEAD_DIM
    block = min(512, length)
    count = length // block
    query_blocks = query_heads.reshape(count, block, heads, HEAD_DIM)
    start_blocks = starts.reshape(count, block)
    grad_blocks = grad_heads.reshape(count, block, heads, HEAD_DIM)
    key_rows = key_heads.reshape(length, heads, HEAD_DIM)
    value_rows = value_heads.reshape(length, heads, HEAD_DIM)

    def one_block(carry, items):
        key_grad, value_grad = carry
        query_block, start_block, block_logsum, grad_block = items
        scores = block_scores(query_block, start_block, key_rows, starts)
        probs = jnp.exp(scores - block_logsum[..., None])
        value_grad = value_grad + jnp.einsum(
            "hqk,qhd->khd",
            probs.astype(jnp.bfloat16),
            grad_block,
            preferred_element_type=jnp.float32,
        )
        grad_probs = jnp.einsum(
            "qhd,khd->hqk", grad_block, value_rows, preferred_element_type=jnp.float32
        )
        inner_sum = jnp.sum(probs * grad_probs, axis=-1, keepdims=True)
        grad_scores = (probs * (grad_probs - inner_sum)).astype(jnp.bfloat16)
        query_grad = jnp.einsum(
            "hqk,khd->qhd", grad_scores, key_rows, preferred_element_type=jnp.float32
        )
        key_grad = key_grad + jnp.einsum(
            "hqk,qhd->khd", grad_scores, query_block, preferred_element_type=jnp.float32
        )
        return ((key_grad, value_grad), query_grad.reshape(block, width).astype(jnp.bfloat16))

    empty = jnp.zeros((length, heads, HEAD_DIM), jnp.float32)
    (key_grad, value_grad), query_grad = lax.scan(
        one_block, (empty, empty), (query_blocks, start_blocks, logsum, grad_blocks)
    )
    return (
        query_grad.reshape(length, width),
        key_grad.reshape(length, width).astype(jnp.bfloat16),
        value_grad.reshape(length, width).astype(jnp.bfloat16),
    )


def body(
    stream_in,
    timestep,
    doc_start,
    query_weight,
    key_weight,
    value_weight,
    output_weight,
    query_bias,
    value_bias,
    output_bias,
    first_gain,
    first_shift,
    inner_weight,
    inner_bias,
    outer_weight,
    outer_bias,
    second_gain,
    second_shift,
    cotangent,
):
    streams, tok_rows, width = stream_in.shape
    flat_rows = streams * tok_rows
    hidden = (stream_in.astype(jnp.float32) + timestep.astype(jnp.float32)[:, None, :]).reshape(
        flat_rows, width
    )
    hidden_low = hidden.astype(jnp.bfloat16)
    attention_set = (
        lax.all_gather(query_weight, "fsdp", axis=0, tiled=True),
        lax.all_gather(key_weight, "fsdp", axis=0, tiled=True),
        lax.all_gather(value_weight, "fsdp", axis=0, tiled=True),
        lax.all_gather(output_weight, "fsdp", axis=0, tiled=True),
        lax.all_gather(query_bias, "fsdp", axis=0, tiled=True),
        lax.all_gather(value_bias, "fsdp", axis=0, tiled=True),
        lax.all_gather(output_bias, "fsdp", axis=0, tiled=True),
        lax.all_gather(first_gain, "fsdp", axis=0, tiled=True),
        lax.all_gather(first_shift, "fsdp", axis=0, tiled=True),
    )
    (
        full_query,
        full_key,
        full_value,
        full_output,
        full_qbias,
        full_vbias,
        full_obias,
        gain_first,
        shift_first,
    ) = attention_set
    queries = (
        ((matmul(hidden_low, full_query) + full_qbias.astype(jnp.float32)) * 0.125)
        .astype(jnp.bfloat16)
        .reshape(streams, tok_rows, width)
    )
    key_rows = matmul(hidden_low, full_key).astype(jnp.bfloat16).reshape(streams, tok_rows, width)
    values = (
        (matmul(hidden_low, full_value) + full_vbias.astype(jnp.float32))
        .astype(jnp.bfloat16)
        .reshape(streams, tok_rows, width)
    )
    query_heads, key_heads, value_heads = (
        lax.all_to_all(queries, "seq", split_axis=2, concat_axis=1, tiled=True),
        lax.all_to_all(key_rows, "seq", split_axis=2, concat_axis=1, tiled=True),
        lax.all_to_all(values, "seq", split_axis=2, concat_axis=1, tiled=True),
    )
    mixed_list = []
    logsum_list = []
    for index in range(streams):
        mixed_one, logsum_one = attend_forward(
            query_heads[index], key_heads[index], value_heads[index], doc_start[index]
        )
        mixed_list.append(mixed_one)
        logsum_list.append(logsum_one)
    mixed_heads = jnp.stack(mixed_list)
    mixed = lax.all_to_all(mixed_heads, "seq", split_axis=1, concat_axis=2, tiled=True).reshape(
        flat_rows, width
    )
    attended = matmul(mixed, full_output) + full_obias.astype(jnp.float32)
    first_out, first_normed, first_factor = layer_norm(
        hidden + attended, gain_first.astype(jnp.float32), shift_first.astype(jnp.float32)
    )
    first_low = first_out.astype(jnp.bfloat16)
    ffn_set = (
        lax.all_gather(inner_weight, "fsdp", axis=0, tiled=True),
        lax.all_gather(inner_bias, "fsdp", axis=0, tiled=True),
        lax.all_gather(outer_weight, "fsdp", axis=0, tiled=True),
        lax.all_gather(outer_bias, "fsdp", axis=0, tiled=True),
        lax.all_gather(second_gain, "fsdp", axis=0, tiled=True),
        lax.all_gather(second_shift, "fsdp", axis=0, tiled=True),
    )
    full_inner, full_ibias, full_outer, full_obias_two, gain_second, shift_second = ffn_set
    inner = matmul(first_low, full_inner) + full_ibias.astype(jnp.float32)
    active_low = jax.nn.gelu(inner, approximate=False).astype(jnp.bfloat16)
    second_in = first_out + matmul(active_low, full_outer) + full_obias_two.astype(jnp.float32)
    result, second_normed, second_factor = layer_norm(
        second_in, gain_second.astype(jnp.float32), shift_second.astype(jnp.float32)
    )
    back_attention = (
        lax.all_gather(query_weight, "fsdp", axis=0, tiled=True),
        lax.all_gather(key_weight, "fsdp", axis=0, tiled=True),
        lax.all_gather(value_weight, "fsdp", axis=0, tiled=True),
        lax.all_gather(output_weight, "fsdp", axis=0, tiled=True),
        lax.all_gather(query_bias, "fsdp", axis=0, tiled=True),
        lax.all_gather(value_bias, "fsdp", axis=0, tiled=True),
        lax.all_gather(output_bias, "fsdp", axis=0, tiled=True),
        lax.all_gather(first_gain, "fsdp", axis=0, tiled=True),
        lax.all_gather(first_shift, "fsdp", axis=0, tiled=True),
    )
    back_ffn = (
        lax.all_gather(inner_weight, "fsdp", axis=0, tiled=True),
        lax.all_gather(inner_bias, "fsdp", axis=0, tiled=True),
        lax.all_gather(outer_weight, "fsdp", axis=0, tiled=True),
        lax.all_gather(outer_bias, "fsdp", axis=0, tiled=True),
        lax.all_gather(second_gain, "fsdp", axis=0, tiled=True),
        lax.all_gather(second_shift, "fsdp", axis=0, tiled=True),
    )
    back_query, back_key, back_value, back_output = (
        back_attention[0],
        back_attention[1],
        back_attention[2],
        back_attention[3],
    )
    back_gain_first = back_attention[7].astype(jnp.float32)
    back_inner, back_outer = (back_ffn[0], back_ffn[2])
    back_gain_second = back_ffn[4].astype(jnp.float32)
    upstream = cotangent.astype(jnp.float32).reshape(flat_rows, width)
    grad_second_gain = jnp.sum(upstream * second_normed, axis=0)
    grad_second_shift = jnp.sum(upstream, axis=0)
    grad_second_in = norm_back(upstream, second_normed, second_factor, back_gain_second)
    grad_outer = grad_second_in.astype(jnp.bfloat16)
    grad_outer_weight = contract_rows(active_low, grad_outer)
    grad_outer_bias = column_sum(grad_outer)
    grad_active = contract_cols(grad_outer, back_outer)
    gelu_back = jax.vjp(partial(jax.nn.gelu, approximate=False), inner)[1]
    grad_inner = gelu_back(grad_active)[0].astype(jnp.bfloat16)
    grad_inner_weight = contract_rows(first_low, grad_inner)
    grad_inner_bias = column_sum(grad_inner)
    grad_first_out = grad_second_in + contract_cols(grad_inner, back_inner)
    grad_first_gain = jnp.sum(grad_first_out * first_normed, axis=0)
    grad_first_shift = jnp.sum(grad_first_out, axis=0)
    grad_first_in = norm_back(grad_first_out, first_normed, first_factor, back_gain_first)
    grad_attended = grad_first_in.astype(jnp.bfloat16)
    grad_output_weight = contract_rows(mixed, grad_attended)
    grad_output_bias = column_sum(grad_attended)
    grad_mixed = (
        contract_cols(grad_attended, back_output)
        .astype(jnp.bfloat16)
        .reshape(streams, tok_rows, width)
    )
    grad_mixed_heads = lax.all_to_all(grad_mixed, "seq", split_axis=2, concat_axis=1, tiled=True)
    query_list = []
    key_list = []
    value_list = []
    for index in range(streams):
        grad_query_one, grad_key_one, grad_value_one = attend_backward(
            query_heads[index],
            key_heads[index],
            value_heads[index],
            doc_start[index],
            logsum_list[index],
            grad_mixed_heads[index],
        )
        query_list.append(grad_query_one)
        key_list.append(grad_key_one)
        value_list.append(grad_value_one)
    grad_queries, grad_keys, grad_values = (
        lax.all_to_all(jnp.stack(query_list), "seq", split_axis=1, concat_axis=2, tiled=True),
        lax.all_to_all(jnp.stack(key_list), "seq", split_axis=1, concat_axis=2, tiled=True),
        lax.all_to_all(jnp.stack(value_list), "seq", split_axis=1, concat_axis=2, tiled=True),
    )
    grad_queries = grad_queries.reshape(flat_rows, width)
    grad_keys = grad_keys.reshape(flat_rows, width)
    grad_values = grad_values.reshape(flat_rows, width)
    grad_query_weight = contract_rows(hidden_low, grad_queries) * 0.125
    grad_query_bias = column_sum(grad_queries) * 0.125
    grad_key_weight = contract_rows(hidden_low, grad_keys)
    grad_value_weight = contract_rows(hidden_low, grad_values)
    grad_value_bias = column_sum(grad_values)
    grad_hidden = (
        grad_first_in
        + 0.125 * contract_cols(grad_queries, back_query)
        + contract_cols(grad_keys, back_key)
        + contract_cols(grad_values, back_value)
    )
    shares = (
        lax.psum_scatter(grad_query_weight, "fsdp", scatter_dimension=0, tiled=True),
        lax.psum_scatter(grad_key_weight, "fsdp", scatter_dimension=0, tiled=True),
        lax.psum_scatter(grad_value_weight, "fsdp", scatter_dimension=0, tiled=True),
        lax.psum_scatter(grad_output_weight, "fsdp", scatter_dimension=0, tiled=True),
        lax.psum_scatter(grad_query_bias, "fsdp", scatter_dimension=0, tiled=True),
        lax.psum_scatter(grad_value_bias, "fsdp", scatter_dimension=0, tiled=True),
        lax.psum_scatter(grad_output_bias, "fsdp", scatter_dimension=0, tiled=True),
        lax.psum_scatter(grad_first_gain, "fsdp", scatter_dimension=0, tiled=True),
        lax.psum_scatter(grad_first_shift, "fsdp", scatter_dimension=0, tiled=True),
        lax.psum_scatter(grad_inner_weight, "fsdp", scatter_dimension=0, tiled=True),
        lax.psum_scatter(grad_inner_bias, "fsdp", scatter_dimension=0, tiled=True),
        lax.psum_scatter(grad_outer_weight, "fsdp", scatter_dimension=0, tiled=True),
        lax.psum_scatter(grad_outer_bias, "fsdp", scatter_dimension=0, tiled=True),
        lax.psum_scatter(grad_second_gain, "fsdp", scatter_dimension=0, tiled=True),
        lax.psum_scatter(grad_second_shift, "fsdp", scatter_dimension=0, tiled=True),
    )
    totals = (
        lax.psum(shares[0].astype(jnp.bfloat16), "seq").astype(jnp.float32),
        lax.psum(shares[1].astype(jnp.bfloat16), "seq").astype(jnp.float32),
        lax.psum(shares[2].astype(jnp.bfloat16), "seq").astype(jnp.float32),
        lax.psum(shares[3].astype(jnp.bfloat16), "seq").astype(jnp.float32),
        lax.psum(shares[4].astype(jnp.bfloat16), "seq").astype(jnp.float32),
        lax.psum(shares[5].astype(jnp.bfloat16), "seq").astype(jnp.float32),
        lax.psum(shares[6].astype(jnp.bfloat16), "seq").astype(jnp.float32),
        lax.psum(shares[7].astype(jnp.bfloat16), "seq").astype(jnp.float32),
        lax.psum(shares[8].astype(jnp.bfloat16), "seq").astype(jnp.float32),
        lax.psum(shares[9].astype(jnp.bfloat16), "seq").astype(jnp.float32),
        lax.psum(shares[10].astype(jnp.bfloat16), "seq").astype(jnp.float32),
        lax.psum(shares[11].astype(jnp.bfloat16), "seq").astype(jnp.float32),
        lax.psum(shares[12].astype(jnp.bfloat16), "seq").astype(jnp.float32),
        lax.psum(shares[13].astype(jnp.bfloat16), "seq").astype(jnp.float32),
        lax.psum(shares[14].astype(jnp.bfloat16), "seq").astype(jnp.float32),
    )
    return (
        result.astype(jnp.bfloat16).reshape(streams, tok_rows, width),
        grad_hidden.reshape(streams, tok_rows, width),
        totals[0],
        totals[1],
        totals[2],
        totals[3],
        totals[4],
        totals[5],
        totals[6],
        totals[7],
        totals[8],
        totals[9],
        totals[10],
        totals[11],
        totals[12],
        totals[13],
        totals[14],
    )


def solution(mesh):
    in_specs = (
        P("fsdp", "seq", None),
        P("fsdp", None),
        P("fsdp", None),
        P("fsdp", None),
        P("fsdp", None),
        P("fsdp", None),
        P("fsdp", None),
        P("fsdp"),
        P("fsdp"),
        P("fsdp"),
        P("fsdp"),
        P("fsdp"),
        P("fsdp", None),
        P("fsdp"),
        P("fsdp", None),
        P("fsdp"),
        P("fsdp"),
        P("fsdp"),
        P("fsdp", "seq", None),
    )
    out_specs = (
        P("fsdp", "seq", None),
        P("fsdp", "seq", None),
        P("fsdp", None),
        P("fsdp", None),
        P("fsdp", None),
        P("fsdp", None),
        P("fsdp"),
        P("fsdp"),
        P("fsdp"),
        P("fsdp"),
        P("fsdp"),
        P("fsdp", None),
        P("fsdp"),
        P("fsdp", None),
        P("fsdp"),
        P("fsdp"),
        P("fsdp"),
    )
    return jax.shard_map(body, mesh=mesh, in_specs=in_specs, out_specs=out_specs, check_vma=False)
```

profile of v0, /device:TPU:0, one launch (start us, length us, event | category | flops | bytes accessed | tf_op | source)
XLA Modules:
  0.0 1031.7 jit_solution(2584062967114833172)
XLA Ops:
  11.3 10.3 all-gather
  25.6 14.9 %all-gather.16.cloned.1.call-done = bf16[1024,1024]{1,0:T(8,128)(2,1)} async-done(((bf16[128,1024]{1,0:T(8,128)(2,1)}), bf16[1024,1024]{1,0:T(8,128)(2,1)}) %all-gather.16.cloned.1.call-update) | async-done | bytes 2097168 | tf_op jit(solution)/shard_map/all_gather | solution.py:153
  45.4 4.6 all-to-all-start
  50.0 8.7 all-gather.1
  58.7 11.6 %all-gather.20.cloned.1.call-done = bf16[1024,1024]{1,0:T(8,128)(2,1)} async-done(((bf16[128,1024]{1,0:T(8,128)(2,1)}), bf16[1024,1024]{1,0:T(8,128)(2,1)}) %all-gather.20.cloned.1.call-update) | async-done | bytes 2097168 | tf_op jit(solution)/shard_map/all_gather | solution.py:155
  77.2 3.7 all-to-all-start.2
  80.8 19.4 %all-gather.18.cloned.1.call-done = bf16[1024,1024]{1,0:T(8,128)(2,1)} async-done(((bf16[128,1024]{1,0:T(8,128)(2,1)}), bf16[1024,1024]{1,0:T(8,128)(2,1)}) %all-gather.18.cloned.1.call-update) | async-done | bytes 2097168 | tf_op jit(solution)/shard_map/all_gather | solution.py:154
  107.0 3.5 all-to-all-start.1
  118.5 17.3 %all-to-all-done.1 = bf16[2,256,1024]{1,0,2:T(2,128)(2,1)S(1)} async-done(((bf16[2,256,1024]{1,0,2:T(2,128)(2,1)}), bf16[2,256,1024]{1,0,2:T(2,128)(2,1)S(1)}, u32[]{:S(2)}, u32[]{:S(2)}) %all-to-all-start.1) | async-done | bytes 1048608 | tf_op jit(solution)/shard_map/all_to_all | solution.py:187
  140.0 17.0 %while.54 = (s32[]{:T(128)}, bf16[2,512,256]{2,1,0:T(8,128)(2,1)}, f32[2,4,512]{2,1,0:T(4,128)S(1)}, s32[2,512]{1,0:T(2,128)S(1)}, s32[1,1024]{1,0:T(1,128)S(1)}...) while((s32[]{:T(128)}, bf16[2,512,256]{2,1,0:T(8,128)(2,1)}, ...), condition=%wide.region_3.4_spmd, body=%wide.region_0.3_spmd.sunk | while | flops 556398592 | bytes 29961316 | solution.py:75
  162.2 15.0 %while.55 = (s32[]{:T(128)}, bf16[2,512,256]{2,1,0:T(8,128)(2,1)S(1)}, f32[2,4,512]{2,1,0:T(4,128)}, s32[2,512]{1,0:T(2,128)S(1)}, s32[1,1024]{1,0:T(1,128)S(1)}...) while((s32[]{:T(128)}, ...), condition=%wide.region_7.8_spmd, body=%wide.region_4.7_spmd.sunk | while | flops 556398592 | bytes 29960808 | solution.py:75
  181.1 4.3 all-to-all-start.3
  185.4 8.2 all-gather.2
  193.6 8.3 all-gather.3
  201.9 8.2 all-gather.4
  210.2 8.4 all-gather.5
  218.6 8.2 all-gather.6
  226.9 8.3 all-gather.7
  236.1 8.2 all-gather.8
  246.7 3.9 fusion.106
  252.4 28.2 %multiply_convert_fusion.2 = (bf16[512,4096]{1,0:T(8,128)(2,1)}, f32[512,4096]{1,0:T(8,128)}, f32[512,4096]{1,0:T(8,128)}) fusion(f32[4096]{0:T(1024)S(1)} %bitcast.382, bf16[1024,4096]{1,0:T(8,128)(2,1)} %all-gather.24.cloned.1.call-done, f32[512,1024]{1,0:T(8,128)} %copy-done.29, f32[1024]{0:T(1024)S(1)} %bitcast.386, f32[1024]{0:T(1024)S(1)} %bitcast.374, ...), kind=kOutput, calls=%fused_computation.98 | convolution fusion | flops 4436000768 | bytes 31485952 | tf_op jit(solution)/shard_map/dot_general | solution.py:28
  280.5 9.9 fusion.107
  294.6 16.4 %convert_reduce_fusion = (f32[4096]{0:T(1024)}, bf16[512,4096]{1,0:T(8,128)(2,1)}) fusion(f32[512,4096]{1,0:T(8,128)} %get-tuple-element.570, bf16[4096,1024]{1,0:T(8,128)(2,1)} %all-gather.26.cloned.1.call-done, f32[512,1024]{1,0:T(8,128)S(1)} %get-tuple-element.566, f32[512,4096]{1,0:T(8,128)} %get-tuple-element.594, f32[4096]{0:T(1024)S(1)} %bitcast.383), kind=kOutput, calls=%fused_computation.96 | convolution fusion | flops 4331139072 | bytes 31490048 | tf_op jit(solution)/shard_map/dot_general | solution.py:38
  311.0 9.6 multiply_reduce_fusion.2
  325.5 5.0 all-to-all-start.4
  330.5 4.5 fusion.87
  335.2 21.6 %all-to-all-done.4 = bf16[2,256,1024]{1,0,2:T(2,128)(2,1)} async-done(((bf16[2,256,1024]{1,0,2:T(2,128)(2,1)}), bf16[2,256,1024]{1,0,2:T(2,128)(2,1)}, u32[]{:S(2)}, u32[]{:S(2)}) %all-to-all-start.4) | async-done | bytes 1048608 | tf_op jit(solution)/shard_map/all_to_all | solution.py:274
  361.6 47.2 %while.56 = (s32[]{:T(128)}, f32[1024,4,64]{0,2,1:T(8,128)}, f32[1024,4,64]{0,2,1:T(8,128)}, bf16[2,512,256]{2,1,0:T(8,128)(2,1)}, bf16[2,512,4,64]{1,3,2,0:T(8,...) while((s32[]{:T(128)}, f32[1024,4,64]{0,2,1:T(8,128)}, ...), condition=%wide.region_18.19_spmd.clone, body=%wide.region_16.18_spmd.clone.sunk | while | flops 1369044992 | bytes 163385168 | solution.py:115
  376.0 4.4 fusion.206
  381.5 3.4 fusion.207
  398.9 4.5 fusion.206
  404.3 4.5 fusion.207
  413.3 41.3 %while.57 = (s32[]{:T(128)}, f32[1024,4,64]{0,2,1:T(8,128)S(1)}, f32[1024,4,64]{0,2,1:T(8,128)}, bf16[2,512,256]{2,1,0:T(8,128)(2,1)}, bf16[2,512,4,64]{1,3,2,0:...) while((s32[]{:T(128)}, f32[1024,4,64]{0,2,1:T(8,128)S(1)}, ...), condition=%wide.region_21.22_spmd.clone, body=%wide.region_19.21_spmd.clone.sunk | while | flops 1369044992 | bytes 163384144 | solution.py:115
  430.2 3.4 fusion.219
  450.2 4.4 fusion.219
  457.0 27.7 %all_to_all.120 = bf16[2,1024,256]{2,0,1:T(2,128)(2,1)S(1)} all-to-all(bf16[2,1024,256]{2,0,1:T(2,128)(2,1)S(1)} %copy.128), channel_id=1, replica_groups=mesh['seq'=4,'fsdp'=8] {'seq'}, dimensions={1} | all-to-all | bytes 2097152 | tf_op jit(solution)/shard_map/all_to_all | solution.py:291
  491.6 27.8 %all_to_all.121 = bf16[2,1024,256]{2,0,1:T(2,128)(2,1)S(1)} all-to-all(bf16[2,1024,256]{2,0,1:T(2,128)(2,1)S(1)} %copy.130), channel_id=1, replica_groups=mesh['seq'=4,'fsdp'=8] {'seq'}, dimensions={1} | all-to-all | bytes 2097152 | tf_op jit(solution)/shard_map/all_to_all | solution.py:292
  521.6 3.4 fusion.110
  528.7 27.8 %all_to_all.122 = bf16[2,1024,256]{2,0,1:T(2,128)(2,1)S(1)} all-to-all(bf16[2,1024,256]{2,0,1:T(2,128)(2,1)S(1)} %copy.133), channel_id=1, replica_groups=mesh['seq'=4,'fsdp'=8] {'seq'}, dimensions={1} | all-to-all | bytes 2097152 | tf_op jit(solution)/shard_map/all_to_all | solution.py:293
  558.6 3.3 fusion.111
  562.1 13.3 %fusion.96 = f32[1024,4096]{1,0:T(8,128)} fusion(bf16[512,4096]{1,0:T(8,128)(2,1)} %get-tuple-element.599, f32[512,1024]{1,0:T(8,128)} %copy-done.29, f32[1024]{0:T(1024)S(1)} %bitcast.388, f32[1024]{0:T(1024)S(1)} %bitcast.378, f32[512]{0:T(512)S(1)} %copy-done.66, f32[512]{0:T(512)S(1)} %copy-done.57), kind=kOutput, calls=%fused_computation.181 | convolution fusion | flops 4297588736 | bytes 23080960 | tf_op jit(solution)/shard_map/dot_general | solution.py:32
  575.7 13.4 %fusion.90 = f32[4096,1024]{1,0:T(8,128)} fusion(bf16[512,4096]{1,0:T(8,128)(2,1)} %get-tuple-element.569, f32[512,1024]{1,0:T(8,128)} %copy-done.41), kind=kOutput, calls=%fused_computation.175 | convolution fusion | flops 4295491584 | bytes 23068672 | tf_op jit(solution)/shard_map/dot_general | solution.py:32
  596.2 53.2 %reduce-scatter.11.cloned.1.call-done = f32[128,1024]{1,0:T(8,128)} async-done(((f32[1024,1024]{1,0:T(8,128)}), f32[128,1024]{1,0:T(8,128)}) %reduce-scatter.11.cloned.1.call-update) | async-done | bytes 524304 | tf_op jit(solution)/shard_map/reduce_scatter | solution.py:312
  651.1 117.8 %reduce-scatter.15.cloned.1.call-done = f32[128,4096]{1,0:T(8,128)} async-done(((f32[1024,4096]{1,0:T(8,128)}), f32[128,4096]{1,0:T(8,128)}) %reduce-scatter.15.cloned.1.call-update) | async-done | bytes 2097168 | tf_op jit(solution)/shard_map/reduce_scatter | solution.py:319
  771.6 116.7 %reduce-scatter.17.cloned.1.call-done = f32[512,1024]{1,0:T(8,128)} async-done(((f32[4096,1024]{1,0:T(8,128)}), f32[512,1024]{1,0:T(8,128)}) %reduce-scatter.17.cloned.1.call-update) | async-done | bytes 2097168 | tf_op jit(solution)/shard_map/reduce_scatter | solution.py:321
  894.1 24.8 %all-reduce.9 = (bf16[1024]{0:T(1024)(128)(2,1)S(1)}, bf16[1024]{0:T(1024)(128)(2,1)S(1)}, bf16[1024]{0:T(1024)(128)(2,1)S(1)}, bf16[1024]{0:T(1024)(128)(2,1)S(...) all-reduce(f32[1024]{0:T(1024)S(1)} %bitcast.380, ...), channel_id=6, replica_groups=mesh['seq'=4,'fsdp'=8] {'fsdp'}, use_global_device_ids=true, to_apply=%region_31.32.clone | all-reduce | flops 12288 | bytes 73728
  919.5 12.8 %all-reduce.10 = (bf16[128]{0:T(256)(128)(2,1)S(1)}, bf16[128]{0:T(256)(128)(2,1)S(1)}, bf16[128]{0:T(256)(128)(2,1)S(1)}, bf16[128]{0:T(256)(128)(2,1)S(1)}, bf...) all-reduce(bf16[128]{0:T(256)(128)(2,1)S(1)} %dynamic-slice.35, ...), channel_id=1, replica_groups=mesh['seq'=4,'fsdp'=8] {'seq'}, use_global_device_ids=true, to_apply=%region_32.33 | all-reduce | flops 1536 | bytes 6144 | tf_op jit(solution)/shard_map/psum | solution.py:331
  945.3 70.4 %all-reduce.14.cloned.1.call-done = (bf16[128,1024]{1,0:T(8,128)(2,1)}, bf16[128,1024]{1,0:T(8,128)(2,1)}, bf16[128,1024]{1,0:T(8,128)(2,1)}, bf16[128,1024]{1,0...) async-done(((bf16[128,1024]{1,0:T(8,128)(2,1)}, bf16[128,1024]{1,0:T(8,128)(2,1)}, bf16[128,1024]{1,0:T(8,128)(2,1)}, bf16[128,1024]{1,0:T(8,128)(2,1)}, ...) | async-done | bytes 3145744 | tf_op jit(solution)/shard_map/psum | solution.py:327
  (431 shorter events, 221.1 us)
Async XLA Ops:
  7.2 33.4 %all-gather.16.cloned.1.call-start = ((), (), s32[]{:S(2)}) async-start(), calls=%async_computation.14 | async-start | bytes 2359296 | tf_op jit(solution)/shard_map/all_gather | solution.py:153
  7.9 62.4 %all-gather.20.cloned.1.call-start = ((), (), s32[]{:S(2)}) async-start(), calls=%async_computation.16 | async-start | bytes 2359296 | tf_op jit(solution)/shard_map/all_gather | solution.py:155
  8.7 91.5 %all-gather.18.cloned.1.call-start = ((), (), s32[]{:S(2)}) async-start(), calls=%async_computation.15 | async-start | bytes 2359296 | tf_op jit(solution)/shard_map/all_gather | solution.py:154
  9.4 237.3 %all-gather.22.cloned.1.call-start = ((), (), s32[]{:S(2)}) async-start(), calls=%async_computation.17 | async-start | bytes 2359296 | tf_op jit(solution)/shard_map/all_gather | solution.py:156
  10.0 242.4 %all-gather.24.cloned.1.call-start = ((), (), s32[]{:S(2)}) async-start(), calls=%async_computation.18 | async-start | bytes 9437184 | tf_op jit(solution)/shard_map/all_gather | solution.py:208
  45.4 30.8 %all-to-all-start = ((bf16[2,256,1024]{1,0,2:T(2,128)(2,1)}), bf16[2,256,1024]{1,0,2:T(2,128)(2,1)S(1)}, u32[]{:S(2)}, u32[]{:S(2)}) async-start(bf16[2,256,1024]{1,0,2:T(2,128)(2,1)} %copy.102), calls=%async_computation | async-start | bytes 2097152 | tf_op jit(solution)/shard_map/all_to_all | solution.py:186
  77.2 29.8 %all-to-all-start.2 = ((bf16[2,256,1024]{1,0,2:T(2,128)(2,1)}), bf16[2,256,1024]{1,0,2:T(2,128)(2,1)S(1)}, u32[]{:S(2)}, u32[]{:S(2)}) async-start(bf16[2,256,1024]{1,0,2:T(2,128)(2,1)} %copy.107), calls=%async_computation.2 | async-start | bytes 2097152 | tf_op jit(solution)/shard_map/all_to_all | solution.py:188
  107.0 28.9 %all-to-all-start.1 = ((bf16[2,256,1024]{1,0,2:T(2,128)(2,1)}), bf16[2,256,1024]{1,0,2:T(2,128)(2,1)S(1)}, u32[]{:S(2)}, u32[]{:S(2)}) async-start(bf16[2,256,1024]{1,0,2:T(2,128)(2,1)} %copy.105), calls=%async_computation.1 | async-start | bytes 2097152 | tf_op jit(solution)/shard_map/all_to_all | solution.py:187
  110.5 170.0 %all-gather.26.cloned.1.call-start = ((), (), s32[]{:S(2)}) async-start(), calls=%async_computation.19 | async-start | bytes 9437184 | tf_op jit(solution)/shard_map/all_gather | solution.py:210
  177.2 69.2 %copy-start.6 = (bf16[1024,4,64]{0,2,1:T(8,128)(2,1)}, bf16[1024,4,64]{0,2,1:T(8,128)(2,1)S(1)}, u32[]{:S(2)}) copy-start(bf16[1024,4,64]{0,2,1:T(8,128)(2,1)S(1)} %get-tuple-element.1006) | copy-start | bytes 1572868
  177.2 69.2 %copy-start.11 = (bf16[2,512,4,64]{1,3,2,0:T(8,128)(2,1)}, bf16[2,512,4,64]{1,3,2,0:T(8,128)(2,1)S(1)}, u32[]{:S(2)}) copy-start(bf16[2,512,4,64]{1,3,2,0:T(8,128)(2,1)S(1)} %get-tuple-element.1008) | copy-start | bytes 1572868
  177.2 69.2 %copy-start.18 = (bf16[1024,4,64]{0,2,1:T(8,128)(2,1)}, bf16[1024,4,64]{0,2,1:T(8,128)(2,1)S(1)}, u32[]{:S(2)}) copy-start(bf16[1024,4,64]{0,2,1:T(8,128)(2,1)S(1)} %get-tuple-element.1017) | copy-start | bytes 1572868
  177.2 69.2 %copy-start.42 = (s32[1,1024]{1,0:T(1,128)}, s32[1,1024]{1,0:T(1,128)S(1)}, u32[]{:S(2)}) copy-start(s32[1,1024]{1,0:T(1,128)S(1)} %get-tuple-element.1051) | copy-start | bytes 12292
  177.2 69.2 %copy-start.52 = (s32[2,512]{1,0:T(2,128)}, s32[2,512]{1,0:T(2,128)S(1)}, u32[]{:S(2)}) copy-start(s32[2,512]{1,0:T(2,128)S(1)} %get-tuple-element.1065) | copy-start | bytes 12292
  177.3 32.9 %copy-start.72 = (bf16[512]{0:T(512)(128)(2,1)S(1)}, bf16[512]{0:T(512)(128)(2,1)}, u32[]{:S(2)}) copy-start(bf16[512]{0:T(512)(128)(2,1)} %param.40) | copy-start | bytes 3076
  177.3 41.3 %copy-start.77 = (bf16[128]{0:T(256)(128)(2,1)S(1)}, bf16[128]{0:T(256)(128)(2,1)}, u32[]{:S(2)}) copy-start(bf16[128]{0:T(256)(128)(2,1)} %param.42) | copy-start | bytes 772
  177.3 49.6 %copy-start.78 = (bf16[128]{0:T(256)(128)(2,1)S(1)}, bf16[128]{0:T(256)(128)(2,1)}, u32[]{:S(2)}) copy-start(bf16[128]{0:T(256)(128)(2,1)} %param.43) | copy-start | bytes 772
  177.3 57.8 %copy-start.26 = (bf16[2,256,1024]{2,1,0:T(8,128)(2,1)S(1)}, bf16[2,256,1024]{2,1,0:T(8,128)(2,1)}, u32[]{:S(2)}) copy-start(bf16[2,256,1024]{2,1,0:T(8,128)(2,1)} %param.45) | copy-start | bytes 3145732
  177.3 58.8 %copy-start.79 = (bf16[128]{0:T(256)(128)(2,1)S(1)}, bf16[128]{0:T(256)(128)(2,1)}, u32[]{:S(2)}) copy-start(bf16[128]{0:T(256)(128)(2,1)} %param.44) | copy-start | bytes 772
  181.1 63.3 %all-to-all-start.3 = ((bf16[2,1024,256]{2,0,1:T(2,128)(2,1)}), bf16[2,1024,256]{2,0,1:T(2,128)(2,1)}, u32[]{:S(2)}, u32[]{:S(2)}) async-start(bf16[2,1024,256]{2,0,1:T(2,128)(2,1)} %copy.116), calls=%async_computation.3 | async-start | bytes 2097152 | tf_op jit(solution)/shard_map/all_to_all | solution.py:199
  201.9 118.7 %copy-start.61 = (f32[8,1,128]{2,1,0:T(1,128)}, f32[8,1,128]{2,1,0:T(1,128)S(1)}, u32[]{:S(2)}) copy-start(f32[8,1,128]{2,1,0:T(1,128)S(1)} %convert_element_type.390) | copy-start | bytes 12292
  210.1 70.4 %copy-start.70 = (f32[8,1,128]{2,1,0:T(1,128)}, f32[8,1,128]{2,1,0:T(1,128)S(1)}, u32[]{:S(2)}) copy-start(f32[8,1,128]{2,1,0:T(1,128)S(1)} %convert_element_type.391) | copy-start | bytes 12292
  250.7 69.9 %copy-start.56 = (f32[512]{0:T(512)}, f32[512]{0:T(512)S(1)}, u32[]{:S(2)}) copy-start(f32[512]{0:T(512)S(1)} %broadcast_multiply_fusion.4) | copy-start | bytes 6148
  252.3 68.3 %copy-start.65 = (f32[512]{0:T(512)}, f32[512]{0:T(512)S(1)}, u32[]{:S(2)}) copy-start(f32[512]{0:T(512)S(1)} %add_rsqrt_fusion.1) | copy-start | bytes 6148
  325.5 31.3 %all-to-all-start.4 = ((bf16[2,256,1024]{1,0,2:T(2,128)(2,1)}), bf16[2,256,1024]{1,0,2:T(2,128)(2,1)}, u32[]{:S(2)}, u32[]{:S(2)}) async-start(bf16[2,256,1024]{1,0,2:T(2,128)(2,1)} %copy.118), calls=%async_computation.4 | async-start | bytes 2097152 | tf_op jit(solution)/shard_map/all_to_all | solution.py:274
  330.5 258.8 %reduce-scatter.13.cloned.1.call-start = ((), (), s32[]{:S(2)}) async-start(), calls=%async_computation.23 | async-start | bytes 4718592 | tf_op jit(solution)/shard_map/reduce_scatter | solution.py:313
  335.1 26.4 %copy-start.9 = (bf16[1024,4,64]{0,2,1:T(8,128)(2,1)S(1)}, bf16[1024,4,64]{0,2,1:T(8,128)(2,1)}, u32[]{:S(2)}) copy-start(bf16[1024,4,64]{0,2,1:T(8,128)(2,1)} %copy-done.8) | copy-start | bytes 1572868
  335.2 255.9 %reduce-scatter.7.cloned.1.call-start = ((), (), s32[]{:S(2)}) async-start(), calls=%async_computation.20 | async-start | bytes 4718592 | tf_op jit(solution)/shard_map/reduce_scatter | solution.py:310
  361.6 51.7 %copy-start.7 = (bf16[1024,4,64]{0,2,1:T(8,128)(2,1)S(1)}, bf16[1024,4,64]{0,2,1:T(8,128)(2,1)}, u32[]{:S(2)}) copy-start(bf16[1024,4,64]{0,2,1:T(8,128)(2,1)} %copy-done.6) | copy-start | bytes 1572868
  361.6 51.7 %copy-start.12 = (bf16[2,512,4,64]{1,3,2,0:T(8,128)(2,1)S(1)}, bf16[2,512,4,64]{1,3,2,0:T(8,128)(2,1)}, u32[]{:S(2)}) copy-start(bf16[2,512,4,64]{1,3,2,0:T(8,128)(2,1)} %copy-done.11) | copy-start | bytes 1572868
  361.6 51.7 %copy-start.43 = (s32[1,1024]{1,0:T(1,128)S(1)}, s32[1,1024]{1,0:T(1,128)}, u32[]{:S(2)}) copy-start(s32[1,1024]{1,0:T(1,128)} %copy-done.42) | copy-start | bytes 12292
  361.6 51.7 %copy-start.53 = (s32[2,512]{1,0:T(2,128)S(1)}, s32[2,512]{1,0:T(2,128)}, u32[]{:S(2)}) copy-start(s32[2,512]{1,0:T(2,128)} %copy-done.52) | copy-start | bytes 12292
  455.9 30.9 %copy-start.13 = (bf16[2,256,1024]{2,1,0:T(8,128)(2,1)S(1)}, bf16[2,256,1024]{2,1,0:T(8,128)(2,1)}, u32[]{:S(2)}) copy-start(bf16[2,256,1024]{2,1,0:T(8,128)(2,1)} %get-tuple-element.580) | copy-start | bytes 3145732
  490.1 104.3 %reduce-scatter.9.cloned.1.call-start = ((), (), s32[]{:S(2)}) async-start(), calls=%async_computation.21 | async-start | bytes 4718592 | tf_op jit(solution)/shard_map/reduce_scatter | solution.py:311
  525.0 124.4 %reduce-scatter.11.cloned.1.call-start = ((), (), s32[]{:S(2)}) async-start(), calls=%async_computation.22 | async-start | bytes 4718592 | tf_op jit(solution)/shard_map/reduce_scatter | solution.py:312
  562.0 206.9 %reduce-scatter.15.cloned.1.call-start = ((), (), s32[]{:S(2)}) async-start(), calls=%async_computation.24 | async-start | bytes 18874368 | tf_op jit(solution)/shard_map/reduce_scatter | solution.py:319
  575.4 312.9 %reduce-scatter.17.cloned.1.call-start = ((), (), s32[]{:S(2)}) async-start(), calls=%async_computation.25 | async-start | bytes 18874368 | tf_op jit(solution)/shard_map/reduce_scatter | solution.py:321
  589.2 426.5 %all-reduce.14.cloned.1.call-start = ((), (), s32[]{:S(2)}) async-start(), calls=%async_computation.26 | async-start | bytes 6291456 | tf_op jit(solution)/shard_map/psum | solution.py:327
  651.1 240.0 %copy-start.82 = (u32[32]{0:T(128)S(1)}, u32[32]{0:T(128)}, u32[]{:S(2)}) copy-start(u32[32]{0:T(128)} %constant.154) | copy-start | bytes 388
  651.1 241.9 %copy-start.25 = (bf16[2,1024,256]{2,0,1:T(2,128)(2,1)S(1)}, bf16[2,1024,256]{2,0,1:T(2,128)(2,1)}, u32[]{:S(2)}) copy-start(bf16[2,1024,256]{2,0,1:T(2,128)(2,1)} %copy-done.24) | copy-start | bytes 3145732
  771.6 122.4 %copy-start.58 = (f32[1024]{0:T(1024)S(1)}, f32[1024]{0:T(1024)}, u32[]{:S(2)}) copy-start(f32[1024]{0:T(1024)} %get-tuple-element.461) | copy-start | bytes 12292
  771.6 122.4 %copy-start.59 = (f32[1024]{0:T(1024)S(1)}, f32[1024]{0:T(1024)}, u32[]{:S(2)}) copy-start(f32[1024]{0:T(1024)} %get-tuple-element.457) | copy-start | bytes 12292
  771.6 122.4 %copy-start.60 = (f32[1024]{0:T(1024)S(1)}, f32[1024]{0:T(1024)}, u32[]{:S(2)}) copy-start(f32[1024]{0:T(1024)} %get-tuple-element.567) | copy-start | bytes 12292
  771.6 122.4 %copy-start.63 = (f32[4096]{0:T(1024)S(1)}, f32[4096]{0:T(1024)}, u32[]{:S(2)}) copy-start(f32[4096]{0:T(1024)} %get-tuple-element.598) | copy-start | bytes 49156
  771.6 122.4 %copy-start.64 = (f32[1024]{0:T(1024)S(1)}, f32[1024]{0:T(1024)}, u32[]{:S(2)}) copy-start(f32[1024]{0:T(1024)} %get-tuple-element.565) | copy-start | bytes 12292
  771.6 122.4 %copy-start.68 = (f32[1024]{0:T(1024)S(1)}, f32[1024]{0:T(1024)}, u32[]{:S(2)}) copy-start(f32[1024]{0:T(1024)} %get-tuple-element.455) | copy-start | bytes 12292
  771.6 122.4 %copy-start.69 = (f32[1024]{0:T(1024)S(1)}, f32[1024]{0:T(1024)}, u32[]{:S(2)}) copy-start(f32[1024]{0:T(1024)} %get-tuple-element.460) | copy-start | bytes 12292
  771.6 165.4 %copy-start.36 = (bf16[64,8,4,256]{3,1,2,0:T(8,128)(2,1)S(1)}, bf16[64,8,4,256]{3,1,2,0:T(8,128)(2,1)}, u32[]{:S(2)}) copy-start(bf16[64,8,4,256]{3,1,2,0:T(8,128)(2,1)} %copy-done.35) | copy-start | bytes 3145732
  (65 other events, 393.8 us)
Sparse Core Ops, SparseCore 0:
  9.9 30.5 all-gather.15
  42.4 27.8 all-gather.19
  72.3 27.8 all-gather.17
  101.9 27.8 all-gather.21
  131.6 54.4 all-gather.23
  187.8 54.4 all-gather.25
  335.2 51.8 reduce-scatter.12
  490.2 49.4 reduce-scatter.6
  543.1 51.2 reduce-scatter.8
  598.0 51.3 reduce-scatter.10
  652.9 115.9 reduce-scatter.14
  772.3 115.9 reduce-scatter.16
  892.3 123.3 all-reduce.13
where the time goes:
time: 1040 us; the launch traced here: 1030 us
  waiting for transfers between devices  451 us (43%)
  matrix products  200 us (19%)
  blocking collectives  198 us (19%)
  local copies, waits for them, and re-layouts  77.7 us (7%)
  other arithmetic  64.8 us (6%)
  starting transfers between devices  22 us (2%)
  between operations  16.7 us (2%)
    reduce_scatter x1, waiting for transfers between devices, body(): lax.psum_scatter(grad_inner_weight, 'fsdp', scatter_dimension=0, tiled=True)  118 us
    reduce_scatter x1, waiting for transfers between devices, body(): lax.psum_scatter(grad_outer_weight, 'fsdp', scatter_dimension=0, tiled=True)  117 us
    psum x1, waiting for transfers between devices, body(): lax.psum(shares[0].astype(jnp.bfloat16), 'seq').astype(jnp.float32)  70.4 us
    reduce_scatter x1, waiting for transfers between devices, body(): lax.psum_scatter(grad_value_weight, 'fsdp', scatter_dimension=0, tiled=True)  53.2 us
    dot_general x6, matrix products, matmul(): return jnp.dot(left, right, preferred_element_type=jnp.float32)  50.5 us
    dot_general x6, matrix products, contract_rows(): lax.dot_general(left, right, (((0,), (0,)), ((), ())), preferred_element_...  41.3 us
    dot_general x6, matrix products, contract_cols(): lax.dot_general(left, right, (((1,), (1,)), ((), ())), preferred_element_...  34.3 us
    all_to_all x1, blocking collectives, body(): lax.all_to_all(jnp.stack(key_list), 'seq', split_axis=1, concat_axis=2, t...  27.8 us
  transfers between devices with their start and end apart: 18, of which 12 were waited for; matrix products, arithmetic and copies ran while one was open for 26% of the time, Pallas kernels for 0%

commit v1 on v0

v1 whole, which is shorter than its diff:
```python
from functools import partial

import jax
import jax.numpy as jnp
from jax import lax
from jax.experimental import pallas as pl
from jax.experimental.pallas import tpu as pltpu
from jax.sharding import PartitionSpec as P

HEAD_DIM = 64
PAIR = 2 * HEAD_DIM
BLOCK = 256
F32 = jnp.float32
BF16 = jnp.bfloat16

PHI_POLY = (
    0.11962928975633808,
    0.12075411058236112,
    0.09991242675653945,
    0.12856547821204567,
    -0.053691543682108024,
    0.20636272322745108,
    -0.15720876784307727,
    0.03567620985200702,
)


def normal_cdf_pdf(z):
    u = jnp.abs(z)
    bell = jnp.exp(-0.5 * u * u)
    t = 1.0 / (1.0 + 0.3 * u)
    poly = jnp.full_like(t, PHI_POLY[-1])
    for coef in PHI_POLY[-2::-1]:
        poly = poly * t + coef
    tail = bell * (t * poly)
    return jnp.where(z < 0, tail, 1.0 - tail), bell * 0.3989422804014327


def layer_norm(rows, gain, shift):
    centred = rows - jnp.mean(rows, axis=-1, keepdims=True)
    factor = lax.rsqrt(jnp.mean(centred * centred, axis=-1, keepdims=True) + 1e-05)
    normed = centred * factor
    return (normed * gain + shift, normed, factor)


def norm_back(upstream, normed, factor, gain):
    scaled = upstream * gain
    return factor * (
        scaled
        - jnp.mean(scaled, axis=-1, keepdims=True)
        - normed * jnp.mean(scaled * normed, axis=-1, keepdims=True)
    )


def matmul(left, right):
    return jnp.dot(left, right, preferred_element_type=F32)


def contract_rows(left, right):
    return lax.dot_general(left, right, (((0,), (0,)), ((), ())), preferred_element_type=F32)


def contract_cols(left, right):
    return lax.dot_general(left, right, (((1,), (1,)), ((), ())), preferred_element_type=F32)


def column_sum(rows):
    return jnp.sum(rows.astype(F32), axis=0)


def half_rows(block, head):
    zero = jnp.zeros((HEAD_DIM, block.shape[1]), block.dtype)
    part = block[head * HEAD_DIM : (head + 1) * HEAD_DIM]
    return jnp.concatenate([part, zero] if head == 0 else [zero, part], axis=0)


def forward_kernel(bounds, qkv_ref, row_ref, col_ref, mixed_ref, logsum_ref, vt_ref):
    length = qkv_ref.shape[0]
    q_t = qkv_ref[:, :PAIR].T
    vt_ref[...] = qkv_ref[:, 2 * PAIR :].T
    for i in range(length // BLOCK):
        at = slice(i * BLOCK, (i + 1) * BLOCK)
        row = row_ref[:, at]
        halves = [half_rows(q_t[:, at], head) for head in range(2)]

        def step(j, carry):
            span = pl.ds(pl.multiple_of(j * BLOCK, BLOCK), BLOCK)
            keys = qkv_ref[span, PAIR : 2 * PAIR]
            same = col_ref[span, :] == row
            new = []
            for head in range(2):
                peak, total, mix = carry[head]
                scores = jnp.where(same, matmul(keys, halves[head]), -1e30)
                top = jnp.maximum(peak, jnp.max(scores, axis=0, keepdims=True))
                weights = jnp.exp(scores - top)
                decay = jnp.exp(peak - top)
                total = total * decay + jnp.sum(weights, axis=0, keepdims=True)
                v_t = vt_ref[head * HEAD_DIM : (head + 1) * HEAD_DIM, span]
                mix = mix * decay + matmul(v_t, weights.astype(BF16))
                new.append((top, total, mix))
            return tuple(new)

        first = (
            jnp.full((1, BLOCK), -1e30, F32),
            jnp.zeros((1, BLOCK), F32),
            jnp.zeros((HEAD_DIM, BLOCK), F32),
        )
        done = lax.fori_loop(bounds[i, 0], bounds[i, 1], step, (first, first))
        mixed_ref[at, :] = jnp.concatenate([d[2] / d[1] for d in done], axis=0).T.astype(BF16)
        for head in range(2):
            logsum_ref[0, head : head + 1, at] = done[head][0] + jnp.log(done[head][1])


def backward_kernel(
    bounds, qkv_ref, row_ref, col_ref, mixed_ref, logsum_ref, grad_ref, out_ref, kt_ref, dk_ref, dv_ref
):
    length = qkv_ref.shape[0]
    q_all = qkv_ref[:, :PAIR]
    g_all = grad_ref[...]
    q_t = q_all.T
    g_t = g_all.T
    kt_ref[...] = qkv_ref[:, PAIR : 2 * PAIR].T
    dk_ref[...] = jnp.zeros_like(dk_ref)
    dv_ref[...] = jnp.zeros_like(dv_ref)
    product_t = (g_all.astype(F32) * mixed_ref[...].astype(F32)).T
    delta = [
        jnp.sum(product_t[head * HEAD_DIM : (head + 1) * HEAD_DIM], axis=0, keepdims=True) for head in range(2)
    ]
    lane = lax.broadcasted_iota(jnp.int32, (BLOCK, PAIR), 1)
    for i in range(length // BLOCK):
        at = slice(i * BLOCK, (i + 1) * BLOCK)
        row = row_ref[:, at]
        q_halves = [half_rows(q_t[:, at], head) for head in range(2)]
        g_halves = [half_rows(g_t[:, at], head) for head in range(2)]
        low, high = lane < HEAD_DIM, lane >= HEAD_DIM
        zero = jnp.zeros((BLOCK, PAIR), BF16)
        q_split = jnp.concatenate([jnp.where(low, q_all[at], zero), jnp.where(high, q_all[at], zero)], axis=0)
        g_split = jnp.concatenate([jnp.where(low, g_all[at], zero), jnp.where(high, g_all[at], zero)], axis=0)
        logsum = [logsum_ref[0, head : head + 1, at] for head in range(2)]

        def step(j, carry):
            span = pl.ds(pl.multiple_of(j * BLOCK, BLOCK), BLOCK)
            keys = qkv_ref[span, PAIR : 2 * PAIR]
            values = qkv_ref[span, 2 * PAIR :]
            same = col_ref[span, :] == row
            probs_low, grad_low, new = [], [], []
            for head in range(2):
                scores = jnp.where(same, matmul(keys, q_halves[head]), -1e30)
                probs = jnp.exp(scores - logsum[head])
                grad_probs = matmul(values, g_halves[head])
                grad_scores = (probs * (grad_probs - delta[head][:, at])).astype(BF16)
                probs_low.append(probs.astype(BF16))
                grad_low.append(grad_scores)
                k_t = kt_ref[head * HEAD_DIM : (head + 1) * HEAD_DIM, span]
                new.append(carry[head] + matmul(k_t, grad_scores))
            dv_ref[span, :] += matmul(jnp.concatenate(probs_low, axis=1), g_split)
            dk_ref[span, :] += matmul(jnp.concatenate(grad_low, axis=1), q_split)
            return tuple(new)

        empty = jnp.zeros((HEAD_DIM, BLOCK), F32)
        done = lax.fori_loop(bounds[i, 0], bounds[i, 1], step, (empty, empty))
        grad_q = jnp.concatenate(done, axis=0).T
        out_ref[at, :PAIR] = (grad_q * 0.125).astype(BF16)
    out_ref[:, PAIR : 2 * PAIR] = dk_ref[...].astype(BF16)
    out_ref[:, 2 * PAIR :] = dv_ref[...].astype(BF16)


def block_bounds(starts):
    blocks = starts.reshape(-1, BLOCK)
    least, most = blocks[:, 0], blocks[:, -1]
    low = jnp.sum(most[None, :] < least[:, None], axis=1)
    high = jnp.sum(least[None, :] <= most[:, None], axis=1)
    return jnp.stack([low, high], axis=1).astype(jnp.int32)


def attention_forward(qkv, starts):
    length, packed = qkv.shape
    pairs = packed // (3 * PAIR)
    return pl.pallas_call(
        forward_kernel,
        grid_spec=pltpu.PrefetchScalarGridSpec(
            num_scalar_prefetch=1,
            grid=(pairs,),
            in_specs=[
                pl.BlockSpec((length, 3 * PAIR), lambda p, b: (0, p)),
                pl.BlockSpec((1, length), lambda p, b: (0, 0)),
                pl.BlockSpec((length, 1), lambda p, b: (0, 0)),
            ],
            out_specs=[
                pl.BlockSpec((length, PAIR), lambda p, b: (0, p)),
                pl.BlockSpec((1, 2, length), lambda p, b: (p, 0, 0)),
            ],
            scratch_shapes=[pltpu.VMEM((PAIR, length), BF16)],
        ),
        out_shape=[
            jax.ShapeDtypeStruct((length, pairs * PAIR), BF16),
            jax.ShapeDtypeStruct((pairs, 2, length), F32),
        ],
        compiler_params=pltpu.CompilerParams(vmem_limit_bytes=40 * 1024 * 1024),
        cost_estimate=pl.CostEstimate(
            flops=pairs * 2 * length * length * HEAD_DIM * 4,
            bytes_accessed=length * packed * 3,
            transcendentals=pairs * 2 * length * length,
        ),
        name="attend",
    )(block_bounds(starts), qkv, starts[None, :], starts[:, None])


def attention_backward(qkv, starts, mixed, logsum, grad):
    length, packed = qkv.shape
    pairs = packed // (3 * PAIR)
    return pl.pallas_call(
        backward_kernel,
        grid_spec=pltpu.PrefetchScalarGridSpec(
            num_scalar_prefetch=1,
            grid=(pairs,),
            in_specs=[
                pl.BlockSpec((length, 3 * PAIR), lambda p, b: (0, p)),
                pl.BlockSpec((1, length), lambda p, b: (0, 0)),
                pl.BlockSpec((length, 1), lambda p, b: (0, 0)),
                pl.BlockSpec((length, PAIR), lambda p, b: (0, p)),
                pl.BlockSpec((1, 2, length), lambda p, b: (p, 0, 0)),
                pl.BlockSpec((length, PAIR), lambda p, b: (0, p)),
            ],
            out_specs=pl.BlockSpec((length, 3 * PAIR), lambda p, b: (0, p)),
            scratch_shapes=[
                pltpu.VMEM((PAIR, length), BF16),
                pltpu.VMEM((length, PAIR), F32),
                pltpu.VMEM((length, PAIR), F32),
            ],
        ),
        out_shape=jax.ShapeDtypeStruct((length, packed), BF16),
        compiler_params=pltpu.CompilerParams(vmem_limit_bytes=40 * 1024 * 1024),
        cost_estimate=pl.CostEstimate(
            flops=pairs * 2 * length * length * HEAD_DIM * 10,
            bytes_accessed=length * packed * 6,
            transcendentals=pairs * 2 * length * length,
        ),
        name="attend_back",
    )(block_bounds(starts), qkv, starts[None, :], starts[:, None], mixed, logsum, grad)


def flip(x, axis, size, bit):
    return lax.ppermute(x, axis, [(i, i ^ bit) for i in range(size)])


class Cube:
    def __init__(self):
        self.me = lax.axis_index("fsdp")
        self.n = 8

    def swap(self, x, bit):
        return flip(x, "fsdp", 8, bit)

    def gather(self, piece, route):
        first, second = (2, 4) if route == 0 else (4, 2)
        near = self.swap(piece, first)
        side = self.swap(piece, second)
        far = self.swap(near, second)
        out = []
        for mask, block in ((0, piece), (first, near), (second, side), (6, far)):
            out.append((self.me ^ mask, block))
            out.append((self.me ^ mask ^ 1, self.swap(block, 1)))
        return out

    def scatter(self, left, right, route):
        block = left.shape[1] // 8
        width = right.shape[1]

        def part(masks):
            picked = [lax.dynamic_slice_in_dim(left, (self.me ^ m) * block, block, 1) for m in masks]
            return contract_rows(jnp.concatenate(picked, axis=1), right).astype(BF16)

        first, second = (2, 4) if route == 0 else (4, 2)
        order = (0, second, first, 6)
        send = part([m ^ 1 for m in order]).reshape(4, block, width)
        keep = part(order).reshape(4, block, width)
        got = self.swap(send, 1)
        there = (keep[2:].astype(F32) + got[2:].astype(F32)).astype(BF16)
        got_two = self.swap(there, first)
        here = keep[:2].astype(F32) + got[:2].astype(F32) + got_two.astype(F32)
        last = self.swap(here[1].astype(BF16), second)
        return here[0] + last.astype(F32)

    def scatter_small(self, rows):
        cube = rows.reshape(2, 2, 2, -1)
        for axis, bit in ((0, 4), (1, 2), (2, 1)):
            cube = jnp.where(self.me & bit != 0, jnp.flip(cube, axis), cube)
        cube = cube[:, :, 0] + self.swap(cube[:, :, 1], 1)
        cube = cube[:, 0] + self.swap(cube[:, 1], 2)
        return cube[0] + self.swap(cube[1], 4)


class Line:
    def __init__(self, n):
        self.n = n

    def gather(self, piece, route):
        whole = lax.all_gather(piece, "fsdp", axis=0, tiled=False)
        return [(i, whole[i]) for i in range(self.n)]

    def scatter(self, left, right, route):
        part = contract_rows(left, right).astype(BF16)
        return lax.psum_scatter(part, "fsdp", scatter_dimension=0, tiled=True).astype(F32)

    def scatter_small(self, rows):
        return lax.psum_scatter(rows, "fsdp", scatter_dimension=0, tiled=False)


def assemble(pieces, rows):
    cols = pieces[0][1].shape[1]
    whole = jnp.zeros((rows * len(pieces), cols), pieces[0][1].dtype)
    for owner, block in pieces:
        whole = lax.dynamic_update_slice(whole, block[:rows], (owner * rows, 0))
    return whole


def pair_pack(parts):
    rows = parts[0].shape[0]
    return jnp.stack([p.reshape(rows, -1, PAIR) for p in parts], axis=2).reshape(rows, -1)


def pair_unpack(packed):
    rows = packed.shape[0]
    cut = packed.reshape(rows, -1, 3, PAIR)
    return [cut[:, :, i].reshape(rows, -1) for i in range(3)]


def body(
    fsdp,
    stream_in,
    timestep,
    doc_start,
    query_weight,
    key_weight,
    value_weight,
    output_weight,
    query_bias,
    value_bias,
    output_bias,
    first_gain,
    first_shift,
    inner_weight,
    inner_bias,
    outer_weight,
    outer_bias,
    second_gain,
    second_shift,
    cotangent,
):
    links = Cube() if fsdp == 8 else Line(fsdp)
    streams, tok, width = stream_in.shape
    own_rows = query_weight.shape[0]
    half = width // 2
    ff = inner_weight.shape[1]
    length = 4 * tok
    z = lax.axis_index("seq")
    h, s = z % 2, z // 2

    def flip_h(x):
        return flip(x, "seq", 4, 1)

    def flip_s(x):
        return flip(x, "seq", 4, 2)

    def in_order(mine, other):
        return jnp.where(s == 0, jnp.concatenate([mine, other]), jnp.concatenate([other, mine]))

    def pick(x, index, axis=0):
        return lax.dynamic_index_in_dim(x, index, axis, keepdims=False)

    own = pick(stream_in, s)
    distant = flip_s(pick(stream_in, 1 - s))
    beside = flip_h(own)
    corner = flip_h(distant)
    moved = flip_s(pick(cotangent, 1 - s))
    upstream = in_order(pick(cotangent, s), moved).astype(F32)

    head_cols = [lax.dynamic_slice_in_dim(w, h * half, half, 1) for w in (query_weight, key_weight, value_weight)]
    small = jnp.concatenate(
        [
            query_bias,
            value_bias,
            output_bias,
            first_gain,
            first_shift,
            outer_bias,
            second_gain,
            second_shift,
            inner_bias,
        ]
    )
    packed = pair_pack(head_cols)
    if fsdp == 8:
        packed = jnp.concatenate([packed, jnp.broadcast_to(small[None, :], (16, small.shape[0]))])
        qkv_pieces = links.gather(packed, 0)
        small_rows = jnp.zeros((fsdp, small.shape[0]), BF16)
        for owner, block in qkv_pieces:
            small_rows = lax.dynamic_update_slice(small_rows, block[own_rows : own_rows + 1], (owner, 0))
    else:
        qkv_pieces = links.gather(packed, 0)
        small_rows = lax.all_gather(small, "fsdp", axis=0, tiled=False)
    full_qkv = assemble(qkv_pieces, own_rows)
    full_output = assemble(links.gather(output_weight, 1), own_rows)
    full_inner = assemble(links.gather(inner_weight, 0), own_rows)
    full_outer = assemble(links.gather(outer_weight, 1), outer_weight.shape[0])
    small_rows = small_rows.astype(F32)
    qbias, vbias, obias, gain_one, shift_one, obias_two, gain_two, shift_two = [
        small_rows[:, i * own_rows : (i + 1) * own_rows].reshape(-1) for i in range(8)
    ]
    ibias = small_rows[:, 8 * own_rows :].reshape(-1)

    ts = pick(timestep, s).astype(F32)
    stream = jnp.zeros((length, width), BF16)
    for mask, block in ((0, own), (1, beside), (2, distant), (3, corner)):
        stream = lax.dynamic_update_slice(stream, block, ((z ^ mask) * tok, 0))
    stream_low = (stream.astype(F32) + ts).astype(BF16)
    hidden = in_order(own, distant).astype(F32) + ts
    starts = pick(doc_start, s)

    qb = lax.dynamic_slice_in_dim(qbias, h * half, half, 0)
    vb = lax.dynamic_slice_in_dim(vbias, h * half, half, 0)
    bias_row = pair_pack([qb[None], jnp.zeros_like(qb)[None], vb[None]])
    scale_row = pair_pack([jnp.full((1, half), 0.125, F32), jnp.ones((1, half), F32), jnp.ones((1, half), F32)])
    qkv = ((matmul(stream_low, full_qkv) + bias_row) * scale_row).astype(BF16)
    mixed_heads, logsum = attention_forward(qkv, starts)

    def rows_of(x, parity):
        cut = x.reshape(2, 2, tok, x.shape[1])
        return pick(cut, parity, 1).reshape(2 * tok, x.shape[1])

    def swap_heads(mine, other):
        return jnp.where(h == 0, jnp.concatenate([mine, other], axis=1), jnp.concatenate([other, mine], axis=1))

    mixed = swap_heads(rows_of(mixed_heads, h), flip_h(rows_of(mixed_heads, 1 - h)))
    attended = matmul(mixed, full_output) + obias
    first_out, first_normed, first_factor = layer_norm(hidden + attended, gain_one, shift_one)
    first_low = first_out.astype(BF16)

    inner = matmul(first_low, full_inner) + ibias
    cdf, pdf = normal_cdf_pdf(inner)
    active = (inner * cdf).astype(BF16)
    slope = (cdf + inner * pdf).astype(BF16)
    second_in = first_out + matmul(active, full_outer) + obias_two
    result, second_normed, second_factor = layer_norm(second_in, gain_two, shift_two)
    result = result.astype(BF16)

    grad_second_gain = jnp.sum(upstream * second_normed, axis=0)
    grad_second_shift = jnp.sum(upstream, axis=0)
    grad_second_in = norm_back(upstream, second_normed, second_factor, gain_two)
    grad_outer = grad_second_in.astype(BF16)
    grad_outer_bias = column_sum(grad_outer)
    outer_share = links.scatter(active, grad_outer, 0)
    grad_active = contract_cols(grad_outer, full_outer)
    grad_inner = (grad_active * slope.astype(F32)).astype(BF16)
    grad_inner_bias = column_sum(grad_inner)
    inner_share = links.scatter(first_low, grad_inner, 1)
    grad_first_out = grad_second_in + contract_cols(grad_inner, full_inner)
    grad_first_gain = jnp.sum(grad_first_out * first_normed, axis=0)
    grad_first_shift = jnp.sum(grad_first_out, axis=0)
    grad_first_in = norm_back(grad_first_out, first_normed, first_factor, gain_one)
    grad_attended = grad_first_in.astype(BF16)
    grad_output_bias = column_sum(grad_attended)
    grad_mixed = contract_cols(grad_attended, full_output).astype(BF16)
    grad_cols = grad_mixed.reshape(2 * tok, 2, half)
    received = flip_h(pick(grad_cols, 1 - h, 1)).reshape(2, 1, tok, half)
    kept = pick(grad_cols, h, 1).reshape(2, 1, tok, half)
    grad_heads = jnp.where(
        h == 0, jnp.concatenate([kept, received], axis=1), jnp.concatenate([received, kept], axis=1)
    ).reshape(length, half)
    output_share = links.scatter(mixed, grad_attended, 0)
    grad_qkv = attention_backward(qkv, starts, mixed_heads, logsum, grad_heads)
    partial_hidden = contract_cols(grad_qkv, full_qkv)
    away = flip_h(rows_of(partial_hidden, 1 - h).astype(BF16)).astype(F32)
    grad_hidden = (grad_first_in + rows_of(partial_hidden, h) + away).reshape(2, tok, width)
    qkv_share = links.scatter(stream_low, grad_qkv, 0)
    grad_q_cols, _, grad_v_cols = pair_unpack(column_sum(grad_qkv)[None])

    grad_own = pick(grad_hidden, s)
    grad_away = flip_s(pick(grad_hidden, 1 - s).astype(BF16)).astype(F32)
    input_grad = jnp.where(s == 0, jnp.stack([grad_own, grad_away]), jnp.stack([grad_away, grad_own]))
    result = result.reshape(2, tok, width)
    result_own = pick(result, s)
    result_away = flip_s(pick(result, 1 - s))
    layer_out = jnp.where(s == 0, jnp.stack([result_own, result_away]), jnp.stack([result_away, result_own]))

    def seq_sum(share):
        rows = share.shape[0]
        cut = share.reshape(2, rows // 2, -1)
        mine = pick(cut, h) + flip_h(pick(cut, 1 - h).astype(BF16)).astype(F32)
        cut = mine.reshape(2, rows // 4, -1)
        mine = (pick(cut, s) + flip_s(pick(cut, 1 - s).astype(BF16)).astype(F32)).astype(BF16)
        by_s = flip_s(mine)
        by_h = flip_h(mine)
        by_both = flip_h(by_s)
        out = jnp.zeros(share.shape, F32)
        for hh, ss, block in ((h, s, mine), (h, 1 - s, by_s), (1 - h, s, by_h), (1 - h, 1 - s, by_both)):
            out = lax.dynamic_update_slice(out, block.astype(F32), ((2 * hh + ss) * (rows // 4), 0))
        return out

    def seq_sum_small(share):
        share = share + flip_h(share)
        return share + flip_s(share)

    outer_grad = seq_sum(outer_share)
    inner_grad = seq_sum(inner_share)
    output_grad = seq_sum(output_share)
    qkv_half = (qkv_share + flip_s(qkv_share.astype(BF16)).astype(F32)).astype(BF16)
    qkv_other = flip_h(qkv_half)
    qkv_grads = [
        swap_heads(mine, other).astype(F32) for mine, other in zip(pair_unpack(qkv_half), pair_unpack(qkv_other))
    ]
    early = jnp.concatenate(
        [
            v.reshape(fsdp, -1)
            for v in (
                grad_output_bias,
                grad_first_gain,
                grad_first_shift,
                grad_outer_bias,
                grad_second_gain,
                grad_second_shift,
                grad_inner_bias,
            )
        ],
        axis=1,
    )
    early = seq_sum_small(links.scatter_small(early))
    zero_half = jnp.zeros((half,), F32)

    def widen(v):
        v = v.reshape(-1)
        return jnp.where(h == 0, jnp.concatenate([v, zero_half]), jnp.concatenate([zero_half, v])).reshape(fsdp, -1)

    late = jnp.concatenate([widen(grad_q_cols), widen(grad_v_cols)], axis=1)
    late = seq_sum_small(links.scatter_small(late))
    cut = [early[i * own_rows : (i + 1) * own_rows] for i in range(6)]
    return (
        layer_out,
        input_grad,
        qkv_grads[0],
        qkv_grads[1],
        qkv_grads[2],
        output_grad,
        late[:own_rows],
        late[own_rows:],
        cut[0],
        cut[1],
        cut[2],
        inner_grad,
        early[6 * own_rows :],
        outer_grad,
        cut[3],
        cut[4],
        cut[5],
    )


def solution(mesh):
    rows = P("fsdp", "seq", None)
    mat = P("fsdp", None)
    vec = P("fsdp")
    in_specs = (
        (rows, mat, mat) + (mat,) * 4 + (vec,) * 5 + (mat, vec, mat, vec, vec, vec) + (rows,)
    )
    out_specs = (rows, rows) + (mat,) * 4 + (vec,) * 5 + (mat, vec, mat, vec, vec, vec)
    return jax.shard_map(
        partial(body, mesh.shape["fsdp"]), mesh=mesh, in_specs=in_specs, out_specs=out_specs, check_vma=False
    )
```

time: 1040 us -> 635 us (0.61)
  waiting for transfers between devices: 451 us -> 199 us
  blocking collectives: 198 us -> 0 us
  matrix products: 200 us -> 88.5 us
  local copies, waits for them, and re-layouts: 77.7 us -> 161 us
  Pallas kernels: 0 us -> 63.6 us
  starting transfers between devices: 22 us -> 62.1 us
  other arithmetic: 64.8 us -> 47.2 us
  between operations: 16.7 us -> 2.91 us
    reduce_scatter x6 -> x0, waiting for transfers between devices: 289 us -> none  [the longest x1 118 us: body(): lax.psum_scatter(grad_inner_weight, 'fsdp', scatter_dimension=0, tiled=True)]
    ppermute x0 -> x76, waiting for transfers between devices: none -> 199 us  [flip(): return lax.ppermute(x, axis, [(i, i ^ bit) for i in range(size)])]
    dot_general x34 -> x4, matrix products: 125 us -> 33.1 us  [matmul(): return jnp.dot(left, right, preferred_element_type=F32)]
    all_to_all x3 -> x0, blocking collectives: 83.3 us -> none  [the longest x1 27.8 us: body(): lax.all_to_all(jnp.stack(key_list), 'seq', split_axis=1, concat_axis=2, t...]
    all_gather x9 -> x0, blocking collectives: 76.9 us -> none  [the longest x1 10.3 us: body(): lax.all_gather(query_bias, 'fsdp', axis=0, tiled=True)]
    psum x1 -> x0, waiting for transfers between devices: 70.4 us -> none  [body(): lax.psum(shares[0].astype(jnp.bfloat16), 'seq').astype(jnp.float32)]
    pallas_call x0 -> x2, Pallas kernels: none -> 63.6 us  [the longest x1 33.3 us: attention_backward(): pl.pallas_call(backward_kernel, grid_spec=pltpu.PrefetchScalarGridSpec(nu...]
    ppermute x0 -> x76, starting transfers between devices: none -> 62.1 us  [flip(): return lax.ppermute(x, axis, [(i, i ^ bit) for i in range(size)])]
  transfers between devices with their start and end apart: 18 -> 76, of which waited for: 12 -> 28; matrix products, arithmetic and copies ran while one was open for 26% -> 44% of each run, Pallas kernels for 0% -> 10%
where the time goes in v1:
time: 635 us; the launch traced here: 624 us
  waiting for transfers between devices  199 us (31%)
  local copies, waits for them, and re-layouts  161 us (25%)
  matrix products  88.5 us (14%)
  Pallas kernels  63.6 us (10%)
  starting transfers between devices  62.1 us (10%)
  other arithmetic  47.2 us (7%)
    ppermute x76, waiting for transfers between devices, flip(): return lax.ppermute(x, axis, [(i, i ^ bit) for i in range(size)])  199 us
    ppermute x76, starting transfers between devices, flip(): return lax.ppermute(x, axis, [(i, i ^ bit) for i in range(size)])  62.1 us
    dynamic_update_slice x32, local copies, waits for them, and re-layouts, assemble(): whole = lax.dynamic_update_slice(whole, block[:rows], (owner * rows, 0))  54.6 us
    pallas_call x1, Pallas kernels, attention_backward(): pl.pallas_call(backward_kernel, grid_spec=pltpu.PrefetchScalarGridSpec(nu...  33.3 us
    dot_general x4, matrix products, contract_cols(): lax.dot_general(left, right, (((1,), (1,)), ((), ())), preferred_element_...  33.2 us
    dot_general x4, matrix products, matmul(): return jnp.dot(left, right, preferred_element_type=F32)  33.1 us
    pallas_call x1, Pallas kernels, attention_forward(): pl.pallas_call(forward_kernel, grid_spec=pltpu.PrefetchScalarGridSpec(num...  30.2 us
    slice x14, local copies, waits for them, and re-layouts, assemble(): whole = lax.dynamic_update_slice(whole, block[:rows], (owner * rows, 0))  24.8 us
  transfers between devices with their start and end apart: 76, of which 28 were waited for; matrix products, arithmetic and copies ran while one was open for 44% of the time, Pallas kernels for 10%

profile of v1, /device:TPU:0, one launch (start us, length us, event | category | flops | bytes accessed | tf_op | source)
XLA Modules:
  0.0 624.3 jit_solution(4857643007109268160)
XLA Ops:
  11.5 2.5 collective-permute-start.4
  27.1 4.4 broadcast_in_dim.24
  34.8 4.4 broadcast_in_dim.26
  66.0 2.7 collective-permute-start
  77.5 15.0 %collective-permute-done = bf16[256,1024]{1,0:T(8,128)(2,1)} collective-permute-done((bf16[256,1024]{1,0:T(8,128)(2,1)}, bf16[256,1024]{1,0:T(8,128)(2,1)}, u32[]{:S(2)}, u32[]{:S(2)}) %collective-permute-start) | collective-permute-done | bytes 524320 | tf_op jit(solution)/shard_map/ppermute | solution.py:244
  127.8 5.3 collective-permute-done.26
  144.6 5.6 multiply_convert_fusion.2.qkv_ref
  150.2 30.2 %attend.1 = (bf16[1024,512]{1,0:T(8,128)(2,1)S(1)}, f32[4,2,1024]{2,1,0:T(2,128)S(1)}) custom-call(s32[4,2]{1,0:T(4,128)S(1)} %pad_add_fusion.bounds, bf16[1024,1536]{1,0:T(8,128)(2,1)S(1)} %multiply_convert_fusion.2.qkv_ref, s32[1,1024]{1,0:T(1,128)S(1)} %get-tuple-element.48.row_ref, s32[1024,1]{1,0:T(8,128)S(1)} %copy.175.col_ref), custom_call_target="tpu_custom_call" | custom-call | flops 2147483648 | bytes 4718592 | tf_op jit(solution)/shard_map/attend/pallas_call | solution.py:179
  186.4 8.5 %collective-permute-done.10 = bf16[512,512]{1,0:T(8,128)(2,1)S(1)} collective-permute-done((bf16[512,512]{1,0:T(8,128)(2,1)S(1)}, bf16[512,512]{1,0:T(8,128)(2,1)S(1)}, u32[]{:S(2)}, u32[]{:S(2)}) %collective-permute-start.10) | collective-permute-done | bytes 524320 | tf_op jit(solution)/shard_map/ppermute | solution.py:244
  195.2 3.6 fusion.127
  221.1 16.2 %multiply_convert_fusion.1 = (bf16[512,4096]{1,0:T(8,128)(2,1)S(1)}, f32[512,4096]{1,0:T(8,128)}) fusion(f32[4096]{0:T(1024)S(1)} %bitcast.277, bf16[512,1024]{1,0:T(8,128)(2,1)S(1)} %fusion.29, bf16[1024,4096]{1,0:T(8,128)(2,1)} %constant_dynamic-update-slice_fusion.8), kind=kOutput, calls=%fused_computation.6 | convolution fusion | flops 4353687552 | bytes 22036480 | tf_op jit(solution)/shard_map/dot_general | solution.py:56
  238.4 7.8 %fusion.128 = (f32[512]{0:T(512)S(1)}, f32[512,1024]{1,0:T(8,128)S(1)}) fusion(f32[1024]{0:T(1024)S(1)} %get-tuple-element.107, bf16[512,4096]{1,0:T(8,128)(2,1)S(1)} %get-tuple-element.135, bf16[4096,1024]{1,0:T(8,128)(2,1)} %constant_dynamic-update-slice_fusion, f32[1024]{0:T(1024)S(1)} %get-tuple-element.108, f32[1024]{0:T(1024)S(1)} %get-tuple-element.109, ...), kind=kOutput, calls=%fused_computation.352 | convolution fusion | flops 4298636800 | bytes 16795648 | tf_op jit(solution)/shard_map/dot_general | solution.py:56
  247.6 2.5 convert_reduce_fusion.3
  253.3 16.5 %convert_reduce_fusion = (f32[4096]{0:T(1024)S(1)}, bf16[512,4096]{1,0:T(8,128)(2,1)S(1)}) fusion(f32[512,4096]{1,0:T(8,128)} %get-tuple-element.136, f32[4096]{0:T(1024)S(1)} %bitcast.278, bf16[512,1024]{1,0:T(8,128)(2,1)S(1)} %get-tuple-element.39, bf16[4096,1024]{1,0:T(8,128)(2,1)} %constant_dynamic-update-slice_fusion), kind=kOutput, calls=%fused_computation.3 | convolution fusion | flops 4368363520 | bytes 22052864 | tf_op jit(solution)/shard_map/dot_general | solution.py:64
  269.8 10.4 %multiply_reduce_fusion = (f32[1024]{0:T(1024)S(1)}, f32[512]{0:T(512)S(1)}, f32[512]{0:T(512)S(1)}, f32[1024]{0:T(1024)S(1)}, f32[512,1024]{1,0:T(8,128)S(1)}) fusion(f32[512,1024]{1,0:T(8,128)S(1)} %get-tuple-element.134, f32[512]{0:T(512)S(1)} %add_rsqrt_fusion.1, f32[512]{0:T(512)S(1)} %broadcast_multiply_fusion.5, f32[1024]{0:T(1024)S(1)} %get-tuple-element.109, ...), kind=kOutput, calls=%fused_computation.59 | convolution fusion | flops 4309120000 | bytes 19955712 | tf_op jit(solution)/shard_map/dot_general | solution.py:64
  282.3 2.9 convolution_convert_fusion.6
  297.9 4.4 convolution_convert_fusion.2
  305.5 2.4 fusion.114
  313.4 4.5 convolution_convert_fusion
  318.8 2.6 fusion.113
  325.3 33.3 %attend_back.1 = bf16[1024,1536]{1,0:T(8,128)(2,1)S(1)} custom-call(s32[4,2]{1,0:T(4,128)S(1)} %pad_add_fusion.bounds, bf16[1024,1536]{1,0:T(8,128)(2,1)S(1)} %copy-done.7, s32[1,1024]{1,0:T(1,128)S(1)} %get-tuple-element.48.row_ref, s32[1024,1]{1,0:T(8,128)S(1)} %copy-done.5, bf16[1024,512]{1,0:T(8,128)(2,1)S(1)} %copy-done.3, ...), custom_call_target="tpu_custom_call" | custom-call | flops 5368709120 | bytes 9437184 | tf_op jit(solution)/shard_map/attend_back/pallas_call | solution.py:212
  358.6 3.4 fusion.129
  365.7 2.9 convolution_convert_fusion.5
  376.2 3.0 convolution_convert_fusion.4
  382.0 2.9 copy.182
  384.9 4.4 collective-permute-done.53
  398.6 2.7 copy.183
  411.5 22.9 %collective-permute-done.46 = bf16[32,1024]{1,0:T(8,128)(2,1)S(1)} collective-permute-done((bf16[32,1024]{1,0:T(8,128)(2,1)S(1)}, bf16[32,1024]{1,0:T(8,128)(2,1)S(1)}, u32[]{:S(2)}, u32[]{:S(2)}) %collective-permute-start.46) | collective-permute-done | bytes 65568 | tf_op jit(solution)/shard_map/ppermute | solution.py:244
  442.4 3.7 fusion.3
  447.0 6.3 %collective-permute-done.39 = bf16[128,1536]{0,1:T(8,128)(2,1)S(1)} collective-permute-done((bf16[128,1536]{0,1:T(8,128)(2,1)S(1)}, bf16[128,1536]{0,1:T(8,128)(2,1)S(1)}, u32[]{:S(2)}, u32[]{:S(2)}) %collective-permute-start.39) | collective-permute-done | bytes 393248 | tf_op jit(solution)/shard_map/ppermute | solution.py:244
  455.8 13.6 %collective-permute-done.40 = bf16[128,1536]{0,1:T(8,128)(2,1)S(1)} collective-permute-done((bf16[128,1536]{0,1:T(8,128)(2,1)S(1)}, bf16[128,1536]{0,1:T(8,128)(2,1)S(1)}, u32[]{:S(2)}, u32[]{:S(2)}) %collective-permute-start.40) | collective-permute-done | bytes 393248 | tf_op jit(solution)/shard_map/ppermute | solution.py:244
  470.1 4.0 fusion.1
  474.6 21.5 %collective-permute-done.61 = bf16[2,128,4096]{2,1,0:T(8,128)(2,1)} collective-permute-done((bf16[2,128,4096]{2,1,0:T(8,128)(2,1)}, bf16[2,128,4096]{2,1,0:T(8,128)(2,1)}, u32[]{:S(2)}, u32[]{:S(2)}) %collective-permute-start.61) | collective-permute-done | bytes 2097184 | tf_op jit(solution)/shard_map/ppermute | solution.py:244
  496.1 3.2 fusion.4
  504.9 18.0 %collective-permute-done.69 = bf16[2,512,1024]{2,1,0:T(8,128)(2,1)} collective-permute-done((bf16[2,512,1024]{2,1,0:T(8,128)(2,1)}, bf16[2,512,1024]{2,1,0:T(8,128)(2,1)}, u32[]{:S(2)}, u32[]{:S(2)}) %collective-permute-start.69) | collective-permute-done | bytes 2097184 | tf_op jit(solution)/shard_map/ppermute | solution.py:244
  523.0 3.8 fusion.2
  529.9 13.4 %collective-permute-done.62 = bf16[128,4096]{1,0:T(8,128)(2,1)} collective-permute-done((bf16[128,4096]{1,0:T(8,128)(2,1)}, bf16[128,4096]{1,0:T(8,128)(2,1)}, u32[]{:S(2)}, u32[]{:S(2)}) %collective-permute-start.62) | collective-permute-done | bytes 1048608 | tf_op jit(solution)/shard_map/ppermute | solution.py:244
  554.0 9.7 %collective-permute-done.63 = bf16[64,4096]{1,0:T(8,128)(2,1)} collective-permute-done((bf16[64,4096]{1,0:T(8,128)(2,1)}, bf16[64,4096]{1,0:T(8,128)(2,1)}, u32[]{:S(2)}, u32[]{:S(2)}) %collective-permute-start.63) | collective-permute-done | bytes 524320 | tf_op jit(solution)/shard_map/ppermute | solution.py:244
  564.9 9.0 %collective-permute-done.71 = bf16[256,1024]{1,0:T(8,128)(2,1)S(1)} collective-permute-done((bf16[256,1024]{1,0:T(8,128)(2,1)S(1)}, bf16[256,1024]{1,0:T(8,128)(2,1)S(1)}, u32[]{:S(2)}, u32[]{:S(2)}) %collective-permute-start.71) | collective-permute-done | bytes 524320 | tf_op jit(solution)/shard_map/ppermute | solution.py:244
  574.4 11.6 %collective-permute-done.64 = bf16[32,4096]{1,0:T(8,128)(2,1)S(1)} collective-permute-done((bf16[32,4096]{1,0:T(8,128)(2,1)S(1)}, bf16[32,4096]{1,0:T(8,128)(2,1)S(1)}, u32[]{:S(2)}, u32[]{:S(2)}) %collective-permute-start.64) | collective-permute-done | bytes 262176 | tf_op jit(solution)/shard_map/ppermute | solution.py:244
  587.3 2.6 collective-permute-start.66
  589.9 6.5 %collective-permute-done.72 = bf16[128,1024]{1,0:T(8,128)(2,1)S(1)} collective-permute-done((bf16[128,1024]{1,0:T(8,128)(2,1)S(1)}, bf16[128,1024]{1,0:T(8,128)(2,1)S(1)}, u32[]{:S(2)}, u32[]{:S(2)}) %collective-permute-start.72) | collective-permute-done | bytes 262176 | tf_op jit(solution)/shard_map/ppermute | solution.py:244
  596.8 3.3 collective-permute-start.74
  600.1 5.7 collective-permute-done.65
  605.9 4.4 collective-permute-done.73
  610.4 2.9 collective-permute-done.74
  613.4 5.6 collective-permute-done.67
  619.0 3.7 collective-permute-done.75
  (504 shorter events, 240.8 us)
Async XLA Ops:
  11.0 36.0 %collective-permute-start.3 = (bf16[144,1536]{1,0:T(8,128)(2,1)}, bf16[144,1536]{1,0:T(8,128)(2,1)}, u32[]{:S(2)}, u32[]{:S(2)}) collective-permute-start(bf16[144,1536]{1,0:T(8,128)(2,1)} %copy.165), channel_id=1, source_target_pairs={{0,1},{1,0},{2,3},{3,2},{4,5},{5,4},{6,7},{7,6},{8,9},{9,8},{10,11... | collective-permute-start | bytes 1327112 | tf_op jit(solution)/shard_map/ppermute | solution.py:244
  11.5 42.5 %collective-permute-start.4 = (bf16[144,1536]{1,0:T(8,128)(2,1)}, bf16[144,1536]{1,0:T(8,128)(2,1)}, u32[]{:S(2)}, u32[]{:S(2)}) collective-permute-start(bf16[144,1536]{1,0:T(8,128)(2,1)} %copy.165), channel_id=1, source_target_pairs={{0,2},{1,3},{2,0},{3,1},{4,6},{5,7},{6,4},{7,5},{8,10},{9,11},{10,... | collective-permute-start | bytes 1327112 | tf_op jit(solution)/shard_map/ppermute | solution.py:244
  14.0 45.7 %collective-permute-start.6 = (bf16[144,1536]{1,0:T(8,128)(2,1)}, bf16[144,1536]{1,0:T(8,128)(2,1)}, u32[]{:S(2)}, u32[]{:S(2)}) collective-permute-start(bf16[144,1536]{1,0:T(8,128)(2,1)} %copy.165), channel_id=1, source_target_pairs={{0,4},{1,5},{2,6},{3,7},{4,0},{5,1},{6,2},{7,3},{8,12},{9,13},{10,... | collective-permute-start | bytes 1327112 | tf_op jit(solution)/shard_map/ppermute | solution.py:244
  15.5 26.0 %collective-permute-start.11 = (bf16[128,1024]{1,0:T(8,128)(2,1)}, bf16[128,1024]{1,0:T(8,128)(2,1)}, u32[]{:S(2)}, u32[]{:S(2)}) collective-permute-start(bf16[128,1024]{1,0:T(8,128)(2,1)} %param.25), channel_id=1, source_target_pairs={{0,1},{1,0},{2,3},{3,2},{4,5},{5,4},{6,7},{7,6},{8,9},{9,8},{10,11... | collective-permute-start | bytes 786440 | tf_op jit(solution)/shard_map/ppermute | solution.py:244
  15.5 28.0 %collective-permute-start.12 = (bf16[128,1024]{1,0:T(8,128)(2,1)}, bf16[128,1024]{1,0:T(8,128)(2,1)}, u32[]{:S(2)}, u32[]{:S(2)}) collective-permute-start(bf16[128,1024]{1,0:T(8,128)(2,1)} %param.25), channel_id=1, source_target_pairs={{0,4},{1,5},{2,6},{3,7},{4,0},{5,1},{6,2},{7,3},{8,12},{9,13},{10,... | collective-permute-start | bytes 786440 | tf_op jit(solution)/shard_map/ppermute | solution.py:244
  43.5 32.4 %collective-permute-start.1 = (bf16[256,1024]{1,0:T(8,128)(2,1)}, bf16[256,1024]{1,0:T(8,128)(2,1)}, u32[]{:S(2)}, u32[]{:S(2)}) collective-permute-start(bf16[256,1024]{1,0:T(8,128)(2,1)} %get-tuple-element.46), channel_id=1, source_target_pairs={{0,8},{8,0},{16,24},{24,16},{1,9},{9,1},{17,25},{25,17},{2,10},{10... | collective-permute-start | bytes 1572872 | tf_op jit(solution)/shard_map/ppermute | solution.py:244
  47.0 19.0 %collective-permute-start.13 = (bf16[128,1024]{1,0:T(8,128)(2,1)}, bf16[128,1024]{1,0:T(8,128)(2,1)}, u32[]{:S(2)}, u32[]{:S(2)}) collective-permute-start(bf16[128,1024]{1,0:T(8,128)(2,1)} %collective-permute-done.12), channel_id=1, source_target_pairs={{0,1},{1,0},{2,3},{3,2},{4,5},{5,4},{6,7},{7,6},{8,9},{9,8},{10,11... | collective-permute-start | bytes 786440 | tf_op jit(solution)/shard_map/ppermute | solution.py:244
  52.5 19.6 %collective-permute-start.16 = (bf16[128,1024]{1,0:T(8,128)(2,1)}, bf16[128,1024]{1,0:T(8,128)(2,1)}, u32[]{:S(2)}, u32[]{:S(2)}) collective-permute-start(bf16[128,1024]{1,0:T(8,128)(2,1)} %collective-permute-done.12), channel_id=1, source_target_pairs={{0,2},{1,3},{2,0},{3,1},{4,6},{5,7},{6,4},{7,5},{8,10},{9,11},{10,... | collective-permute-start | bytes 786440 | tf_op jit(solution)/shard_map/ppermute | solution.py:244
  54.0 18.1 %collective-permute-start.15 = (bf16[128,1024]{1,0:T(8,128)(2,1)}, bf16[128,1024]{1,0:T(8,128)(2,1)}, u32[]{:S(2)}, u32[]{:S(2)}) collective-permute-start(bf16[128,1024]{1,0:T(8,128)(2,1)} %collective-permute-done.14), channel_id=1, source_target_pairs={{0,1},{1,0},{2,3},{3,2},{4,5},{5,4},{6,7},{7,6},{8,9},{9,8},{10,11... | collective-permute-start | bytes 786440 | tf_op jit(solution)/shard_map/ppermute | solution.py:244
  59.7 63.7 %collective-permute-start.18 = (bf16[128,4096]{1,0:T(8,128)(2,1)}, bf16[128,4096]{1,0:T(8,128)(2,1)}, u32[]{:S(2)}, u32[]{:S(2)}) collective-permute-start(bf16[128,4096]{1,0:T(8,128)(2,1)} %param.31), channel_id=1, source_target_pairs={{0,1},{1,0},{2,3},{3,2},{4,5},{5,4},{6,7},{7,6},{8,9},{9,8},{10,11... | collective-permute-start | bytes 3145736 | tf_op jit(solution)/shard_map/ppermute | solution.py:244
  66.0 26.4 %collective-permute-start = (bf16[256,1024]{1,0:T(8,128)(2,1)}, bf16[256,1024]{1,0:T(8,128)(2,1)}, u32[]{:S(2)}, u32[]{:S(2)}) collective-permute-start(bf16[256,1024]{1,0:T(8,128)(2,1)} %dynamic-slice_bitcast_fusion.3), channel_id=1, source_target_pairs={{0,16},{8,24},{16,0},{24,8},{1,17},{9,25},{17,1},{25,9},{2,18},{10... | collective-permute-start | bytes 1572872 | tf_op jit(solution)/shard_map/ppermute | solution.py:244
  72.0 23.8 %collective-permute-start.5 = (bf16[144,1536]{1,0:T(8,128)(2,1)}, bf16[144,1536]{1,0:T(8,128)(2,1)S(1)}, u32[]{:S(2)}, u32[]{:S(2)}) collective-permute-start(bf16[144,1536]{1,0:T(8,128)(2,1)} %collective-permute-done.4), channel_id=1, source_target_pairs={{0,1},{1,0},{2,3},{3,2},{4,5},{5,4},{6,7},{7,6},{8,9},{9,8},{10,11... | collective-permute-start | bytes 1327112 | tf_op jit(solution)/shard_map/ppermute | solution.py:244
  72.1 21.6 %collective-permute-start.17 = (bf16[128,1024]{1,0:T(8,128)(2,1)}, bf16[128,1024]{1,0:T(8,128)(2,1)S(1)}, u32[]{:S(2)}, u32[]{:S(2)}) collective-permute-start(bf16[128,1024]{1,0:T(8,128)(2,1)} %collective-permute-done.16), channel_id=1, source_target_pairs={{0,1},{1,0},{2,3},{3,2},{4,5},{5,4},{6,7},{7,6},{8,9},{9,8},{10,11... | collective-permute-start | bytes 786440 | tf_op jit(solution)/shard_map/ppermute | solution.py:244
  75.9 50.6 %collective-permute-start.19 = (bf16[128,4096]{1,0:T(8,128)(2,1)}, bf16[128,4096]{1,0:T(8,128)(2,1)}, u32[]{:S(2)}, u32[]{:S(2)}) collective-permute-start(bf16[128,4096]{1,0:T(8,128)(2,1)} %param.31), channel_id=1, source_target_pairs={{0,2},{1,3},{2,0},{3,1},{4,6},{5,7},{6,4},{7,5},{8,10},{9,11},{10,... | collective-permute-start | bytes 3145736 | tf_op jit(solution)/shard_map/ppermute | solution.py:244
  95.9 22.0 %collective-permute-start.2 = (bf16[256,1024]{1,0:T(8,128)(2,1)}, bf16[256,1024]{1,0:T(8,128)(2,1)}, u32[]{:S(2)}, u32[]{:S(2)}) collective-permute-start(bf16[256,1024]{1,0:T(8,128)(2,1)} %collective-permute-done), channel_id=1, source_target_pairs={{0,8},{8,0},{16,24},{24,16},{1,9},{9,1},{17,25},{25,17},{2,10},{10... | collective-permute-start | bytes 1572872 | tf_op jit(solution)/shard_map/ppermute | solution.py:244
  103.0 23.5 %collective-permute-start.25 = (bf16[512,1024]{1,0:T(8,128)(2,1)}, bf16[512,1024]{1,0:T(8,128)(2,1)}, u32[]{:S(2)}, u32[]{:S(2)}) collective-permute-start(bf16[512,1024]{1,0:T(8,128)(2,1)} %param.33), channel_id=1, source_target_pairs={{0,1},{1,0},{2,3},{3,2},{4,5},{5,4},{6,7},{7,6},{8,9},{9,8},{10,11... | collective-permute-start | bytes 3145736 | tf_op jit(solution)/shard_map/ppermute | solution.py:244
  106.8 26.3 %collective-permute-start.26 = (bf16[512,1024]{1,0:T(8,128)(2,1)}, bf16[512,1024]{1,0:T(8,128)(2,1)}, u32[]{:S(2)}, u32[]{:S(2)}) collective-permute-start(bf16[512,1024]{1,0:T(8,128)(2,1)} %param.33), channel_id=1, source_target_pairs={{0,4},{1,5},{2,6},{3,7},{4,0},{5,1},{6,2},{7,3},{8,12},{9,13},{10,... | collective-permute-start | bytes 3145736 | tf_op jit(solution)/shard_map/ppermute | solution.py:244
  117.9 89.0 %collective-permute-start.21 = (bf16[128,4096]{1,0:T(8,128)(2,1)}, bf16[128,4096]{1,0:T(8,128)(2,1)}, u32[]{:S(2)}, u32[]{:S(2)}) collective-permute-start(bf16[128,4096]{1,0:T(8,128)(2,1)} %param.31), channel_id=1, source_target_pairs={{0,4},{1,5},{2,6},{3,7},{4,0},{5,1},{6,2},{7,3},{8,12},{9,13},{10,... | collective-permute-start | bytes 3145736 | tf_op jit(solution)/shard_map/ppermute | solution.py:244
  123.3 62.3 %collective-permute-start.28 = (bf16[512,1024]{1,0:T(8,128)(2,1)}, bf16[512,1024]{1,0:T(8,128)(2,1)}, u32[]{:S(2)}, u32[]{:S(2)}) collective-permute-start(bf16[512,1024]{1,0:T(8,128)(2,1)} %param.33), channel_id=1, source_target_pairs={{0,2},{1,3},{2,0},{3,1},{4,6},{5,7},{6,4},{7,5},{8,10},{9,11},{10,... | collective-permute-start | bytes 3145736 | tf_op jit(solution)/shard_map/ppermute | solution.py:244
  126.5 82.6 %collective-permute-start.23 = (bf16[128,4096]{1,0:T(8,128)(2,1)}, bf16[128,4096]{1,0:T(8,128)(2,1)}, u32[]{:S(2)}, u32[]{:S(2)}) collective-permute-start(bf16[128,4096]{1,0:T(8,128)(2,1)} %collective-permute-done.19), channel_id=1, source_target_pairs={{0,4},{1,5},{2,6},{3,7},{4,0},{5,1},{6,2},{7,3},{8,12},{9,13},{10,... | collective-permute-start | bytes 3145736 | tf_op jit(solution)/shard_map/ppermute | solution.py:244
  133.1 67.2 %collective-permute-start.27 = (bf16[512,1024]{1,0:T(8,128)(2,1)}, bf16[512,1024]{1,0:T(8,128)(2,1)}, u32[]{:S(2)}, u32[]{:S(2)}) collective-permute-start(bf16[512,1024]{1,0:T(8,128)(2,1)} %collective-permute-done.26), channel_id=1, source_target_pairs={{0,1},{1,0},{2,3},{3,2},{4,5},{5,4},{6,7},{7,6},{8,9},{9,8},{10,11... | collective-permute-start | bytes 3145736 | tf_op jit(solution)/shard_map/ppermute | solution.py:244
  185.6 25.5 %collective-permute-start.30 = (bf16[512,1024]{1,0:T(8,128)(2,1)}, bf16[512,1024]{1,0:T(8,128)(2,1)S(1)}, u32[]{:S(2)}, u32[]{:S(2)}) collective-permute-start(bf16[512,1024]{1,0:T(8,128)(2,1)} %collective-permute-done.26), channel_id=1, source_target_pairs={{0,2},{1,3},{2,0},{3,1},{4,6},{5,7},{6,4},{7,5},{8,10},{9,11},{10,... | collective-permute-start | bytes 3145736 | tf_op jit(solution)/shard_map/ppermute | solution.py:244
  206.9 39.7 %collective-permute-start.33 = (bf16[256,1024]{1,0:T(8,128)(2,1)S(1)}, bf16[256,1024]{1,0:T(8,128)(2,1)S(1)}, u32[]{:S(2)}, u32[]{:S(2)}) collective-permute-start(bf16[256,1024]{1,0:T(8,128)(2,1)S(1)} %copy-done.44), channel_id=1, source_target_pairs={{0,16},{8,24},{16,0},{24,8},{1,17},{9,25},{17,1},{25,9},{2,18},{10... | collective-permute-start | bytes 1572872 | tf_op jit(solution)/shard_map/ppermute | solution.py:244
  211.1 26.2 %collective-permute-start.31 = (bf16[512,1024]{1,0:T(8,128)(2,1)S(1)}, bf16[512,1024]{1,0:T(8,128)(2,1)S(1)}, u32[]{:S(2)}, u32[]{:S(2)}) collective-permute-start(bf16[512,1024]{1,0:T(8,128)(2,1)S(1)} %collective-permute-done.30), channel_id=1, source_target_pairs={{0,1},{1,0},{2,3},{3,2},{4,5},{5,4},{6,7},{7,6},{8,9},{9,8},{10,11... | collective-permute-start | bytes 3145736 | tf_op jit(solution)/shard_map/ppermute | solution.py:244
  251.2 142.5 %collective-permute-start.32 = (bf16[256,1024]{1,0:T(8,128)(2,1)}, bf16[256,1024]{1,0:T(8,128)(2,1)}, u32[]{:S(2)}, u32[]{:S(2)}) collective-permute-start(bf16[256,1024]{1,0:T(8,128)(2,1)} %get-tuple-element.96), channel_id=1, source_target_pairs={{0,16},{8,24},{16,0},{24,8},{1,17},{9,25},{17,1},{25,9},{2,18},{10... | collective-permute-start | bytes 1572872 | tf_op jit(solution)/shard_map/ppermute | solution.py:244
  289.1 34.5 %collective-permute-start.34 = (bf16[512,512]{1,0:T(8,128)(2,1)}, bf16[512,512]{1,0:T(8,128)(2,1)}, u32[]{:S(2)}, u32[]{:S(2)}) collective-permute-start(bf16[512,512]{1,0:T(8,128)(2,1)} %bitcast.222), channel_id=1, source_target_pairs={{0,8},{8,0},{16,24},{24,16},{1,9},{9,1},{17,25},{25,17},{2,10},{10... | collective-permute-start | bytes 1572872 | tf_op jit(solution)/shard_map/ppermute | solution.py:244
  294.0 79.2 %collective-permute-start.42 = (bf16[4,128,1024]{2,1,0:T(8,128)(2,1)}, bf16[4,128,1024]{2,1,0:T(8,128)(2,1)}, u32[]{:S(2)}, u32[]{:S(2)}) collective-permute-start(bf16[4,128,1024]{2,1,0:T(8,128)(2,1)} %bitcast.53), channel_id=1, source_target_pairs={{0,1},{1,0},{2,3},{3,2},{4,5},{5,4},{6,7},{7,6},{8,9},{9,8},{10,11... | collective-permute-start | bytes 3145736 | tf_op jit(solution)/shard_map/ppermute | solution.py:244
  321.5 121.0 %collective-permute-start.60 = (bf16[4,128,4096]{2,1,0:T(8,128)(2,1)}, bf16[4,128,4096]{2,1,0:T(8,128)(2,1)}, u32[]{:S(2)}, u32[]{:S(2)}) collective-permute-start(bf16[4,128,4096]{2,1,0:T(8,128)(2,1)} %bitcast.80), channel_id=1, source_target_pairs={{0,1},{1,0},{2,3},{3,2},{4,5},{5,4},{6,7},{7,6},{8,9},{9,8},{10,11... | collective-permute-start | bytes 12582920 | tf_op jit(solution)/shard_map/ppermute | solution.py:244
  364.3 39.2 %collective-permute-start.35 = (bf16[512,1024]{1,0:T(8,128)(2,1)}, bf16[512,1024]{1,0:T(8,128)(2,1)}, u32[]{:S(2)}, u32[]{:S(2)}) collective-permute-start(bf16[512,1024]{1,0:T(8,128)(2,1)} %bitcast.34), channel_id=1, source_target_pairs={{0,8},{8,0},{16,24},{24,16},{1,9},{9,1},{17,25},{25,17},{2,10},{10... | collective-permute-start | bytes 3145736 | tf_op jit(solution)/shard_map/ppermute | solution.py:244
  389.2 19.9 %collective-permute-start.37 = (bf16[4,128,1536]{1,2,0:T(8,128)(2,1)}, bf16[4,128,1536]{1,2,0:T(8,128)(2,1)}, u32[]{:S(2)}, u32[]{:S(2)}) collective-permute-start(bf16[4,128,1536]{1,2,0:T(8,128)(2,1)} %copy.182), channel_id=1, source_target_pairs={{0,1},{1,0},{2,3},{3,2},{4,5},{5,4},{6,7},{7,6},{8,9},{9,8},{10,11... | collective-permute-start | bytes 4718600 | tf_op jit(solution)/shard_map/ppermute | solution.py:244
  401.3 68.7 %collective-permute-start.68 = (bf16[4,512,1024]{2,1,0:T(8,128)(2,1)}, bf16[4,512,1024]{2,1,0:T(8,128)(2,1)}, u32[]{:S(2)}, u32[]{:S(2)}) collective-permute-start(bf16[4,512,1024]{2,1,0:T(8,128)(2,1)} %bitcast.296), channel_id=1, source_target_pairs={{0,1},{1,0},{2,3},{3,2},{4,5},{5,4},{6,7},{7,6},{8,9},{9,8},{10,11... | collective-permute-start | bytes 12582920 | tf_op jit(solution)/shard_map/ppermute | solution.py:244
  406.0 28.5 %collective-permute-start.36 = (bf16[256,1024]{1,0:T(8,128)(2,1)S(1)}, bf16[256,1024]{1,0:T(8,128)(2,1)S(1)}, u32[]{:S(2)}, u32[]{:S(2)}) collective-permute-start(bf16[256,1024]{1,0:T(8,128)(2,1)S(1)} %fusion.49), channel_id=1, source_target_pairs={{0,16},{8,24},{16,0},{24,8},{1,17},{9,25},{17,1},{25,9},{2,18},{10... | collective-permute-start | bytes 1572872 | tf_op jit(solution)/shard_map/ppermute | solution.py:244
  408.0 26.4 %collective-permute-start.46 = (bf16[32,1024]{1,0:T(8,128)(2,1)S(1)}, bf16[32,1024]{1,0:T(8,128)(2,1)S(1)}, u32[]{:S(2)}, u32[]{:S(2)}) collective-permute-start(bf16[32,1024]{1,0:T(8,128)(2,1)S(1)} %fusion.93), channel_id=1, source_target_pairs={{0,16},{8,24},{16,0},{24,8},{1,17},{9,25},{17,1},{25,9},{2,18},{10... | collective-permute-start | bytes 196616 | tf_op jit(solution)/shard_map/ppermute | solution.py:244
  410.5 29.3 %collective-permute-start.38 = (bf16[2,128,1536]{1,2,0:T(8,128)(2,1)S(1)}, bf16[2,128,1536]{1,2,0:T(8,128)(2,1)S(1)}, u32[]{:S(2)}, u32[]{:S(2)}) collective-permute-start(bf16[2,128,1536]{1,2,0:T(8,128)(2,1)S(1)} %add_convert_fusion.3), channel_id=1, source_target_pairs={{0,2},{1,3},{2,0},{3,1},{4,6},{5,7},{6,4},{7,5},{8,10},{9,11},{10,... | collective-permute-start | bytes 2359304 | tf_op jit(solution)/shard_map/ppermute | solution.py:244
  434.5 21.2 %collective-permute-start.48 = (bf16[32,1024]{1,0:T(8,128)(2,1)S(1)}, bf16[32,1024]{1,0:T(8,128)(2,1)S(1)}, u32[]{:S(2)}, u32[]{:S(2)}) collective-permute-start(bf16[32,1024]{1,0:T(8,128)(2,1)S(1)} %get-tuple-element.44), channel_id=1, source_target_pairs={{0,8},{8,0},{16,24},{24,16},{1,9},{9,1},{17,25},{25,17},{2,10},{10... | collective-permute-start | bytes 196616 | tf_op jit(solution)/shard_map/ppermute | solution.py:244
  439.7 16.1 %collective-permute-start.49 = (bf16[32,1024]{1,0:T(8,128)(2,1)S(1)}, bf16[32,1024]{1,0:T(8,128)(2,1)S(1)}, u32[]{:S(2)}, u32[]{:S(2)}) collective-permute-start(bf16[32,1024]{1,0:T(8,128)(2,1)S(1)} %collective-permute-done.47), channel_id=1, source_target_pairs={{0,8},{8,0},{16,24},{24,16},{1,9},{9,1},{17,25},{25,17},{2,10},{10... | collective-permute-start | bytes 196616 | tf_op jit(solution)/shard_map/ppermute | solution.py:244
  446.1 50.0 %collective-permute-start.61 = (bf16[2,128,4096]{2,1,0:T(8,128)(2,1)}, bf16[2,128,4096]{2,1,0:T(8,128)(2,1)}, u32[]{:S(2)}, u32[]{:S(2)}) collective-permute-start(bf16[2,128,4096]{2,1,0:T(8,128)(2,1)} %fusion.3), channel_id=1, source_target_pairs={{0,4},{1,5},{2,6},{3,7},{4,0},{5,1},{6,2},{7,3},{8,12},{9,13},{10,... | collective-permute-start | bytes 6291464 | tf_op jit(solution)/shard_map/ppermute | solution.py:244
  469.5 33.6 %collective-permute-start.41 = (bf16[128,1536]{0,1:T(8,128)(2,1)S(1)}, bf16[128,1536]{0,1:T(8,128)(2,1)S(1)}, u32[]{:S(2)}, u32[]{:S(2)}) collective-permute-start(bf16[128,1536]{0,1:T(8,128)(2,1)S(1)} %add_convert_fusion.4), channel_id=1, source_target_pairs={{0,8},{8,0},{16,24},{24,16},{1,9},{9,1},{17,25},{25,17},{2,10},{10... | collective-permute-start | bytes 1179656 | tf_op jit(solution)/shard_map/ppermute | solution.py:244
  474.1 48.9 %collective-permute-start.69 = (bf16[2,512,1024]{2,1,0:T(8,128)(2,1)}, bf16[2,512,1024]{2,1,0:T(8,128)(2,1)}, u32[]{:S(2)}, u32[]{:S(2)}) collective-permute-start(bf16[2,512,1024]{2,1,0:T(8,128)(2,1)} %fusion.1), channel_id=1, source_target_pairs={{0,2},{1,3},{2,0},{3,1},{4,6},{5,7},{6,4},{7,5},{8,10},{9,11},{10,... | collective-permute-start | bytes 6291464 | tf_op jit(solution)/shard_map/ppermute | solution.py:244
  502.5 40.8 %collective-permute-start.62 = (bf16[128,4096]{1,0:T(8,128)(2,1)}, bf16[128,4096]{1,0:T(8,128)(2,1)}, u32[]{:S(2)}, u32[]{:S(2)}) collective-permute-start(bf16[128,4096]{1,0:T(8,128)(2,1)} %fusion.30), channel_id=1, source_target_pairs={{0,2},{1,3},{2,0},{3,1},{4,6},{5,7},{6,4},{7,5},{8,10},{9,11},{10,... | collective-permute-start | bytes 3145736 | tf_op jit(solution)/shard_map/ppermute | solution.py:244
  528.1 22.4 %collective-permute-start.70 = (bf16[512,1024]{1,0:T(8,128)(2,1)}, bf16[512,1024]{1,0:T(8,128)(2,1)S(1)}, u32[]{:S(2)}, u32[]{:S(2)}) collective-permute-start(bf16[512,1024]{1,0:T(8,128)(2,1)} %fusion.31), channel_id=1, source_target_pairs={{0,4},{1,5},{2,6},{3,7},{4,0},{5,1},{6,2},{7,3},{8,12},{9,13},{10,... | collective-permute-start | bytes 3145736 | tf_op jit(solution)/shard_map/ppermute | solution.py:244
  545.6 18.0 %collective-permute-start.63 = (bf16[64,4096]{1,0:T(8,128)(2,1)}, bf16[64,4096]{1,0:T(8,128)(2,1)}, u32[]{:S(2)}, u32[]{:S(2)}) collective-permute-start(bf16[64,4096]{1,0:T(8,128)(2,1)} %fusion.50), channel_id=1, source_target_pairs={{0,8},{8,0},{16,24},{24,16},{1,9},{9,1},{17,25},{25,17},{2,10},{10... | collective-permute-start | bytes 1572872 | tf_op jit(solution)/shard_map/ppermute | solution.py:244
  552.5 21.4 %collective-permute-start.71 = (bf16[256,1024]{1,0:T(8,128)(2,1)S(1)}, bf16[256,1024]{1,0:T(8,128)(2,1)S(1)}, u32[]{:S(2)}, u32[]{:S(2)}) collective-permute-start(bf16[256,1024]{1,0:T(8,128)(2,1)S(1)} %fusion.51), channel_id=1, source_target_pairs={{0,8},{8,0},{16,24},{24,16},{1,9},{9,1},{17,25},{25,17},{2,10},{10... | collective-permute-start | bytes 1572872 | tf_op jit(solution)/shard_map/ppermute | solution.py:244
  564.8 21.2 %collective-permute-start.64 = (bf16[32,4096]{1,0:T(8,128)(2,1)S(1)}, bf16[32,4096]{1,0:T(8,128)(2,1)S(1)}, u32[]{:S(2)}, u32[]{:S(2)}) collective-permute-start(bf16[32,4096]{1,0:T(8,128)(2,1)S(1)} %fusion.85), channel_id=1, source_target_pairs={{0,16},{8,24},{16,0},{24,8},{1,17},{9,25},{17,1},{25,9},{2,18},{10... | collective-permute-start | bytes 786440 | tf_op jit(solution)/shard_map/ppermute | solution.py:244
  574.1 22.3 %collective-permute-start.72 = (bf16[128,1024]{1,0:T(8,128)(2,1)S(1)}, bf16[128,1024]{1,0:T(8,128)(2,1)S(1)}, u32[]{:S(2)}, u32[]{:S(2)}) collective-permute-start(bf16[128,1024]{1,0:T(8,128)(2,1)S(1)} %fusion.86), channel_id=1, source_target_pairs={{0,16},{8,24},{16,0},{24,8},{1,17},{9,25},{17,1},{25,9},{2,18},{10... | collective-permute-start | bytes 786440 | tf_op jit(solution)/shard_map/ppermute | solution.py:244
  586.3 19.5 %collective-permute-start.65 = (bf16[32,4096]{1,0:T(8,128)(2,1)S(1)}, bf16[32,4096]{1,0:T(8,128)(2,1)S(1)}, u32[]{:S(2)}, u32[]{:S(2)}) collective-permute-start(bf16[32,4096]{1,0:T(8,128)(2,1)S(1)} %get-tuple-element.37), channel_id=1, source_target_pairs={{0,16},{8,24},{16,0},{24,8},{1,17},{9,25},{17,1},{25,9},{2,18},{10... | collective-permute-start | bytes 786440 | tf_op jit(solution)/shard_map/ppermute | solution.py:244
  587.3 23.0 %collective-permute-start.66 = (bf16[32,4096]{1,0:T(8,128)(2,1)S(1)}, bf16[32,4096]{1,0:T(8,128)(2,1)S(1)}, u32[]{:S(2)}, u32[]{:S(2)}) collective-permute-start(bf16[32,4096]{1,0:T(8,128)(2,1)S(1)} %get-tuple-element.37), channel_id=1, source_target_pairs={{0,8},{8,0},{16,24},{24,16},{1,9},{9,1},{17,25},{25,17},{2,10},{10... | collective-permute-start | bytes 786440 | tf_op jit(solution)/shard_map/ppermute | solution.py:244
  596.8 16.5 %collective-permute-start.74 = (bf16[128,1024]{1,0:T(8,128)(2,1)S(1)}, bf16[128,1024]{1,0:T(8,128)(2,1)S(1)}, u32[]{:S(2)}, u32[]{:S(2)}) collective-permute-start(bf16[128,1024]{1,0:T(8,128)(2,1)S(1)} %get-tuple-element.35), channel_id=1, source_target_pairs={{0,8},{8,0},{16,24},{24,16},{1,9},{9,1},{17,25},{25,17},{2,10},{10... | collective-permute-start | bytes 786440 | tf_op jit(solution)/shard_map/ppermute | solution.py:244
  (93 other events, 853.0 us)

commit v2 on v1

v2 whole, which is shorter than its diff:
```python
from functools import partial

import jax
import jax.numpy as jnp
from jax import lax
from jax.experimental import pallas as pl
from jax.experimental.pallas import tpu as pltpu
from jax.sharding import PartitionSpec as P

HEAD_DIM = 64
PAIR = 2 * HEAD_DIM
BLOCK = 256
F32 = jnp.float32
BF16 = jnp.bfloat16

PHI_POLY = (
    0.11962928975633808,
    0.12075411058236112,
    0.09991242675653945,
    0.12856547821204567,
    -0.053691543682108024,
    0.20636272322745108,
    -0.15720876784307727,
    0.03567620985200702,
)


def normal_cdf_pdf(z):
    u = jnp.abs(z)
    bell = jnp.exp(-0.5 * u * u)
    t = 1.0 / (1.0 + 0.3 * u)
    poly = jnp.full_like(t, PHI_POLY[-1])
    for coef in PHI_POLY[-2::-1]:
        poly = poly * t + coef
    tail = bell * (t * poly)
    return jnp.where(z < 0, tail, 1.0 - tail), bell * 0.3989422804014327


def layer_norm(rows, gain, shift):
    centred = rows - jnp.mean(rows, axis=-1, keepdims=True)
    factor = lax.rsqrt(jnp.mean(centred * centred, axis=-1, keepdims=True) + 1e-05)
    normed = centred * factor
    return (normed * gain + shift, normed, factor)


def norm_back(upstream, normed, factor, gain):
    scaled = upstream * gain
    return factor * (
        scaled
        - jnp.mean(scaled, axis=-1, keepdims=True)
        - normed * jnp.mean(scaled * normed, axis=-1, keepdims=True)
    )


def matmul(left, right):
    return jnp.dot(left, right, preferred_element_type=F32)


def contract_rows(left, right):
    return lax.dot_general(left, right, (((0,), (0,)), ((), ())), preferred_element_type=F32)


def contract_cols(left, right):
    return lax.dot_general(left, right, (((1,), (1,)), ((), ())), preferred_element_type=F32)


def column_sum(rows):
    return jnp.sum(rows.astype(F32), axis=0)


def half_rows(block, head):
    zero = jnp.zeros((HEAD_DIM, block.shape[1]), block.dtype)
    part = block[head * HEAD_DIM : (head + 1) * HEAD_DIM]
    return jnp.concatenate([part, zero] if head == 0 else [zero, part], axis=0)


def columns(pair, kind):
    return slice((3 * pair + kind) * PAIR, (3 * pair + kind + 1) * PAIR)


def head_rows(n):
    return slice(n * HEAD_DIM, (n + 1) * HEAD_DIM)


def forward_kernel(bounds, qkv_ref, row_ref, col_ref, mixed_ref, logsum_ref, vt_ref):
    length = qkv_ref.shape[0]
    pairs = logsum_ref.shape[0]
    heads = [(p, head) for p in range(pairs) for head in range(2)]
    q_t = [qkv_ref[:, columns(p, 0)].T for p in range(pairs)]
    for p in range(pairs):
        vt_ref[p * PAIR : (p + 1) * PAIR, :] = qkv_ref[:, columns(p, 2)].T
    for i in range(length // BLOCK):
        at = slice(i * BLOCK, (i + 1) * BLOCK)
        row = row_ref[:, at]
        halves = [half_rows(q_t[p][:, at], head) for p, head in heads]

        def step(j, carry):
            span = pl.ds(pl.multiple_of(j * BLOCK, BLOCK), BLOCK)
            same = col_ref[span, :] == row
            products = [matmul(qkv_ref[span, columns(p, 1)], halves[2 * p + head]) for p, head in heads]
            new = []
            for n, (peak, total, mix) in enumerate(carry):
                scores = jnp.where(same, products[n], -1e30)
                top = jnp.maximum(peak, jnp.max(scores, axis=0, keepdims=True))
                weights = jnp.exp(scores - top)
                decay = jnp.exp(peak - top)
                total = total * decay + jnp.sum(weights, axis=0, keepdims=True)
                mix = mix * decay + matmul(vt_ref[head_rows(n), span], weights.astype(BF16))
                new.append((top, total, mix))
            return tuple(new)

        first = (
            jnp.full((1, BLOCK), -1e30, F32),
            jnp.zeros((1, BLOCK), F32),
            jnp.zeros((HEAD_DIM, BLOCK), F32),
        )
        done = lax.fori_loop(bounds[i, 0], bounds[i, 1], step, (first,) * len(heads))
        for p in range(pairs):
            mixes = [mix / total for _, total, mix in done[2 * p : 2 * p + 2]]
            mixed_ref[at, p * PAIR : (p + 1) * PAIR] = jnp.concatenate(mixes, axis=0).T.astype(BF16)
        for n, (p, head) in enumerate(heads):
            logsum_ref[p, head : head + 1, at] = done[n][0] + jnp.log(done[n][1])


def backward_kernel(
    bounds, qkv_ref, row_ref, col_ref, mixed_ref, logsum_ref, grad_ref, out_ref, sums_ref, kt_ref, dk_ref, dv_ref
):
    length = qkv_ref.shape[0]
    pairs = logsum_ref.shape[0]
    heads = [(p, head) for p in range(pairs) for head in range(2)]
    dk_ref[...] = jnp.zeros_like(dk_ref)
    dv_ref[...] = jnp.zeros_like(dv_ref)
    q_t, g_t, delta = [], [], []
    for p in range(pairs):
        lanes = slice(p * PAIR, (p + 1) * PAIR)
        q_t.append(qkv_ref[:, columns(p, 0)].T)
        g_t.append(grad_ref[:, lanes].T)
        kt_ref[lanes, :] = qkv_ref[:, columns(p, 1)].T
        product_t = (grad_ref[:, lanes].astype(F32) * mixed_ref[:, lanes].astype(F32)).T
        for head in range(2):
            delta.append(jnp.sum(product_t[head_rows(head)], axis=0, keepdims=True))
    lane = lax.broadcasted_iota(jnp.int32, (BLOCK, PAIR), 1)
    zero = jnp.zeros((BLOCK, PAIR), BF16)

    def split(x):
        return jnp.concatenate(
            [jnp.where(lane < HEAD_DIM, x, zero), jnp.where(lane >= HEAD_DIM, x, zero)], axis=0
        )

    for i in range(length // BLOCK):
        at = slice(i * BLOCK, (i + 1) * BLOCK)
        row = row_ref[:, at]
        q_halves = [half_rows(q_t[p][:, at], head) for p, head in heads]
        g_halves = [half_rows(g_t[p][:, at], head) for p, head in heads]
        q_split = [split(qkv_ref[at, columns(p, 0)]) for p in range(pairs)]
        g_split = [split(grad_ref[at, p * PAIR : (p + 1) * PAIR]) for p in range(pairs)]
        logsum = [logsum_ref[p, head : head + 1, at] for p, head in heads]

        def step(j, carry):
            span = pl.ds(pl.multiple_of(j * BLOCK, BLOCK), BLOCK)
            same = col_ref[span, :] == row
            scores = [matmul(qkv_ref[span, columns(p, 1)], q_halves[2 * p + head]) for p, head in heads]
            grad_probs = [matmul(qkv_ref[span, columns(p, 2)], g_halves[2 * p + head]) for p, head in heads]
            new = []
            for p in range(pairs):
                probs_low, grad_low = [], []
                for n in (2 * p, 2 * p + 1):
                    probs = jnp.exp(jnp.where(same, scores[n], -1e30) - logsum[n])
                    grad_low.append((probs * (grad_probs[n] - delta[n][:, at])).astype(BF16))
                    probs_low.append(probs.astype(BF16))
                    new.append(carry[n] + matmul(kt_ref[head_rows(n), span], grad_low[-1]))
                lanes = slice(p * PAIR, (p + 1) * PAIR)
                dv_ref[span, lanes] += matmul(jnp.concatenate(probs_low, axis=1), g_split[p])
                dk_ref[span, lanes] += matmul(jnp.concatenate(grad_low, axis=1), q_split[p])
            return tuple(new)

        empty = jnp.zeros((HEAD_DIM, BLOCK), F32)
        done = lax.fori_loop(bounds[i, 0], bounds[i, 1], step, (empty,) * len(heads))
        for p in range(pairs):
            grad_q = jnp.concatenate(done[2 * p : 2 * p + 2], axis=0).T
            out_ref[at, columns(p, 0)] = (grad_q * 0.125).astype(BF16)
    for p in range(pairs):
        lanes = slice(p * PAIR, (p + 1) * PAIR)
        out_ref[:, columns(p, 1)] = dk_ref[:, lanes].astype(BF16)
        out_ref[:, columns(p, 2)] = dv_ref[:, lanes].astype(BF16)
    sums_ref[...] = jnp.sum(out_ref[...].astype(F32), axis=0, keepdims=True)


def block_bounds(starts):
    blocks = starts.reshape(-1, BLOCK)
    least, most = blocks[:, 0], blocks[:, -1]
    low = jnp.sum(most[None, :] < least[:, None], axis=1)
    high = jnp.sum(least[None, :] <= most[:, None], axis=1)
    return jnp.stack([low, high], axis=1).astype(jnp.int32)


def attention_forward(bounds, qkv, starts, index, pairs):
    length = qkv.shape[0]
    operands = (bounds, qkv, starts[None, :], starts[:, None])
    shapes = [shape_of((length, pairs * PAIR), BF16), shape_of((pairs, 2, length), F32)]
    return call(
        forward_kernel,
        "attend",
        (1,),
        [
            pl.BlockSpec((length, pairs * 3 * PAIR), lambda g, b: (0, index)),
            whole((1, length)),
            whole((length, 1)),
        ],
        [whole(x.shape) for x in shapes],
        shapes,
        pairs * 2 * length * length * HEAD_DIM * 4,
        operands,
        scratch=[pltpu.VMEM((pairs * PAIR, length), BF16)],
        prefetch=1,
        vmem=16,
    )


def attention_backward(bounds, qkv, starts, mixed, logsum, grad, index, pairs):
    length = qkv.shape[0]
    operands = (bounds, qkv, starts[None, :], starts[:, None], mixed, logsum, grad)
    shapes = [shape_of((length, pairs * 3 * PAIR), BF16), shape_of((1, pairs * 3 * PAIR), F32)]
    return call(
        backward_kernel,
        "attend_back",
        (1,),
        [
            pl.BlockSpec((length, pairs * 3 * PAIR), lambda g, b: (0, index)),
            whole((1, length)),
            whole((length, 1)),
            whole(mixed.shape),
            whole(logsum.shape),
            pl.BlockSpec((length, pairs * PAIR), lambda g, b: (0, index)),
        ],
        [whole(x.shape) for x in shapes],
        shapes,
        pairs * 2 * length * length * HEAD_DIM * 10,
        operands,
        scratch=[
            pltpu.VMEM((pairs * PAIR, length), BF16),
            pltpu.VMEM((length, pairs * PAIR), F32),
            pltpu.VMEM((length, pairs * PAIR), F32),
        ],
        prefetch=1,
        vmem=24,
    )


MEGA = 1024 * 1024


def whole(shape):
    return pl.BlockSpec(shape, lambda *_: (0,) * len(shape), pipeline_mode=pl.Buffered(1))


def call(kernel, name, grid, in_specs, out_specs, out_shape, flops, operands, scratch=(), prefetch=0, vmem=32):
    moved = sum(x.size * x.dtype.itemsize for x in operands) + sum(
        x.size * x.dtype.itemsize for x in out_shape
    )
    return pl.pallas_call(
        kernel,
        grid_spec=pltpu.PrefetchScalarGridSpec(
            num_scalar_prefetch=prefetch,
            grid=grid,
            in_specs=in_specs,
            out_specs=out_specs,
            scratch_shapes=list(scratch),
        ),
        out_shape=out_shape,
        compiler_params=pltpu.CompilerParams(vmem_limit_bytes=vmem * MEGA),
        cost_estimate=pl.CostEstimate(flops=flops, bytes_accessed=moved, transcendentals=0),
        name=name,
    )(*operands)


def shape_of(shape, dtype):
    return jax.ShapeDtypeStruct(shape, dtype)


def output_kernel(where, *refs):
    (mine_refs, their_refs), (weight_ref, bias_ref, hidden_ref, gain_ref, shift_ref) = (
        (refs[:4], refs[4:6]),
        refs[6:11],
    )
    out_ref, low_ref, normed_ref, factor_ref, mixed_ref = refs[11:]
    h = where[0]
    half = weight_ref.shape[0] // 2
    part = half // 2
    rows = mine_refs[0].shape[0]
    for i in range(2):
        at = slice(i * rows, (i + 1) * rows)
        total = hidden_ref[at, :] + bias_ref[...]
        for cut in range(2):
            mine = pl.ds(pl.multiple_of(h * half + cut * part, 128), part)
            other = pl.ds(pl.multiple_of((1 - h) * half + cut * part, 128), part)
            left, right = mine_refs[2 * cut + i][...], their_refs[cut][at, :]
            mixed_ref[at, mine] = left
            mixed_ref[at, other] = right
            total = total + matmul(left, weight_ref[mine, :]) + matmul(right, weight_ref[other, :])
        out, normed, factor = layer_norm(total, gain_ref[...], shift_ref[...])
        out_ref[at, :] = out
        low_ref[at, :] = out.astype(BF16)
        normed_ref[at, :] = normed
        factor_ref[at, :] = factor


def project_output(h, mine, their, weight, bias, hidden, gain, shift):
    rows, width = hidden.shape
    tok = rows // 2
    part = mine[0].shape[1]
    where = jnp.stack([h, h + 2]).astype(jnp.int32)
    in_specs = [
        pl.BlockSpec((tok, part), lambda g, w: (w[0], 0)),
        pl.BlockSpec((tok, part), lambda g, w: (w[1], 0)),
    ] * 2
    in_specs += [whole((rows, part))] * 2
    in_specs += [whole(weight.shape), whole((1, width)), whole((rows, width)), whole((1, width)), whole((1, width))]
    shapes = [
        shape_of((rows, width), F32),
        shape_of((rows, width), BF16),
        shape_of((rows, width), F32),
        shape_of((rows, 1), F32),
        shape_of((rows, width), BF16),
    ]
    operands = (where, mine[0], mine[0], mine[1], mine[1], their[0], their[1], weight, bias, hidden, gain, shift)
    return call(
        output_kernel,
        "project_output",
        (1,),
        in_specs,
        [whole(x.shape) for x in shapes],
        shapes,
        2 * rows * width * width,
        operands,
        prefetch=1,
    )


def inner_kernel(order, first_ref, *refs):
    pieces, (bias_ref, active_ref, slope_ref, full_ref) = refs[:-4], refs[-4:]
    block = first_ref.shape[1] // 8
    done = 0
    for piece in pieces:
        rows = piece.shape[0]
        at = order[done // block] * block + done % block
        full_ref[pl.ds(pl.multiple_of(at, rows), rows), :] = piece[...]
        done += rows
    rows = first_ref.shape[0]
    step = 256
    for i in range(rows // step):
        at = slice(i * step, (i + 1) * step)
        inner = matmul(first_ref[at, :], full_ref[...]) + bias_ref[...]
        cdf, pdf = normal_cdf_pdf(inner)
        active_ref[0, at, :] = (inner * cdf).astype(BF16)
        slope_ref[0, at, :] = (cdf + inner * pdf).astype(BF16)


def feed_inner(order, first_low, pieces, bias):
    rows, width = first_low.shape
    ff = pieces[0].shape[1]
    tile = ff // 8
    shapes = [
        shape_of((8, rows, tile), BF16),
        shape_of((8, rows, tile), BF16),
        shape_of((width, ff), BF16),
    ]
    return call(
        inner_kernel,
        "feed_inner",
        (8,),
        [whole((rows, width))]
        + [pl.BlockSpec((x.shape[0], tile), lambda t, o: (0, t)) for x in pieces]
        + [pl.BlockSpec((1, tile), lambda t, o: (0, t))],
        [
            pl.BlockSpec((1, rows, tile), lambda t, o: (t, 0, 0)),
            pl.BlockSpec((1, rows, tile), lambda t, o: (t, 0, 0)),
            pl.BlockSpec((width, tile), lambda t, o: (0, t)),
        ],
        shapes,
        2 * rows * width * ff,
        (order, first_low, *pieces, bias),
        prefetch=1,
    )


def outer_kernel(order, active_ref, *refs):
    pieces, refs = refs[:-11], refs[-11:]
    bias_ref, first_ref, up_ref, gain_ref, shift_ref = refs[:5]
    full_ref, out_ref, grad_ref, low_ref, sums_ref, acc_ref = refs[5:]
    t = pl.program_id(0)
    block, tile = full_ref.shape[1:]
    done = 0
    for piece in pieces:
        rows = piece.shape[0]
        full_ref[order[done // block], done % block : done % block + rows] = piece[...]
        done += rows
    total = matmul(active_ref[0], full_ref[0])
    for k in range(1, 8):
        total = total + matmul(active_ref[k], full_ref[k])
    acc_ref[:, pl.ds(pl.multiple_of(t * tile, tile), tile)] = total

    @pl.when(t == pl.num_programs(0) - 1)
    def _():
        rows, width = acc_ref.shape
        step = 128
        gain, shift, bias = gain_ref[...], shift_ref[...], bias_ref[...]
        sums = [jnp.zeros((1, width), F32)] * 3
        for i in range(rows // step):
            at = slice(i * step, (i + 1) * step)
            out, normed, factor = layer_norm(first_ref[at, :] + acc_ref[at, :] + bias, gain, shift)
            out_ref[at, :] = out.astype(BF16)
            up = up_ref[at, :].astype(F32)
            grad = norm_back(up, normed, factor, gain)
            low = grad.astype(BF16)
            grad_ref[at, :] = grad
            low_ref[at, :] = low
            for j, item in enumerate((up * normed, up, low.astype(F32))):
                sums[j] = sums[j] + jnp.sum(item, axis=0, keepdims=True)
        sums_ref[...] = jnp.concatenate(sums + [jnp.zeros((5, width), F32)], axis=0)


def feed_outer(order, active, pieces, bias, first_out, upstream, gain, shift):
    rows, width = first_out.shape
    block = sum(x.shape[0] for x in pieces) // 8
    tile = width // 4
    shapes = [
        shape_of((8, block, width), BF16),
        shape_of((rows, width), BF16),
        shape_of((rows, width), F32),
        shape_of((rows, width), BF16),
        shape_of((8, width), F32),
    ]
    row = whole((1, width))
    return call(
        outer_kernel,
        "feed_outer",
        (4,),
        [whole(active.shape)]
        + [pl.BlockSpec((x.shape[0], tile), lambda t, o: (0, t)) for x in pieces]
        + [row, whole((rows, width)), whole((rows, width)), row, row],
        [pl.BlockSpec((8, block, tile), lambda t, o: (0, 0, t))] + [whole(x.shape) for x in shapes[1:]],
        shapes,
        2 * rows * width * block * 8,
        (order, active, *pieces, bias, first_out, upstream, gain, shift),
        scratch=[pltpu.VMEM((rows, width), F32)],
        prefetch=1,
    )


def gelu_back_kernel(grad_ref, weight_ref, slope_ref, out_ref, sums_ref):
    grad = contract_cols(grad_ref[...], weight_ref[0])
    low = (grad * slope_ref[0].astype(F32)).astype(BF16)
    out_ref[0] = low
    sums_ref[0] = jnp.sum(low.astype(F32), axis=0, keepdims=True)


def gelu_back(grad_outer, full_outer, slope):
    rows, width = grad_outer.shape
    _, block, _ = full_outer.shape
    tile = slope.shape[2]
    shapes = [shape_of(slope.shape, BF16), shape_of((8, 1, tile), F32)]
    return call(
        gelu_back_kernel,
        "gelu_back",
        (8,),
        [
            whole((rows, width)),
            pl.BlockSpec((1, block, width), lambda t: (t, 0, 0)),
            pl.BlockSpec((1, rows, tile), lambda t: (t, 0, 0)),
        ],
        [
            pl.BlockSpec((1, rows, tile), lambda t: (t, 0, 0)),
            pl.BlockSpec((1, 1, tile), lambda t: (t, 0, 0)),
        ],
        shapes,
        2 * rows * width * tile * 8,
        (grad_outer, full_outer, slope),
    )


def first_back_kernel(grad_ref, weight_ref, second_ref, normed_ref, factor_ref, gain_ref, output_ref, *refs):
    out_ref, low_ref, mixed_ref, sums_ref, acc_ref = refs
    t = pl.program_id(0)
    part = contract_cols(grad_ref[0], weight_ref[...])

    @pl.when(t == 0)
    def _():
        acc_ref[...] = second_ref[...] + part

    @pl.when(t > 0)
    def _():
        acc_ref[...] += part

    @pl.when(t == pl.num_programs(0) - 1)
    def _():
        rows, width = acc_ref.shape
        step = 128
        gain = gain_ref[...]
        sums = [jnp.zeros((1, width), F32)] * 3
        for i in range(rows // step):
            at = slice(i * step, (i + 1) * step)
            up, normed = acc_ref[at, :], normed_ref[at, :]
            grad = norm_back(up, normed, factor_ref[at, :], gain)
            low = grad.astype(BF16)
            out_ref[at, :] = grad
            low_ref[at, :] = low
            for j, item in enumerate((up * normed, up, low.astype(F32))):
                sums[j] = sums[j] + jnp.sum(item, axis=0, keepdims=True)
        sums_ref[...] = jnp.concatenate(sums + [jnp.zeros((5, width), F32)], axis=0)
        mixed_ref[...] = contract_cols(low_ref[...], output_ref[...]).astype(BF16)


def first_back(grad_inner, full_inner, grad_second, normed, factor, gain, full_output):
    rows, width = grad_second.shape
    tile = grad_inner.shape[2]
    shapes = [
        shape_of((rows, width), F32),
        shape_of((rows, width), BF16),
        shape_of((rows, width), BF16),
        shape_of((8, width), F32),
    ]
    return call(
        first_back_kernel,
        "first_back",
        (8,),
        [
            pl.BlockSpec((1, rows, tile), lambda t: (t, 0, 0)),
            pl.BlockSpec((width, tile), lambda t: (0, t)),
            whole((rows, width)),
            whole((rows, width)),
            whole((rows, 1)),
            whole((1, width)),
            whole(full_output.shape),
        ],
        [whole(x.shape) for x in shapes],
        shapes,
        2 * rows * width * (tile * 8 + width),
        (grad_inner, full_inner, grad_second, normed, factor, gain, full_output),
        scratch=[pltpu.VMEM((rows, width), F32)],
    )


def block_grad_kernel(order, left_ref, right_ref, out_ref):
    out_ref[0] = contract_rows(left_ref[0], right_ref[...]).astype(BF16)


def block_grad(order, left, right):
    rows, width = right.shape
    block = left.shape[2]
    shapes = [shape_of((4, block, width), BF16)]
    return call(
        block_grad_kernel,
        "block_grad",
        (4,),
        [pl.BlockSpec((1, rows, block), lambda i, o: (o[i], 0, 0)), whole((rows, width))],
        [pl.BlockSpec((1, block, width), lambda i, o: (i, 0, 0))],
        shapes,
        2 * rows * width * block * 4,
        (order, left, right),
        prefetch=1,
    )[0]


def turn_strips(order, left_ref, turned_ref):
    block = turned_ref.shape[0] // 4
    for i in range(4):
        strip = left_ref[:, pl.ds(pl.multiple_of(order[i] * block, block), block)]
        turned_ref[i * block : (i + 1) * block, : strip.shape[0]] = strip.T


def tile_grad_kernel(order, left_ref, right_ref, out_ref, turned_ref):
    block = out_ref.shape[1]

    @pl.when(pl.program_id(0) == 0)
    def _():
        turn_strips(order, left_ref, turned_ref)

    out = matmul(turned_ref[...], right_ref[0]).astype(BF16)
    for i in range(4):
        out_ref[i] = out[i * block : (i + 1) * block]


def tile_grad(order, left, right):
    rows, width = left.shape
    block = width // 8
    tiles, _, tile = right.shape
    shapes = [shape_of((4, block, tiles * tile), BF16)]
    return call(
        tile_grad_kernel,
        "tile_grad",
        (tiles,),
        [whole((rows, width)), pl.BlockSpec((1, rows, tile), lambda t, o: (t, 0, 0))],
        [pl.BlockSpec((4, block, tile), lambda t, o: (0, 0, t))],
        shapes,
        2 * rows * block * 4 * tiles * tile,
        (order, left, right),
        scratch=[pltpu.VMEM((4 * block, rows), BF16)],
        prefetch=1,
        vmem=12,
    )[0]


def strip_grad_kernel(
    parts, order, left_ref, first_ref, second_ref, extra_ref, low_ref, third_ref, out_ref, turned_ref
):
    t = pl.program_id(0)
    last = parts[0] + parts[1]
    block = turned_ref.shape[0] // 4

    @pl.when(t == 0)
    def _():
        turn_strips(order, left_ref, turned_ref)

    @pl.when(t == last)
    def _():
        turn_strips(order, low_ref, turned_ref)

    def put(right, extra):
        out = matmul(turned_ref[:, : right.shape[0]], right).astype(BF16)
        for i in range(4):
            out_ref[i, :block] = out[i * block : (i + 1) * block]
            out_ref[i, block:] = extra_ref[order[i]] if extra else jnp.zeros_like(out_ref[i, block:])

    @pl.when(t < parts[0])
    def _():
        put(first_ref[...], True)

    @pl.when((t >= parts[0]) & (t < last))
    def _():
        put(second_ref[...], True)

    @pl.when(t >= last)
    def _():
        put(third_ref[...], False)


def strip_grad(order, left, first, second, extra, low, third):
    rows, width = left.shape
    block = width // 8
    tile = 512 if first.shape[1] % 512 == 0 else 256
    parts = [x.shape[1] // tile for x in (first, second, third)]
    total = sum(parts)
    tall = block + extra.shape[1]
    shapes = [shape_of((4, tall, total * tile), BF16)]
    return call(
        partial(strip_grad_kernel, parts),
        "strip_grad",
        (total,),
        [
            whole((rows, width)),
            pl.BlockSpec((rows, tile), lambda t, o: (0, jnp.minimum(t, parts[0] - 1))),
            pl.BlockSpec((rows, tile), lambda t, o: (0, jnp.clip(t - parts[0], 0, parts[1] - 1))),
            pl.BlockSpec(
                (8, extra.shape[1], tile), lambda t, o: (0, 0, jnp.minimum(t, parts[0] + parts[1] - 1))
            ),
            whole(low.shape),
            pl.BlockSpec((low.shape[0], tile), lambda t, o: (0, jnp.maximum(t - parts[0] - parts[1], 0))),
        ],
        [pl.BlockSpec((4, tall, tile), lambda t, o: (0, 0, t))],
        shapes,
        2 * rows * block * 4 * total * tile,
        (order, left, first, second, extra, low, third),
        scratch=[pltpu.VMEM((4 * block, rows), BF16)],
        prefetch=1,
        vmem=20,
    )[0]


def hidden_back_kernel(where, *refs):
    lefts, weight_ref, rest = refs[:2], refs[2], refs[3:]
    part = lefts[0].shape[1]
    total = contract_cols(lefts[0][...], weight_ref[:, :part]) + contract_cols(lefts[1][...], weight_ref[:, part:])
    if len(rest) == 2:
        total = total + rest[0][...]
    rest[-1][...] = total.astype(rest[-1].dtype)


def hidden_back(parity, grads, weight, base, tok):
    width = weight.shape[0]
    part = grads[0].shape[1]
    where = jnp.stack([parity, parity + 2]).astype(jnp.int32)
    row = pl.BlockSpec((tok, width), lambda i, w: (i, 0))
    extra = () if base is None else (base,)
    shapes = [shape_of((2 * tok, width), BF16 if base is None else F32)]
    return call(
        hidden_back_kernel,
        "hidden_back",
        (2,),
        [pl.BlockSpec((tok, part), lambda i, w: (w[i], 0))] * 2 + [whole(weight.shape)] + [row] * len(extra),
        [row],
        shapes,
        2 * 2 * tok * width * part * 2,
        (where, *grads, weight, *extra),
        prefetch=1,
    )[0]


def after(x, *deps):
    return lax.optimization_barrier((x, deps))[0]


class Steps:
    def __init__(self):
        self.last = ()

    def __call__(self, fn, *args):
        args, _ = lax.optimization_barrier((args, self.last))
        out = fn(*args)
        self.last = out
        return out


def flip(x, axis, size, bit):
    return lax.ppermute(x, axis, [(i, i ^ bit) for i in range(size)])


def swap(x, bit):
    return flip(x, "fsdp", 8, bit)


def widen(*items):
    return sum(item.astype(F32) for item in items)


class CubeSum:
    def __init__(self, send, width, x_columns):
        self.got = swap(send, 1)
        self.parts = []
        if x_columns > 0:
            self.parts.append((slice(0, x_columns), 1, 2, 2, 4))
        if x_columns < width:
            self.parts.append((slice(x_columns, width), 2, 1, 4, 2))

    def first_hop(self, steps, keep):
        def add(keep, got):
            return [
                jnp.stack([widen(keep[i, :, cols], got[i, :, cols]).astype(BF16) for i in (away, 3)])
                for cols, _, away, _, _ in self.parts
            ]

        self.keep = keep
        there = steps(add, keep, self.got)
        self.back = [swap(x, part[3]) for x, part in zip(there, self.parts)]

    def second_hop(self, steps):
        def add(keep, got, back):
            here, there = [], []
            for (cols, near, _, _, _), b in zip(self.parts, back):
                here.append(widen(keep[0, :, cols], got[0, :, cols], b[0]))
                there.append(widen(keep[near, :, cols], got[near, :, cols], b[1]).astype(BF16))
            return here, there

        self.here, there = steps(add, self.keep, self.got, self.back)
        self.last = [swap(x, part[4]) for x, part in zip(there, self.parts)]

    def result(self, steps):
        def add(here, last):
            sums = [widen(x, y).astype(BF16) for x, y in zip(here, last)]
            return sums[0] if len(sums) == 1 else jnp.concatenate(sums, axis=1)

        return steps(add, self.here, self.last)


class PlainSum:
    def __init__(self, product, extra=()):
        self.product, self.extra = product.astype(BF16), extra

    def first_hop(self, steps, keep):
        pass

    def second_hop(self, steps):
        pass

    def result(self, steps):
        share = lax.psum_scatter(self.product, "fsdp", scatter_dimension=0, tiled=True)
        lines = [lax.psum_scatter(x, "fsdp", scatter_dimension=0, tiled=False) for x in self.extra]
        return (share, *lines) if lines else share


def pair_pack(parts):
    rows = parts[0].shape[0]
    return jnp.stack([p.reshape(rows, -1, PAIR) for p in parts], axis=2).reshape(rows, -1)


def pair_unpack(packed):
    rows = packed.shape[0]
    cut = packed.reshape(rows, -1, 3, PAIR)
    return [cut[:, :, i].reshape(rows, -1) for i in range(3)]


def body(
    fsdp,
    stream_in,
    timestep,
    doc_start,
    query_weight,
    key_weight,
    value_weight,
    output_weight,
    query_bias,
    value_bias,
    output_bias,
    first_gain,
    first_shift,
    inner_weight,
    inner_bias,
    outer_weight,
    outer_bias,
    second_gain,
    second_shift,
    cotangent,
):
    cube = fsdp == 8
    steps = Steps()
    me = lax.axis_index("fsdp")
    streams, tok, width = stream_in.shape
    own_rows = query_weight.shape[0]
    half = width // 2
    ff = inner_weight.shape[1]
    length = 4 * tok
    z = lax.axis_index("seq")
    h, s = z % 2, z // 2

    def flip_h(x):
        return flip(x, "seq", 4, 1)

    def flip_s(x):
        return flip(x, "seq", 4, 2)

    def in_order(mine, other):
        return jnp.where(s == 0, jnp.concatenate([mine, other]), jnp.concatenate([other, mine]))

    def pick(x, index, axis=0):
        return lax.dynamic_index_in_dim(x, index, axis, keepdims=False)

    head_cols = [lax.dynamic_slice_in_dim(w, h * half, half, 1) for w in (query_weight, key_weight, value_weight)]
    small = jnp.concatenate(
        [
            query_bias,
            value_bias,
            output_bias,
            first_gain,
            first_shift,
            outer_bias,
            second_gain,
            second_shift,
            inner_bias,
        ]
    )
    packed = pair_pack(head_cols)
    own = pick(stream_in, s)
    if cube:
        owners = [me ^ m for m in range(8)]
        packed = jnp.concatenate([packed, jnp.broadcast_to(small[None, :], (16, small.shape[0]))])
        gathered = lax.all_gather(packed, "fsdp", axis=0, tiled=False)
        full_qkv = gathered[:, :own_rows].reshape(-1, packed.shape[1])
        small_rows = gathered[:, own_rows]
        output_w = after(output_weight, gathered)
        full_output = lax.all_gather(output_w, "fsdp", axis=0, tiled=True)
        inner_w = after(inner_weight, packed)
        ix, iy = swap(inner_w, 2), swap(inner_w, 4)
        distant = flip_s(pick(stream_in, 1 - s))
        beside = flip_h(own)
        cut = own_rows // 2
        top, bottom, distant, beside, inner_w, outer_w = steps(
            lambda x, y, *rest: (x[:cut], y[cut:], *rest), ix, iy, distant, beside, inner_w, outer_weight
        )
        corner = flip_h(distant)
        jy, jx = swap(top, 4), swap(bottom, 2)
        ic = swap(inner_w, 1)
    else:
        owners = list(range(8))

        def gather(piece):
            full = lax.all_gather(piece, "fsdp", axis=0, tiled=True)
            return list(full.reshape(8, full.shape[0] // 8, full.shape[1]))

        distant, beside = flip_s(pick(stream_in, 1 - s)), flip_h(own)
        corner = flip_h(distant)
        full_qkv = lax.all_gather(packed, "fsdp", axis=0, tiled=True)
        full_output = lax.all_gather(output_weight, "fsdp", axis=0, tiled=True)
        inner_pieces, outer_pieces = gather(inner_weight), gather(outer_weight)
        small_rows = lax.all_gather(small, "fsdp", axis=0, tiled=False)
    order = jnp.stack([jnp.asarray(o, jnp.int32) for o in owners])
    small_rows = small_rows.astype(F32)
    qbias, vbias, obias, gain_one, shift_one, obias_two, gain_two, shift_two = [
        small_rows[:, i * own_rows : (i + 1) * own_rows].reshape(1, -1) for i in range(8)
    ]
    ibias = small_rows[:, 8 * own_rows :].reshape(1, -1)

    ts = pick(timestep, s).astype(F32)

    def place(own, beside, distant, corner):
        stream = jnp.zeros((length, width), BF16)
        for mask, block in ((0, own), (1, beside), (2, distant), (3, corner)):
            stream = lax.dynamic_update_slice(stream, block, ((z ^ mask) * tok, 0))
        stream_low = (stream.astype(F32) + ts).astype(BF16)
        return stream_low, in_order(own, distant).astype(F32) + ts

    if cube:
        own, ic, ix, corner, outer_w = steps(lambda *x: x, own, ic, ix, corner, outer_w)
        ox, oy = swap(outer_w, 2), swap(outer_w, 4)
        ixc = swap(ix, 1)
    stream_low, hidden = steps(place, own, beside, distant, corner)
    starts = pick(doc_start, s)
    bounds = block_bounds(starts)

    qb = lax.dynamic_slice_in_dim(qbias, h * half, half, 1)
    vb = lax.dynamic_slice_in_dim(vbias, h * half, half, 1)
    bias_row = pair_pack([qb, jnp.zeros_like(qb), vb])
    scale_row = pair_pack([jnp.full((1, half), 0.125, F32), jnp.ones((1, half), F32), jnp.ones((1, half), F32)])
    if cube:
        stream_low, ixc, iy = steps(lambda *x: x, stream_low, ixc, iy)
        iyc = swap(iy, 1)
    qkv = steps(
        lambda x, w, b: ((matmul(x, w) + b) * scale_row).astype(BF16), stream_low, full_qkv, bias_row
    )
    pairs = half // PAIR
    part = pairs // 2

    def rows_of(x, parity):
        cut = x.reshape(2, 2, tok, x.shape[1])
        return pick(cut, parity, 1).reshape(2 * tok, x.shape[1])

    def attend(index, qkv):
        return attention_forward(bounds, qkv, starts, index, part)

    if cube:
        jy, jx, iyc, qkv = steps(lambda *x: x, jy, jx, iyc, qkv)
        jyc, jxc = swap(jy, 1), swap(jx, 1)
    mixed_a, logsum_a = steps(partial(attend, 0), qkv)
    out_a, jyc, jxc = steps(
        lambda x, *rest: (rows_of(x, 1 - h), *rest), mixed_a, *((jyc, jxc) if cube else (0.0, 0.0))
    )
    their_a = flip_h(out_a)
    mixed_b, logsum_b = steps(partial(attend, 1), qkv)
    cotangent_out = pick(cotangent, 1 - s)
    if cube:
        inner_pieces = [inner_w, ic, ix, ixc, iy, iyc, jy, jx, jyc, jxc]
        cut = outer_weight.shape[0] // 2
        top, bottom, ox, oy = steps(lambda x, y: (x[:cut], y[cut:], x, y), ox, oy)
        jy, jx = swap(top, 4), swap(bottom, 2)
    out_b, their_a, cotangent_out = steps(lambda x, *rest: (rows_of(x, 1 - h), *rest), mixed_b, their_a, cotangent_out)
    their_b = flip_h(out_b)
    if cube:
        oxc = swap(ox, 1)
    moved = flip_s(cotangent_out)
    first_out, first_low, first_normed, first_factor, mixed = steps(
        partial(project_output, h),
        (mixed_a, mixed_b),
        (their_a, their_b),
        full_output,
        obias,
        hidden,
        gain_one,
        shift_one,
    )

    if cube:
        jy, jx, oxc, oy, outer_w, first_low = steps(lambda *x: x, jy, jx, oxc, oy, outer_w, first_low)
        oc, oyc, jyc, jxc = swap(outer_w, 1), swap(oy, 1), swap(jy, 1), swap(jx, 1)
        outer_pieces = [outer_w, oc, ox, oxc, oy, oyc, jy, jx, jyc, jxc]
    active, slope, full_inner = steps(partial(feed_inner, order), first_low, inner_pieces, ibias)
    upstream = in_order(pick(cotangent, s), moved)
    full_outer, result, grad_second_in, grad_outer, second_sums = steps(
        partial(feed_outer, order), active, outer_pieces, obias_two, first_out, upstream, gain_two, shift_two
    )
    result = result.reshape(2, tok, width)
    result_own, result_out = steps(lambda x: (pick(x, s), pick(x, 1 - s)), result)
    result_away = flip_s(result_out)

    if cube:
        send_order = jnp.stack([me ^ m for m in (1, 5, 3, 7)]).astype(jnp.int32)
        keep_order = jnp.stack([me ^ m for m in (0, 4, 2, 6)]).astype(jnp.int32)

    if cube:
        outer_send = steps(partial(block_grad, send_order), active, grad_outer)
        outer_sum = CubeSum(outer_send, width, half)
        outer_keep = steps(partial(block_grad, keep_order), active, grad_outer)
    else:
        outer_keep = ()
        outer_sum = PlainSum(contract_rows(active.transpose(1, 0, 2).reshape(2 * tok, -1), grad_outer))
    grad_inner, inner_sums = steps(gelu_back, grad_outer, full_outer, slope)
    outer_sum.first_hop(steps, outer_keep)
    if cube:
        inner_send = steps(partial(tile_grad, send_order), first_low, grad_inner)
        inner_sum = CubeSum(inner_send, ff, ff // 2)
    else:
        inner_sum = PlainSum(contract_rows(first_low, grad_inner.transpose(1, 0, 2).reshape(2 * tok, -1)))

    def first_step(*args):
        grad_first_in, grad_attended, grad_mixed, sums = first_back(*args)
        wide = half // 2
        theirs = lax.dynamic_slice_in_dim(grad_mixed, (1 - h) * half, half, 1)
        mine = lax.dynamic_slice_in_dim(grad_mixed, h * half, half, 1)
        return grad_first_in, grad_attended, sums, theirs, mine

    grad_first_in, grad_attended, first_sums, theirs, mine = steps(
        first_step, grad_inner, full_inner, grad_second_in, first_normed, first_factor, gain_one, full_output
    )
    received = flip_h(theirs)
    inner_keep = steps(partial(tile_grad, keep_order), first_low, grad_inner) if cube else ()
    outer_sum.second_hop(steps)

    def to_heads(mine, received):
        mine = mine.reshape(2, 1, tok, half)
        received = received.reshape(2, 1, tok, half)
        return jnp.where(
            h == 0, jnp.concatenate([mine, received], axis=1), jnp.concatenate([received, mine], axis=1)
        ).reshape(length, half)

    grad_heads = steps(to_heads, mine, received)

    def seq_sum(share):
        def halve(x, bit):
            pair = x.reshape(2, x.shape[0] // 2, -1)
            return pick(pair, bit), pick(pair, 1 - bit)

        def join(mine, other, bit):
            return jnp.where(bit == 0, jnp.concatenate([mine, other]), jnp.concatenate([other, mine]))

        mine, out = halve(share, h)
        back = flip_h(out)
        yield
        mine, out = steps(lambda m, b: halve(widen(m, b), s), mine, back)
        back = flip_s(out.astype(BF16))
        yield
        mine = steps(lambda m, b: widen(m, b).astype(BF16), mine, back)
        back = flip_s(mine)
        yield
        mine = steps(lambda m, b: join(m, b, s), mine, back)
        back = flip_h(mine)
        yield
        yield steps(lambda m, b: join(m, b, h).astype(F32), mine, back)

    def attend_back(index, qkv, mixed, logsum, grad):
        return attention_backward(bounds, qkv, starts, mixed, logsum, grad, index, part)

    grad_a, sums_a = steps(partial(attend_back, 0), qkv, mixed_a, logsum_a, grad_heads)
    inner_sum.first_hop(steps, inner_keep)
    outer_share = outer_sum.result(steps)
    outer_share, result_away = steps(lambda *x: x, outer_share, result_away)
    outer_steps = seq_sum(outer_share)
    next(outer_steps)
    grad_b, sums_b = steps(partial(attend_back, 1), qkv, mixed_b, logsum_b, grad_heads)
    away = flip_h(
        steps(lambda a, b, w: hidden_back(1 - h, (a, b), w, None, tok), grad_a, grad_b, full_qkv)
    )
    zero_half = jnp.zeros((half,), F32)

    def spread(v):
        v = v.reshape(-1)
        return jnp.where(h == 0, jnp.concatenate([v, zero_half]), jnp.concatenate([zero_half, v]))

    grad_q_cols, _, grad_v_cols = pair_unpack(jnp.concatenate([sums_a, sums_b], axis=1))
    vectors = jnp.concatenate(
        [
            v.reshape(fsdp, -1)
            for v in (
                spread(grad_q_cols),
                spread(grad_v_cols),
                first_sums[2],
                first_sums[0],
                first_sums[1],
                second_sums[2],
                second_sums[0],
                second_sums[1],
                inner_sums,
            )
        ],
        axis=1,
    ).astype(BF16)
    if cube:
        lines = vectors.reshape(fsdp, 1, -1)
        lines = jnp.concatenate([lines, jnp.zeros((fsdp, 15, lines.shape[2]), BF16)], axis=1)
        qkv_operands = (stream_low, grad_a, grad_b, lines, mixed, grad_attended)
        qkv_send = steps(partial(strip_grad, send_order), *qkv_operands)
        qkv_sum = CubeSum(qkv_send, qkv_send.shape[2], qkv_send.shape[2] // 2)
        inner_sum.second_hop(steps)
        next(outer_steps)
        qkv_keep = steps(partial(strip_grad, keep_order), *qkv_operands)
    else:
        qkv_keep = ()
        both = jnp.concatenate([grad_a, grad_b], axis=1)
        both = jnp.concatenate([contract_rows(stream_low, both), contract_rows(mixed, grad_attended)], axis=1)
        qkv_sum = PlainSum(both, (vectors,))
    kept = steps(lambda a, b, w, g: hidden_back(h, (a, b), w, g, tok), grad_a, grad_b, full_qkv, grad_first_in)

    def split_rows(kept, away):
        grad_hidden = (kept + away.astype(F32)).reshape(2, tok, width)
        return pick(grad_hidden, s), pick(grad_hidden, 1 - s).astype(BF16)

    grad_own, grad_out = steps(split_rows, kept, away)
    grad_away = flip_s(grad_out)
    if not cube:
        next(outer_steps)
    next(outer_steps)
    inner_share = inner_sum.result(steps)
    inner_steps = seq_sum(inner_share)
    next(inner_steps)
    qkv_sum.first_hop(steps, qkv_keep)
    next(outer_steps)
    next(inner_steps)
    qkv_sum.second_hop(steps)
    outer_grad = next(outer_steps)
    next(inner_steps)

    grad_away = grad_away.astype(F32)
    input_grad = jnp.where(s == 0, jnp.stack([grad_own, grad_away]), jnp.stack([grad_away, grad_own]))
    layer_out = jnp.where(s == 0, jnp.stack([result_own, result_away]), jnp.stack([result_away, result_own]))

    def swap_heads(mine, other):
        return jnp.where(h == 0, jnp.concatenate([mine, other], axis=1), jnp.concatenate([other, mine], axis=1))

    qkv_share = qkv_sum.result(steps)
    qkv_share, extra = qkv_share if not cube else (qkv_share, None)
    qkv_back = flip_s(qkv_share)
    next(inner_steps)
    qkv_mine = steps(lambda x, y: widen(x, y).astype(BF16), qkv_share, qkv_back)
    qkv_other = flip_h(qkv_mine)
    inner_grad = next(inner_steps)
    three = 3 * half
    output_grad = widen(qkv_mine[:own_rows, three:], qkv_other[:own_rows, three:])
    if cube:
        sums = widen(qkv_mine[own_rows, :three], qkv_other[own_rows, :three])
    else:
        sums = lax.psum(extra.astype(F32), "seq")
    qkv_grads = [
        swap_heads(mine, other).astype(F32)
        for mine, other in zip(
            pair_unpack(qkv_mine[:own_rows, :three]), pair_unpack(qkv_other[:own_rows, :three])
        )
    ]
    cut = [sums[i * own_rows : (i + 1) * own_rows] for i in range(8)]
    return (
        layer_out,
        input_grad,
        qkv_grads[0],
        qkv_grads[1],
        qkv_grads[2],
        output_grad,
        cut[0],
        cut[1],
        cut[2],
        cut[3],
        cut[4],
        inner_grad,
        sums[8 * own_rows :],
        outer_grad,
        cut[5],
        cut[6],
        cut[7],
    )


def solution(mesh):
    rows = P("fsdp", "seq", None)
    mat = P("fsdp", None)
    vec = P("fsdp")
    in_specs = (rows, mat, mat) + (mat,) * 4 + (vec,) * 5 + (mat, vec, mat, vec, vec, vec) + (rows,)
    out_specs = (rows, rows) + (mat,) * 4 + (vec,) * 5 + (mat, vec, mat, vec, vec, vec)
    return jax.shard_map(
        partial(body, mesh.shape["fsdp"]), mesh=mesh, in_specs=in_specs, out_specs=out_specs, check_vma=False
    )
```

time: 635 us -> 492 us (0.77)
  local copies, waits for them, and re-layouts: 161 us -> 59.9 us
  matrix products: 88.5 us -> 6.49 us
  Pallas kernels: 63.6 us -> 137 us
  waiting for transfers between devices: 199 us -> 168 us
  between operations: 2.91 us -> 16.1 us
  other arithmetic: 47.2 us -> 40.1 us
  starting transfers between devices: 62.1 us -> 55.1 us
    pallas_call x2 -> x17, Pallas kernels: 63.6 us -> 137 us  [call(): pl.pallas_call(kernel, grid_spec=pltpu.PrefetchScalarGridSpec(num_scalar_...]
    dynamic_update_slice x44 -> x4, local copies, waits for them, and re-layouts: 60.7 us -> 2.25 us  [place(): stream = lax.dynamic_update_slice(stream, block, ((z ^ mask) * tok, 0))]
    dot_general x12 -> x0, matrix products: 55.3 us -> none  [the longest x4 33.2 us: contract_cols(): lax.dot_general(left, right, (((1,), (1,)), ((), ())), preferred_element_...]
    ppermute x76 -> x53, waiting for transfers between devices: 199 us -> 168 us  [flip(): return lax.ppermute(x, axis, [(i, i ^ bit) for i in range(size)])]
    slice x35 -> x12, local copies, waits for them, and re-layouts: 38.3 us -> 10.2 us  [the longest x2 3.76 us: body(): top, bottom, ox, oy = steps(lambda x, y: (x[:cut], y[cut:], x, y), ox, oy)]
    dot_general x4 -> x1, matrix products: 33.1 us -> 6.49 us  [matmul(): return jnp.dot(left, right, preferred_element_type=F32)]
    unnamed x152 -> x181, local copies, waits for them, and re-layouts: 16.5 us -> 37.1 us
    add x22 -> x7, other arithmetic: 17.2 us -> 4.45 us  [the longest x1 2.85 us: place(): return (stream_low, in_order(own, distant).astype(F32) + ts)]
  transfers between devices with their start and end apart: 76 -> 55, of which waited for: 28 -> 14; matrix products, arithmetic and copies ran while one was open for 44% -> 12% of each run, Pallas kernels for 10% -> 23%
where the time goes in v2:
time: 492 us; the launch traced here: 482 us
  waiting for transfers between devices  168 us (34%)
  Pallas kernels  137 us (28%)
  local copies, waits for them, and re-layouts  59.9 us (12%)
  starting transfers between devices  55.1 us (11%)
  other arithmetic  40.1 us (8%)
  between operations  16.1 us (3%)
  matrix products  6.49 us (1%)
    ppermute x53, waiting for transfers between devices, flip(): return lax.ppermute(x, axis, [(i, i ^ bit) for i in range(size)])  168 us
    pallas_call x17, Pallas kernels, call(): pl.pallas_call(kernel, grid_spec=pltpu.PrefetchScalarGridSpec(num_scalar_...  137 us
    ppermute x53, starting transfers between devices, flip(): return lax.ppermute(x, axis, [(i, i ^ bit) for i in range(size)])  55.1 us
    unnamed x181, local copies, waits for them, and re-layouts  37.1 us
  transfers between devices with their start and end apart: 55, of which 14 were waited for; matrix products, arithmetic and copies ran while one was open for 12% of the time, Pallas kernels for 23%

profile of v2, /device:TPU:0, one launch (start us, length us, event | category | flops | bytes accessed | tf_op | source)
XLA Modules:
  0.0 482.5 jit_solution(13655640600606989738)
XLA Ops:
  13.0 3.0 collective-permute-start.1
  18.8 2.7 collective-permute-start.2
  23.0 21.3 %collective-permute-done.2 = bf16[256,1024]{1,0:T(8,128)(2,1)} collective-permute-done((bf16[256,1024]{1,0:T(8,128)(2,1)S(1)}, bf16[256,1024]{1,0:T(8,128)(2,1)}, u32[]{:S(2)}, u32[]{:S(2)}) %collective-permute-start.2) | collective-permute-done | bytes 524320 | tf_op jit(solution)/shard_map/ppermute | solution.py:715
  46.1 2.7 collective-permute-done.refs_2_
  53.2 2.4 collective-permute-start.9
  55.6 7.9 %collective-permute-done.5 = bf16[256,1024]{1,0:T(8,128)(2,1)} collective-permute-done((bf16[256,1024]{1,0:T(8,128)(2,1)}, bf16[256,1024]{1,0:T(8,128)(2,1)}, u32[]{:S(2)}, u32[]{:S(2)}) %collective-permute-start.5) | collective-permute-done | bytes 524320 | tf_op jit(solution)/shard_map/ppermute | solution.py:715
  63.5 2.5 collective-permute-start.6
  68.6 2.9 convert_add_fusion.1.refs_8_
  74.9 2.1 slice.468
  78.2 6.5 %multiply_convert_fusion.qkv_ref = bf16[1024,1536]{1,0:T(8,128)(2,1)} fusion(bf16[1024,1024]{1,0:T(8,128)(2,1)} %add_convert_fusion.left_ref, bf16[1024,1536]{1,0:T(8,128)(2,1)S(1)} %bitcast.178, f32[1536]{0:T(1024)S(1)} %copy-done.75, f32[1536]{0:T(1024)S(1)} %reduce.3), kind=kOutput, calls=%fused_computation | convolution fusion | flops 3225944064 | bytes 8400896 | tf_op jit(solution)/shard_map/dot_general | solution.py:56
  91.2 7.7 %attend.2 = (bf16[1024,256]{1,0:T(8,128)(2,1)S(1)}, f32[2,2,1024]{2,1,0:T(2,128)S(1)}) custom-call(s32[4,2]{1,0:T(4,128)S(1)} %pad_add_fusion.bounds, bf16[1024,1536]{1,0:T(8,128)(2,1)S(1)} %copy-done.51, s32[1,1024]{1,0:T(1,128)S(1)} %get-tuple-element.504.row_ref, s32[1024,1]{1,0:T(8,128)S(1)} %copy-done.33), custom_call_target="tpu_custom_call" | custom-call | flops 1073741824 | bytes 3694624 | tf_op jit(solution)/shard_map/attend/pallas_call | solution.py:261
  99.7 8.0 %attend.3 = (bf16[1024,256]{1,0:T(8,128)(2,1)S(1)}, f32[2,2,1024]{2,1,0:T(2,128)S(1)}) custom-call(s32[4,2]{1,0:T(4,128)S(1)} %pad_add_fusion.bounds, bf16[1024,1536]{1,0:T(8,128)(2,1)S(1)} %copy-done.51, s32[1,1024]{1,0:T(1,128)S(1)} %get-tuple-element.504.row_ref, s32[1024,1]{1,0:T(8,128)S(1)} %copy-done.33), custom_call_target="tpu_custom_call" | custom-call | flops 1073741824 | bytes 3694624 | tf_op jit(solution)/shard_map/attend/pallas_call | solution.py:261
  118.7 2.8 collective-permute-start.23
  121.5 9.2 %collective-permute-done.18.refs_5_ = bf16[512,256]{1,0:T(8,128)(2,1)} collective-permute-done((bf16[512,256]{1,0:T(8,128)(2,1)}, bf16[512,256]{1,0:T(8,128)(2,1)}, u32[]{:S(2)}, u32[]{:S(2)}) %collective-permute-start.18) | collective-permute-done | bytes 262176 | tf_op jit(solution)/shard_map/ppermute | solution.py:715
  136.0 3.4 project_output.1
  151.9 17.6 %feed_inner.1 = (bf16[8,512,512]{2,1,0:T(8,128)(2,1)S(1)}, bf16[8,512,512]{2,1,0:T(8,128)(2,1)S(1)}, bf16[1024,4096]{1,0:T(8,128)(2,1)}) custom-call(s32[8]{0:T(128)S(1)} %stack.142.order, bf16[512,1024]{1,0:T(8,128)(2,1)S(1)} %copy-done.17, bf16[128,4096]{1,0:T(8,128)(2,1)S(1)} %copy-done.42, bf16[128,4096]{1,0:T(8,128)(2,1)S(1)} %copy-done.44, ...), custom_call_target="tpu_custom_call" | custom-call | flops 4294967296 | bytes 26230816 | tf_op jit(solution)/shard_map/feed_inner/pallas_call | solution.py:261
  169.5 12.9 %feed_outer.1 = (bf16[8,512,1024]{2,1,0:T(8,128)(2,1)}, bf16[512,1024]{1,0:T(8,128)(2,1)S(1)}, f32[512,1024]{1,0:T(8,128)S(1)}, bf16[512,1024]{1,0:T(8,128)(2,1)S(1)}, f32[8,1024]{1,0:T(8,128)S(1)}) custom-call(s32[8]{0:T(128)S(1)} %stack.142.order, bf16[8,512,512]{2,1,0:T(8,128)(2,1)S(1)} %get-tuple-element.324.active_ref.left_ref, ...), custom_call_target="tpu_custom_call" | custom-call | flops 4294967296 | bytes 28356640 | tf_op jit(solution)/shard_map/feed_outer/pallas_call | solution.py:261
  183.6 4.8 block_grad.2
  188.6 3.6 block_grad.3
  192.2 6.4 %gelu_back.1 = (bf16[8,512,512]{2,1,0:T(8,128)(2,1)S(1)}, f32[8,1,512]{2,1,0:T(1,128)S(1)}) custom-call(bf16[512,1024]{1,0:T(8,128)(2,1)S(1)} %get-tuple-element.326.right_ref.grad_ref, bf16[8,512,1024]{2,1,0:T(8,128)(2,1)S(1)} %bitcast.196, bf16[8,512,512]{2,1,0:T(8,128)(2,1)S(1)} %copy-done.54), custom_call_target="tpu_custom_call" | custom-call | flops 4294967296 | bytes 17842176 | tf_op jit(solution)/shard_map/gelu_back/pallas_call | solution.py:261
  198.7 3.6 add_convert_fusion.15
  204.4 6.5 %tile_grad.2 = bf16[4,128,4096]{2,1,0:T(8,128)(2,1)} custom-call(s32[4]{0:T(128)S(1)} %pad_add_fusion.3.order, bf16[512,1024]{1,0:T(8,128)(2,1)S(1)} %copy-done.17, bf16[8,512,512]{2,1,0:T(8,128)(2,1)S(1)} %get-tuple-element.347.right_ref.grad_ref), custom_call_target="tpu_custom_call" | custom-call | flops 2147483648 | bytes 9437200 | tf_op jit(solution)/shard_map/tile_grad/pallas_call | solution.py:261
  211.3 2.8 collective-permute-start.25
  214.2 2.2 copy-done.10
  222.1 12.3 %first_back.1 = (f32[512,1024]{1,0:T(8,128)S(1)}, bf16[512,1024]{1,0:T(8,128)(2,1)S(1)}, bf16[512,1024]{1,0:T(8,128)(2,1)S(1)}, f32[8,1024]{1,0:T(8,128)S(1)}) custom-call(bf16[8,512,512]{2,1,0:T(8,128)(2,1)S(1)} %copy-done.10, bf16[1024,4096]{1,0:T(8,128)(2,1)} %get-tuple-element.336.weight_ref, f32[512,1024]{1,0:T(8,128)S(1)} %copy-done.50, ...), custom_call_target="tpu_custom_call" | custom-call | flops 5368709120 | bytes 23107584 | tf_op jit(solution)/shard_map/first_back/pallas_call | solution.py:261
  234.6 2.5 collective-permute-start.30
  237.1 13.7 %tile_grad.3 = bf16[4,128,4096]{2,1,0:T(8,128)(2,1)S(1)} custom-call(s32[4]{0:T(128)S(1)} %pad_add_fusion.2.order, bf16[512,1024]{1,0:T(8,128)(2,1)S(1)} %copy-done.18, bf16[8,512,512]{2,1,0:T(8,128)(2,1)S(1)} %copy-done.10), custom_call_target="tpu_custom_call" | custom-call | flops 2147483648 | bytes 9437200 | tf_op jit(solution)/shard_map/tile_grad/pallas_call | solution.py:261
  250.8 4.5 fusion.3
  257.7 10.8 %attend_back.2 = (bf16[1024,768]{1,0:T(8,128)(2,1)S(1)}, f32[1,768]{1,0:T(1,128)S(1)}) custom-call(s32[4,2]{1,0:T(4,128)S(1)} %pad_add_fusion.bounds, bf16[1024,1536]{1,0:T(8,128)(2,1)S(1)} %copy-done.52, s32[1,1024]{1,0:T(1,128)S(1)} %get-tuple-element.504.row_ref, s32[1024,1]{1,0:T(8,128)S(1)} %copy-done.34, bf16[1024,256]{1,0:T(8,128)(2,1)S(1)} %copy-done.28, ...), custom_call_target="tpu_custom_call" | custom-call | flops 2684354560 | bytes 6319136 | tf_op jit(solution)/shard_map/attend_back/pallas_call | solution.py:261
  268.6 2.9 add_convert_fusion.9
  277.1 11.0 %attend_back.3 = (bf16[1024,768]{1,0:T(8,128)(2,1)S(1)}, f32[1,768]{1,0:T(1,128)S(1)}) custom-call(s32[4,2]{1,0:T(4,128)S(1)} %pad_add_fusion.bounds, bf16[1024,1536]{1,0:T(8,128)(2,1)S(1)} %copy-done.52, s32[1,1024]{1,0:T(1,128)S(1)} %get-tuple-element.504.row_ref, s32[1024,1]{1,0:T(8,128)S(1)} %copy-done.34, bf16[1024,256]{1,0:T(8,128)(2,1)S(1)} %copy-done.25, ...), custom_call_target="tpu_custom_call" | custom-call | flops 2684354560 | bytes 6319136 | tf_op jit(solution)/shard_map/attend_back/pallas_call | solution.py:261
  292.5 2.6 hidden_back.2
  297.3 6.2 %strip_grad.2 = bf16[4,144,2560]{2,1,0:T(8,128)(2,1)S(1)} custom-call(s32[4]{0:T(128)S(1)} %pad_add_fusion.3.order, bf16[1024,1024]{1,0:T(8,128)(2,1)S(1)} %copy-done.8, bf16[1024,768]{1,0:T(8,128)(2,1)S(1)} %copy-done.3, bf16[1024,768]{1,0:T(8,128)(2,1)S(1)} %copy-done.6, bf16[8,16,1536]{2,1,0:T(8,128)(2,1)S(1)} %concatenate.143.extra_ref, ...), custom_call_target="tpu_custom_call" | custom-call | flops 2684354560 | bytes 10682384 | tf_op jit(solution)/shard_map/strip_grad/pallas_call | solution.py:261
  304.8 3.5 fusion.5
  310.3 19.6 %collective-permute-done.32 = bf16[256,1024]{1,0:T(8,128)(2,1)S(1)} collective-permute-done((bf16[256,1024]{1,0:T(8,128)(2,1)S(1)}, bf16[256,1024]{1,0:T(8,128)(2,1)S(1)}, u32[]{:S(2)}, u32[]{:S(2)}) %collective-permute-start.32) | collective-permute-done | bytes 524320 | tf_op jit(solution)/shard_map/ppermute | solution.py:715
  330.1 2.3 collective-permute-start.40
  332.5 6.2 %strip_grad.3 = bf16[4,144,2560]{2,1,0:T(8,128)(2,1)S(1)} custom-call(s32[4]{0:T(128)S(1)} %pad_add_fusion.2.order, bf16[1024,1024]{1,0:T(8,128)(2,1)S(1)} %copy-done.8, bf16[1024,768]{1,0:T(8,128)(2,1)S(1)} %copy-done.3, bf16[1024,768]{1,0:T(8,128)(2,1)S(1)} %copy-done.7, bf16[8,16,1536]{2,1,0:T(8,128)(2,1)S(1)} %concatenate.143.extra_ref, ...), custom_call_target="tpu_custom_call" | custom-call | flops 2684354560 | bytes 10682384 | tf_op jit(solution)/shard_map/strip_grad/pallas_call | solution.py:261
  338.7 2.8 hidden_back.3
  343.1 2.3 collective-permute-start.44
  348.8 27.5 %collective-permute-done.44 = bf16[128,1024]{1,0:T(8,128)(2,1)S(1)} collective-permute-done((bf16[128,1024]{1,0:T(8,128)(2,1)S(1)}, bf16[128,1024]{1,0:T(8,128)(2,1)S(1)}, u32[]{:S(2)}, u32[]{:S(2)}) %collective-permute-start.44) | collective-permute-done | bytes 262176 | tf_op jit(solution)/shard_map/ppermute | solution.py:715
  376.7 2.5 collective-permute-start.47
  381.8 14.2 %collective-permute-done.48 = bf16[256,1024]{1,0:T(8,128)(2,1)S(1)} collective-permute-done((bf16[256,1024]{1,0:T(8,128)(2,1)S(1)}, bf16[256,1024]{1,0:T(8,128)(2,1)S(1)}, u32[]{:S(2)}, u32[]{:S(2)}) %collective-permute-start.48) | collective-permute-done | bytes 524320 | tf_op jit(solution)/shard_map/ppermute | solution.py:715
  398.1 3.0 collective-permute-start.49
  402.8 24.2 %collective-permute-done.50 = bf16[32,4096]{1,0:T(8,128)(2,1)S(1)} collective-permute-done((bf16[32,4096]{1,0:T(8,128)(2,1)S(1)}, bf16[32,4096]{1,0:T(8,128)(2,1)S(1)}, u32[]{:S(2)}, u32[]{:S(2)}) %collective-permute-start.50) | collective-permute-done | bytes 262176 | tf_op jit(solution)/shard_map/ppermute | solution.py:715
  427.1 15.6 %collective-permute-done.49 = bf16[144,2560]{1,0:T(8,128)(2,1)S(1)} collective-permute-done((bf16[144,2560]{1,0:T(8,128)(2,1)S(1)}, bf16[144,2560]{1,0:T(8,128)(2,1)S(1)}, u32[]{:S(2)}, u32[]{:S(2)}) %collective-permute-start.49) | collective-permute-done | bytes 737312 | tf_op jit(solution)/shard_map/ppermute | solution.py:715
  443.0 11.0 %collective-permute-done.52 = bf16[64,4096]{1,0:T(8,128)(2,1)} collective-permute-done((bf16[64,4096]{1,0:T(8,128)(2,1)S(1)}, bf16[64,4096]{1,0:T(8,128)(2,1)}, u32[]{:S(2)}, u32[]{:S(2)}) %collective-permute-start.52) | collective-permute-done | bytes 524320 | tf_op jit(solution)/shard_map/ppermute | solution.py:715
  454.3 2.8 fusion.1
  457.1 12.6 %collective-permute-done.51 = bf16[144,2560]{1,0:T(8,128)(2,1)S(1)} collective-permute-done((bf16[144,2560]{1,0:T(8,128)(2,1)S(1)}, bf16[144,2560]{1,0:T(8,128)(2,1)S(1)}, u32[]{:S(2)}, u32[]{:S(2)}) %collective-permute-start.51) | collective-permute-done | bytes 737312 | tf_op jit(solution)/shard_map/ppermute | solution.py:715
  (380 shorter events, 104.6 us)
Async XLA Ops:
  7.3 67.6 %all-gather.6.cloned.1.call-start = ((), (), s32[]{:S(2)}) async-start(), calls=%async_computation.1 | async-start | bytes 3981312 | tf_op jit(solution)/shard_map/all_gather | solution.py:856
  12.9 117.8 %all-gather.4.cloned.1.call-start = ((), (), s32[]{:S(2)}) async-start(), calls=%async_computation | async-start | bytes 2359296 | tf_op jit(solution)/shard_map/all_gather | solution.py:860
  13.0 33.1 %collective-permute-start.1 = (bf16[128,4096]{1,0:T(8,128)(2,1)S(1)}, bf16[128,4096]{1,0:T(8,128)(2,1)}, u32[]{:S(2)}, u32[]{:S(2)}) collective-permute-start(bf16[128,4096]{1,0:T(8,128)(2,1)S(1)} %copy-done.41), channel_id=1, source_target_pairs={{0,4},{1,5},{2,6},{3,7},{4,0},{5,1},{6,2},{7,3},{8,12},{9,13},{10,... | collective-permute-start | bytes 3145736 | tf_op jit(solution)/shard_map/ppermute | solution.py:715
  16.0 32.8 %collective-permute-start = (bf16[128,4096]{1,0:T(8,128)(2,1)S(1)}, bf16[128,4096]{1,0:T(8,128)(2,1)S(1)}, u32[]{:S(2)}, u32[]{:S(2)}) collective-permute-start(bf16[128,4096]{1,0:T(8,128)(2,1)S(1)} %copy-done.41), channel_id=1, source_target_pairs={{0,2},{1,3},{2,0},{3,1},{4,6},{5,7},{6,4},{7,5},{8,10},{9,11},{10,... | collective-permute-start | bytes 3145736 | tf_op jit(solution)/shard_map/ppermute | solution.py:715
  18.8 25.5 %collective-permute-start.2 = (bf16[256,1024]{1,0:T(8,128)(2,1)S(1)}, bf16[256,1024]{1,0:T(8,128)(2,1)}, u32[]{:S(2)}, u32[]{:S(2)}) collective-permute-start(bf16[256,1024]{1,0:T(8,128)(2,1)S(1)} %get-tuple-element.545), channel_id=1, source_target_pairs={{0,16},{8,24},{16,0},{24,8},{1,17},{9,25},{17,1},{25,9},{2,18},{10... | collective-permute-start | bytes 1572872 | tf_op jit(solution)/shard_map/ppermute | solution.py:715
  21.4 22.9 %collective-permute-start.3 = (bf16[256,1024]{1,0:T(8,128)(2,1)S(1)}, bf16[256,1024]{1,0:T(8,128)(2,1)S(1)}, u32[]{:S(2)}, u32[]{:S(2)}) collective-permute-start(bf16[256,1024]{1,0:T(8,128)(2,1)S(1)} %get-tuple-element.236), channel_id=1, source_target_pairs={{0,8},{8,0},{16,24},{24,16},{1,9},{9,1},{17,25},{25,17},{2,10},{10... | collective-permute-start | bytes 1572872 | tf_op jit(solution)/shard_map/ppermute | solution.py:715
  48.8 14.7 %collective-permute-start.4 = (bf16[128,4096]{1,0:T(8,128)(2,1)S(1)}, bf16[128,4096]{1,0:T(8,128)(2,1)S(1)}, u32[]{:S(2)}, u32[]{:S(2)}) collective-permute-start(bf16[128,4096]{1,0:T(8,128)(2,1)S(1)} %copy-done.41), channel_id=1, source_target_pairs={{0,1},{1,0},{2,3},{3,2},{4,5},{5,4},{6,7},{7,6},{8,9},{9,8},{10,11... | collective-permute-start | bytes 3145736 | tf_op jit(solution)/shard_map/ppermute | solution.py:715
  48.8 14.7 %collective-permute-start.5 = (bf16[256,1024]{1,0:T(8,128)(2,1)}, bf16[256,1024]{1,0:T(8,128)(2,1)}, u32[]{:S(2)}, u32[]{:S(2)}) collective-permute-start(bf16[256,1024]{1,0:T(8,128)(2,1)} %collective-permute-done.2), channel_id=1, source_target_pairs={{0,8},{8,0},{16,24},{24,16},{1,9},{9,1},{17,25},{25,17},{2,10},{10... | collective-permute-start | bytes 1572872 | tf_op jit(solution)/shard_map/ppermute | solution.py:715
  53.2 31.6 %collective-permute-start.9 = (bf16[64,4096]{1,0:T(8,128)(2,1)}, bf16[64,4096]{1,0:T(8,128)(2,1)}, u32[]{:S(2)}, u32[]{:S(2)}) collective-permute-start(bf16[64,4096]{1,0:T(8,128)(2,1)} %slice.352), channel_id=1, source_target_pairs={{0,2},{1,3},{2,0},{3,1},{4,6},{5,7},{6,4},{7,5},{8,10},{9,11},{10,... | collective-permute-start | bytes 1572872 | tf_op jit(solution)/shard_map/ppermute | solution.py:715
  55.6 29.1 %collective-permute-start.8 = (bf16[64,4096]{1,0:T(8,128)(2,1)}, bf16[64,4096]{1,0:T(8,128)(2,1)}, u32[]{:S(2)}, u32[]{:S(2)}) collective-permute-start(bf16[64,4096]{1,0:T(8,128)(2,1)} %slice.351), channel_id=1, source_target_pairs={{0,4},{1,5},{2,6},{3,7},{4,0},{5,1},{6,2},{7,3},{8,12},{9,13},{10,... | collective-permute-start | bytes 1572872 | tf_op jit(solution)/shard_map/ppermute | solution.py:715
  63.5 44.2 %collective-permute-start.7 = (bf16[512,1024]{1,0:T(8,128)(2,1)}, bf16[512,1024]{1,0:T(8,128)(2,1)}, u32[]{:S(2)}, u32[]{:S(2)}) collective-permute-start(bf16[512,1024]{1,0:T(8,128)(2,1)} %refs_0_.1), channel_id=1, source_target_pairs={{0,4},{1,5},{2,6},{3,7},{4,0},{5,1},{6,2},{7,3},{8,12},{9,13},{10,... | collective-permute-start | bytes 3145736 | tf_op jit(solution)/shard_map/ppermute | solution.py:715
  63.5 44.2 %collective-permute-start.6 = (bf16[512,1024]{1,0:T(8,128)(2,1)}, bf16[512,1024]{1,0:T(8,128)(2,1)}, u32[]{:S(2)}, u32[]{:S(2)}) collective-permute-start(bf16[512,1024]{1,0:T(8,128)(2,1)} %refs_0_.1), channel_id=1, source_target_pairs={{0,2},{1,3},{2,0},{3,1},{4,6},{5,7},{6,4},{7,5},{8,10},{9,11},{10,... | collective-permute-start | bytes 3145736 | tf_op jit(solution)/shard_map/ppermute | solution.py:715
  84.8 14.2 %collective-permute-start.12 = (bf16[64,4096]{1,0:T(8,128)(2,1)}, bf16[64,4096]{1,0:T(8,128)(2,1)}, u32[]{:S(2)}, u32[]{:S(2)}) collective-permute-start(bf16[64,4096]{1,0:T(8,128)(2,1)} %collective-permute-done.8.refs_6_), channel_id=1, source_target_pairs={{0,1},{1,0},{2,3},{3,2},{4,5},{5,4},{6,7},{7,6},{8,9},{9,8},{10,11... | collective-permute-start | bytes 1572872 | tf_op jit(solution)/shard_map/ppermute | solution.py:715
  107.7 37.1 %collective-permute-start.16 = (bf16[512,1024]{1,0:T(8,128)(2,1)}, bf16[512,1024]{1,0:T(8,128)(2,1)}, u32[]{:S(2)}, u32[]{:S(2)}) collective-permute-start(bf16[512,1024]{1,0:T(8,128)(2,1)} %collective-permute-done.6.refs_2_), channel_id=1, source_target_pairs={{0,1},{1,0},{2,3},{3,2},{4,5},{5,4},{6,7},{7,6},{8,9},{9,8},{10,11... | collective-permute-start | bytes 3145736 | tf_op jit(solution)/shard_map/ppermute | solution.py:715
  113.0 31.7 %collective-permute-start.14 = (bf16[256,1024]{1,0:T(8,128)(2,1)}, bf16[256,1024]{1,0:T(8,128)(2,1)}, u32[]{:S(2)}, u32[]{:S(2)}) collective-permute-start(bf16[256,1024]{1,0:T(8,128)(2,1)} %slice.359), channel_id=1, source_target_pairs={{0,4},{1,5},{2,6},{3,7},{4,0},{5,1},{6,2},{7,3},{8,12},{9,13},{10,... | collective-permute-start | bytes 1572872 | tf_op jit(solution)/shard_map/ppermute | solution.py:715
  115.0 29.8 %collective-permute-start.15 = (bf16[256,1024]{1,0:T(8,128)(2,1)}, bf16[256,1024]{1,0:T(8,128)(2,1)}, u32[]{:S(2)}, u32[]{:S(2)}) collective-permute-start(bf16[256,1024]{1,0:T(8,128)(2,1)} %slice.360), channel_id=1, source_target_pairs={{0,2},{1,3},{2,0},{3,1},{4,6},{5,7},{6,4},{7,5},{8,10},{9,11},{10,... | collective-permute-start | bytes 1572872 | tf_op jit(solution)/shard_map/ppermute | solution.py:715
  118.7 27.4 %collective-permute-start.23 = (bf16[256,1024]{1,0:T(8,128)(2,1)}, bf16[256,1024]{1,0:T(8,128)(2,1)}, u32[]{:S(2)}, u32[]{:S(2)}) collective-permute-start(bf16[256,1024]{1,0:T(8,128)(2,1)} %get-tuple-element.264), channel_id=1, source_target_pairs={{0,16},{8,24},{16,0},{24,8},{1,17},{9,25},{17,1},{25,9},{2,18},{10... | collective-permute-start | bytes 1572872 | tf_op jit(solution)/shard_map/ppermute | solution.py:715
  144.8 24.7 %collective-permute-start.20 = (bf16[512,1024]{1,0:T(8,128)(2,1)}, bf16[512,1024]{1,0:T(8,128)(2,1)}, u32[]{:S(2)}, u32[]{:S(2)}) collective-permute-start(bf16[512,1024]{1,0:T(8,128)(2,1)} %collective-permute-done.7.refs_4_), channel_id=1, source_target_pairs={{0,1},{1,0},{2,3},{3,2},{4,5},{5,4},{6,7},{7,6},{8,9},{9,8},{10,11... | collective-permute-start | bytes 3145736 | tf_op jit(solution)/shard_map/ppermute | solution.py:715
  144.9 24.6 %collective-permute-start.19 = (bf16[512,1024]{1,0:T(8,128)(2,1)}, bf16[512,1024]{1,0:T(8,128)(2,1)}, u32[]{:S(2)}, u32[]{:S(2)}) collective-permute-start(bf16[512,1024]{1,0:T(8,128)(2,1)} %refs_0_.1), channel_id=1, source_target_pairs={{0,1},{1,0},{2,3},{3,2},{4,5},{5,4},{6,7},{7,6},{8,9},{9,8},{10,11... | collective-permute-start | bytes 3145736 | tf_op jit(solution)/shard_map/ppermute | solution.py:715
  145.6 23.9 %collective-permute-start.21 = (bf16[256,1024]{1,0:T(8,128)(2,1)}, bf16[256,1024]{1,0:T(8,128)(2,1)S(1)}, u32[]{:S(2)}, u32[]{:S(2)}) collective-permute-start(bf16[256,1024]{1,0:T(8,128)(2,1)} %collective-permute-done.14.refs_6_), channel_id=1, source_target_pairs={{0,1},{1,0},{2,3},{3,2},{4,5},{5,4},{6,7},{7,6},{8,9},{9,8},{10,11... | collective-permute-start | bytes 1572872 | tf_op jit(solution)/shard_map/ppermute | solution.py:715
  145.7 23.8 %collective-permute-start.22 = (bf16[256,1024]{1,0:T(8,128)(2,1)}, bf16[256,1024]{1,0:T(8,128)(2,1)S(1)}, u32[]{:S(2)}, u32[]{:S(2)}) collective-permute-start(bf16[256,1024]{1,0:T(8,128)(2,1)} %collective-permute-done.15.refs_7_), channel_id=1, source_target_pairs={{0,1},{1,0},{2,3},{3,2},{4,5},{5,4},{6,7},{7,6},{8,9},{9,8},{10,11... | collective-permute-start | bytes 1572872 | tf_op jit(solution)/shard_map/ppermute | solution.py:715
  210.9 57.7 %collective-permute-start.29 = (bf16[4,128,4096]{2,1,0:T(8,128)(2,1)}, bf16[4,128,4096]{2,1,0:T(8,128)(2,1)}, u32[]{:S(2)}, u32[]{:S(2)}) collective-permute-start(bf16[4,128,4096]{2,1,0:T(8,128)(2,1)} %tile_grad.2), channel_id=1, source_target_pairs={{0,1},{1,0},{2,3},{3,2},{4,5},{5,4},{6,7},{7,6},{8,9},{9,8},{10,11... | collective-permute-start | bytes 12582920 | tf_op jit(solution)/shard_map/ppermute | solution.py:715
  211.3 39.5 %collective-permute-start.25 = (bf16[2,512,512]{2,1,0:T(8,128)(2,1)}, bf16[2,512,512]{2,1,0:T(8,128)(2,1)}, u32[]{:S(2)}, u32[]{:S(2)}) collective-permute-start(bf16[2,512,512]{2,1,0:T(8,128)(2,1)} %pad_maximum_fusion), channel_id=1, source_target_pairs={{0,2},{1,3},{2,0},{3,1},{4,6},{5,7},{6,4},{7,5},{8,10},{9,11},{10,... | collective-permute-start | bytes 3145736 | tf_op jit(solution)/shard_map/ppermute | solution.py:715
  214.1 36.7 %collective-permute-start.26 = (bf16[2,512,512]{2,1,0:T(8,128)(2,1)}, bf16[2,512,512]{2,1,0:T(8,128)(2,1)}, u32[]{:S(2)}, u32[]{:S(2)}) collective-permute-start(bf16[2,512,512]{2,1,0:T(8,128)(2,1)} %pad_maximum_fusion.1), channel_id=1, source_target_pairs={{0,4},{1,5},{2,6},{3,7},{4,0},{5,1},{6,2},{7,3},{8,12},{9,13},{10,... | collective-permute-start | bytes 3145736 | tf_op jit(solution)/shard_map/ppermute | solution.py:715
  214.2 63.0 %collective-permute-start.31 = (bf16[256,1024]{1,0:T(8,128)(2,1)}, bf16[256,1024]{1,0:T(8,128)(2,1)S(1)}, u32[]{:S(2)}, u32[]{:S(2)}) collective-permute-start(bf16[256,1024]{1,0:T(8,128)(2,1)} %get-tuple-element.540), channel_id=1, source_target_pairs={{0,16},{8,24},{16,0},{24,8},{1,17},{9,25},{17,1},{25,9},{2,18},{10... | collective-permute-start | bytes 1572872 | tf_op jit(solution)/shard_map/ppermute | solution.py:715
  234.6 22.9 %collective-permute-start.30 = (bf16[512,512]{1,0:T(8,128)(2,1)S(1)}, bf16[512,512]{1,0:T(8,128)(2,1)S(1)}, u32[]{:S(2)}, u32[]{:S(2)}) collective-permute-start(bf16[512,512]{1,0:T(8,128)(2,1)S(1)} %get-tuple-element.542), channel_id=1, source_target_pairs={{0,8},{8,0},{16,24},{24,16},{1,9},{9,1},{17,25},{25,17},{2,10},{10... | collective-permute-start | bytes 1572872 | tf_op jit(solution)/shard_map/ppermute | solution.py:715
  255.4 20.3 %collective-permute-start.28 = (bf16[512,512]{1,0:T(8,128)(2,1)S(1)}, bf16[512,512]{1,0:T(8,128)(2,1)S(1)}, u32[]{:S(2)}, u32[]{:S(2)}) collective-permute-start(bf16[512,512]{1,0:T(8,128)(2,1)S(1)} %get-tuple-element.509), channel_id=1, source_target_pairs={{0,2},{1,3},{2,0},{3,1},{4,6},{5,7},{6,4},{7,5},{8,10},{9,11},{10,... | collective-permute-start | bytes 1572872 | tf_op jit(solution)/shard_map/ppermute | solution.py:715
  257.5 18.2 %collective-permute-start.27 = (bf16[512,512]{1,0:T(8,128)(2,1)S(1)}, bf16[512,512]{1,0:T(8,128)(2,1)S(1)}, u32[]{:S(2)}, u32[]{:S(2)}) collective-permute-start(bf16[512,512]{1,0:T(8,128)(2,1)S(1)} %get-tuple-element.520), channel_id=1, source_target_pairs={{0,4},{1,5},{2,6},{3,7},{4,0},{5,1},{6,2},{7,3},{8,12},{9,13},{10,... | collective-permute-start | bytes 1572872 | tf_op jit(solution)/shard_map/ppermute | solution.py:715
  272.5 32.2 %collective-permute-start.33 = (bf16[2,128,2048]{2,1,0:T(8,128)(2,1)}, bf16[2,128,2048]{2,1,0:T(8,128)(2,1)}, u32[]{:S(2)}, u32[]{:S(2)}) collective-permute-start(bf16[2,128,2048]{2,1,0:T(8,128)(2,1)} %pad_maximum_fusion.2), channel_id=1, source_target_pairs={{0,2},{1,3},{2,0},{3,1},{4,6},{5,7},{6,4},{7,5},{8,10},{9,11},{10,... | collective-permute-start | bytes 3145736 | tf_op jit(solution)/shard_map/ppermute | solution.py:715
  275.0 29.8 %collective-permute-start.34 = (bf16[2,128,2048]{2,1,0:T(8,128)(2,1)}, bf16[2,128,2048]{2,1,0:T(8,128)(2,1)}, u32[]{:S(2)}, u32[]{:S(2)}) collective-permute-start(bf16[2,128,2048]{2,1,0:T(8,128)(2,1)} %pad_maximum_fusion.3), channel_id=1, source_target_pairs={{0,4},{1,5},{2,6},{3,7},{4,0},{5,1},{6,2},{7,3},{8,12},{9,13},{10,... | collective-permute-start | bytes 3145736 | tf_op jit(solution)/shard_map/ppermute | solution.py:715
  295.1 46.5 %collective-permute-start.35 = (bf16[512,1024]{1,0:T(8,128)(2,1)S(1)}, bf16[512,1024]{1,0:T(8,128)(2,1)S(1)}, u32[]{:S(2)}, u32[]{:S(2)}) collective-permute-start(bf16[512,1024]{1,0:T(8,128)(2,1)S(1)} %hidden_back.2), channel_id=1, source_target_pairs={{0,8},{8,0},{16,24},{24,16},{1,9},{9,1},{17,25},{25,17},{2,10},{10... | collective-permute-start | bytes 3145736 | tf_op jit(solution)/shard_map/ppermute | solution.py:715
  297.1 32.9 %collective-permute-start.32 = (bf16[256,1024]{1,0:T(8,128)(2,1)S(1)}, bf16[256,1024]{1,0:T(8,128)(2,1)S(1)}, u32[]{:S(2)}, u32[]{:S(2)}) collective-permute-start(bf16[256,1024]{1,0:T(8,128)(2,1)S(1)} %get-tuple-element.537), channel_id=1, source_target_pairs={{0,8},{8,0},{16,24},{24,16},{1,9},{9,1},{17,25},{25,17},{2,10},{10... | collective-permute-start | bytes 1572872 | tf_op jit(solution)/shard_map/ppermute | solution.py:715
  303.5 42.6 %collective-permute-start.37 = (bf16[4,144,2560]{2,1,0:T(8,128)(2,1)S(1)}, bf16[4,144,2560]{2,1,0:T(8,128)(2,1)S(1)}, u32[]{:S(2)}, u32[]{:S(2)}) collective-permute-start(bf16[4,144,2560]{2,1,0:T(8,128)(2,1)S(1)} %strip_grad.2), channel_id=1, source_target_pairs={{0,1},{1,0},{2,3},{3,2},{4,5},{5,4},{6,7},{7,6},{8,9},{9,8},{10,11... | collective-permute-start | bytes 8847368 | tf_op jit(solution)/shard_map/ppermute | solution.py:715
  308.3 37.1 %collective-permute-start.39 = (bf16[128,2048]{1,0:T(8,128)(2,1)S(1)}, bf16[128,2048]{1,0:T(8,128)(2,1)S(1)}, u32[]{:S(2)}, u32[]{:S(2)}) collective-permute-start(bf16[128,2048]{1,0:T(8,128)(2,1)S(1)} %get-tuple-element.505), channel_id=1, source_target_pairs={{0,2},{1,3},{2,0},{3,1},{4,6},{5,7},{6,4},{7,5},{8,10},{9,11},{10,... | collective-permute-start | bytes 1572872 | tf_op jit(solution)/shard_map/ppermute | solution.py:715
  310.3 35.0 %collective-permute-start.38 = (bf16[128,2048]{1,0:T(8,128)(2,1)S(1)}, bf16[128,2048]{1,0:T(8,128)(2,1)S(1)}, u32[]{:S(2)}, u32[]{:S(2)}) collective-permute-start(bf16[128,2048]{1,0:T(8,128)(2,1)S(1)} %get-tuple-element.514), channel_id=1, source_target_pairs={{0,4},{1,5},{2,6},{3,7},{4,0},{5,1},{6,2},{7,3},{8,12},{9,13},{10,... | collective-permute-start | bytes 1572872 | tf_op jit(solution)/shard_map/ppermute | solution.py:715
  342.1 59.0 %collective-permute-start.36 = (bf16[256,1024]{1,0:T(8,128)(2,1)S(1)}, bf16[256,1024]{1,0:T(8,128)(2,1)S(1)}, u32[]{:S(2)}, u32[]{:S(2)}) collective-permute-start(bf16[256,1024]{1,0:T(8,128)(2,1)S(1)} %fusion.6), channel_id=1, source_target_pairs={{0,16},{8,24},{16,0},{24,8},{1,17},{9,25},{17,1},{25,9},{2,18},{10... | collective-permute-start | bytes 1572872 | tf_op jit(solution)/shard_map/ppermute | solution.py:715
  343.1 33.3 %collective-permute-start.44 = (bf16[128,1024]{1,0:T(8,128)(2,1)S(1)}, bf16[128,1024]{1,0:T(8,128)(2,1)S(1)}, u32[]{:S(2)}, u32[]{:S(2)}) collective-permute-start(bf16[128,1024]{1,0:T(8,128)(2,1)S(1)} %add_convert_fusion.27), channel_id=1, source_target_pairs={{0,16},{8,24},{16,0},{24,8},{1,17},{9,25},{17,1},{25,9},{2,18},{10... | collective-permute-start | bytes 786440 | tf_op jit(solution)/shard_map/ppermute | solution.py:715
  345.7 30.8 %collective-permute-start.43 = (bf16[64,4096]{1,0:T(8,128)(2,1)S(1)}, bf16[64,4096]{1,0:T(8,128)(2,1)S(1)}, u32[]{:S(2)}, u32[]{:S(2)}) collective-permute-start(bf16[64,4096]{1,0:T(8,128)(2,1)S(1)} %get-tuple-element.535), channel_id=1, source_target_pairs={{0,8},{8,0},{16,24},{24,16},{1,9},{9,1},{17,25},{25,17},{2,10},{10... | collective-permute-start | bytes 1572872 | tf_op jit(solution)/shard_map/ppermute | solution.py:715
  346.5 32.8 %collective-permute-start.41 = (bf16[2,144,1280]{2,1,0:T(8,128)(2,1)S(1)}, bf16[2,144,1280]{2,1,0:T(8,128)(2,1)S(1)}, u32[]{:S(2)}, u32[]{:S(2)}) collective-permute-start(bf16[2,144,1280]{2,1,0:T(8,128)(2,1)S(1)} %pad_maximum_fusion.7), channel_id=1, source_target_pairs={{0,2},{1,3},{2,0},{3,1},{4,6},{5,7},{6,4},{7,5},{8,10},{9,11},{10,... | collective-permute-start | bytes 2211848 | tf_op jit(solution)/shard_map/ppermute | solution.py:715
  347.9 31.4 %collective-permute-start.42 = (bf16[2,144,1280]{2,1,0:T(8,128)(2,1)S(1)}, bf16[2,144,1280]{2,1,0:T(8,128)(2,1)S(1)}, u32[]{:S(2)}, u32[]{:S(2)}) collective-permute-start(bf16[2,144,1280]{2,1,0:T(8,128)(2,1)S(1)} %pad_maximum_fusion.8), channel_id=1, source_target_pairs={{0,4},{1,5},{2,6},{3,7},{4,0},{5,1},{6,2},{7,3},{8,12},{9,13},{10,... | collective-permute-start | bytes 2211848 | tf_op jit(solution)/shard_map/ppermute | solution.py:715
  376.5 19.5 %collective-permute-start.48 = (bf16[256,1024]{1,0:T(8,128)(2,1)S(1)}, bf16[256,1024]{1,0:T(8,128)(2,1)S(1)}, u32[]{:S(2)}, u32[]{:S(2)}) collective-permute-start(bf16[256,1024]{1,0:T(8,128)(2,1)S(1)} %maximum_select_fusion.7), channel_id=1, source_target_pairs={{0,8},{8,0},{16,24},{24,16},{1,9},{9,1},{17,25},{25,17},{2,10},{10... | collective-permute-start | bytes 1572872 | tf_op jit(solution)/shard_map/ppermute | solution.py:715
  376.7 21.0 %collective-permute-start.47 = (bf16[32,4096]{1,0:T(8,128)(2,1)S(1)}, bf16[32,4096]{1,0:T(8,128)(2,1)S(1)}, u32[]{:S(2)}, u32[]{:S(2)}) collective-permute-start(bf16[32,4096]{1,0:T(8,128)(2,1)S(1)} %dynamic-slice_bitcast_fusion), channel_id=1, source_target_pairs={{0,16},{8,24},{16,0},{24,8},{1,17},{9,25},{17,1},{25,9},{2,18},{10... | collective-permute-start | bytes 786440 | tf_op jit(solution)/shard_map/ppermute | solution.py:715
  379.8 18.1 %collective-permute-start.46 = (bf16[144,1280]{1,0:T(8,128)(2,1)S(1)}, bf16[144,1280]{1,0:T(8,128)(2,1)S(1)}, u32[]{:S(2)}, u32[]{:S(2)}) collective-permute-start(bf16[144,1280]{1,0:T(8,128)(2,1)S(1)} %get-tuple-element.525), channel_id=1, source_target_pairs={{0,2},{1,3},{2,0},{3,1},{4,6},{5,7},{6,4},{7,5},{8,10},{9,11},{10,... | collective-permute-start | bytes 1105928 | tf_op jit(solution)/shard_map/ppermute | solution.py:715
  381.3 16.6 %collective-permute-start.45 = (bf16[144,1280]{1,0:T(8,128)(2,1)S(1)}, bf16[144,1280]{1,0:T(8,128)(2,1)S(1)}, u32[]{:S(2)}, u32[]{:S(2)}) collective-permute-start(bf16[144,1280]{1,0:T(8,128)(2,1)S(1)} %get-tuple-element.530), channel_id=1, source_target_pairs={{0,4},{1,5},{2,6},{3,7},{4,0},{5,1},{6,2},{7,3},{8,12},{9,13},{10,... | collective-permute-start | bytes 1105928 | tf_op jit(solution)/shard_map/ppermute | solution.py:715
  397.8 29.1 %collective-permute-start.50 = (bf16[32,4096]{1,0:T(8,128)(2,1)S(1)}, bf16[32,4096]{1,0:T(8,128)(2,1)S(1)}, u32[]{:S(2)}, u32[]{:S(2)}) collective-permute-start(bf16[32,4096]{1,0:T(8,128)(2,1)S(1)} %add_convert_fusion.26), channel_id=1, source_target_pairs={{0,16},{8,24},{16,0},{24,8},{1,17},{9,25},{17,1},{25,9},{2,18},{10... | collective-permute-start | bytes 786440 | tf_op jit(solution)/shard_map/ppermute | solution.py:715
  398.1 44.6 %collective-permute-start.49 = (bf16[144,2560]{1,0:T(8,128)(2,1)S(1)}, bf16[144,2560]{1,0:T(8,128)(2,1)S(1)}, u32[]{:S(2)}, u32[]{:S(2)}) collective-permute-start(bf16[144,2560]{1,0:T(8,128)(2,1)S(1)} %pad_maximum_fusion.9), channel_id=1, source_target_pairs={{0,16},{8,24},{16,0},{24,8},{1,17},{9,25},{17,1},{25,9},{2,18},{10... | collective-permute-start | bytes 2211848 | tf_op jit(solution)/shard_map/ppermute | solution.py:715
  427.0 27.0 %collective-permute-start.52 = (bf16[64,4096]{1,0:T(8,128)(2,1)S(1)}, bf16[64,4096]{1,0:T(8,128)(2,1)}, u32[]{:S(2)}, u32[]{:S(2)}) collective-permute-start(bf16[64,4096]{1,0:T(8,128)(2,1)S(1)} %maximum_select_fusion.8), channel_id=1, source_target_pairs={{0,8},{8,0},{16,24},{24,16},{1,9},{9,1},{17,25},{25,17},{2,10},{10... | collective-permute-start | bytes 1572872 | tf_op jit(solution)/shard_map/ppermute | solution.py:715
  443.0 26.7 %collective-permute-start.51 = (bf16[144,2560]{1,0:T(8,128)(2,1)S(1)}, bf16[144,2560]{1,0:T(8,128)(2,1)S(1)}, u32[]{:S(2)}, u32[]{:S(2)}) collective-permute-start(bf16[144,2560]{1,0:T(8,128)(2,1)S(1)} %add_convert_fusion.1), channel_id=1, source_target_pairs={{0,8},{8,0},{16,24},{24,16},{1,9},{9,1},{17,25},{25,17},{2,10},{10... | collective-permute-start | bytes 2211848 | tf_op jit(solution)/shard_map/ppermute | solution.py:715
  (85 other events, 536.6 us)
Sparse Core Ops, SparseCore 0:
  13.0 43.3 all-gather.5
  77.2 30.7 all-gather.3
